TPU v7x, 768 devices: a whole 4x8x12 slice. The times are simulated.
768 devices in a mesh: dp: 64 (over y, x, core), mp: 12 (over z).
Axes of the slice: x: 4, y: 8, z: 12, core: 2. Of those that a mesh axis runs over, the one named last changes fastest.
Arguments:
- query_hidden: bfloat16 [3072, 4096], P('dp'), may hold values from -24 to 24
- passage_hidden: bfloat16 [3072, 4096], P('dp'), may hold values from -6 to 6
- negative_hidden: bfloat16 [21504, 4096], P('dp'), may hold values from -24 to 24
- projection: bfloat16 [4096, 3072], P(None, 'mp'), may hold values from -0.09375 to 0.09375
- positive: int32 [3072], P('dp'), may hold values from 0 to 3071, each once
- hard_ids: int32 [3072, 7], P('dp'), may hold values from 0 to 21503, as said below
Outputs:
- query_loss: float32 [3072], P('dp')
- query_grad: float32 [3072, 3072], P('dp', 'mp')
- passage_grad: float32 [3072, 3072], P('dp', 'mp')
- hard_grad: float32 [3072, 7, 3072], P('dp', None, 'mp')
Inputs may be any that keep to these rules, and one draw needn't show every extreme that they name: `hard_ids`: within each block of 48 queries (one index of dp) at most 11 ids fall in the pool rows of one index of dp (id // 336); in every draw one such owner receives exactly 11 ids from every block. Each passage is the positive of exactly one query.
All inputs are finite; a program needn't handle non-finite values.
Results may differ from a plain program's by a relative error of at most 0.01.
Values may be sent and summed in bfloat16 or wider, within the bound.
No kernel may reach another device: no remote copies, remote signals or barrier semaphores. Data moves between devices by JAX's collectives and lax.ppermute only.
A program may use at most 32 MiB of HBM per device.

v0:
```python
import math

import jax
import jax.numpy as jnp
from jax import lax
from jax.sharding import PartitionSpec as P

E = 3072


def local(query_hidden, passage_hidden, negative_hidden, projection, positive, hard_ids):
    score_scale = 1.0 / math.sqrt(E)
    q_rows = query_hidden.shape[0]
    hard_count = hard_ids.shape[1]
    pool_rows = negative_hidden.shape[0]
    holder_list = lax.axis_size("dp")
    query_emb = jnp.dot(query_hidden, projection, preferred_element_type=jnp.float32).astype(
        jnp.bfloat16
    )
    passage_emb = jnp.dot(passage_hidden, projection, preferred_element_type=jnp.float32).astype(
        jnp.bfloat16
    )
    pool_emb = jnp.dot(negative_hidden, projection, preferred_element_type=jnp.float32).astype(
        jnp.bfloat16
    )
    all_passages = lax.all_gather(passage_emb, "dp", axis=0, tiled=True)
    flat_ids = hard_ids.reshape(-1)
    owner_dp = flat_ids // pool_rows
    local_row = flat_ids - owner_dp * pool_rows
    capacity = 2 * q_rows * hard_count // holder_list + 1
    owner_marks = (owner_dp[:, None] == jnp.arange(holder_list, dtype=jnp.int32)[None, :]).astype(
        jnp.int32
    )
    before = jnp.cumsum(owner_marks, axis=0) - owner_marks
    slot_rank = jnp.sum(owner_marks * before, axis=1)
    slot_index = owner_dp * capacity + slot_rank
    request = jnp.zeros((holder_list * capacity,), jnp.int32).at[slot_index].set(local_row)
    arrived = lax.all_to_all(
        request.reshape(holder_list, capacity), "dp", split_axis=0, concat_axis=0, tiled=True
    )
    looked_up = pool_emb[arrived.reshape(-1)].reshape(holder_list, capacity, pool_emb.shape[1])
    returned = lax.all_to_all(looked_up, "dp", split_axis=0, concat_axis=0, tiled=True)
    fetched = returned.reshape(holder_list * capacity, -1)[slot_index].reshape(
        q_rows, hard_count, -1
    )
    batch_part = jnp.einsum(
        "qe,pe->qp", query_emb, all_passages, preferred_element_type=jnp.float32
    )
    hard_part = jnp.einsum("qe,qke->qk", query_emb, fetched, preferred_element_type=jnp.float32)
    batch_scores, hard_scores = lax.psum((batch_part, hard_part), "mp")
    batch_logits = batch_scores * score_scale
    hard_logits = hard_scores * score_scale
    peak = jnp.maximum(jnp.max(batch_logits, axis=1), jnp.max(hard_logits, axis=1))
    batch_expo = jnp.exp(batch_logits - peak[:, None])
    hard_expo = jnp.exp(hard_logits - peak[:, None])
    denominator = jnp.sum(batch_expo, axis=1) + jnp.sum(hard_expo, axis=1)
    col_index = jnp.arange(batch_logits.shape[1], dtype=jnp.int32)
    target = (col_index[None, :] == positive[:, None]).astype(jnp.float32)
    pos_logit = jnp.sum(target * batch_scores, axis=1) * score_scale
    query_loss = peak + jnp.log(denominator) - pos_logit
    batch_grad = (batch_expo / denominator[:, None] - target).astype(jnp.bfloat16)
    hard_score_grad = (hard_expo / denominator[:, None]).astype(jnp.bfloat16)
    query_grad = jnp.dot(batch_grad, all_passages, preferred_element_type=jnp.float32)
    query_grad = query_grad + jnp.einsum(
        "qk,qke->qe", hard_score_grad, fetched, preferred_element_type=jnp.float32
    )
    hard_grad = (
        hard_score_grad.astype(jnp.float32)[:, :, None] * query_emb.astype(jnp.float32)[:, None, :]
    )
    passage_grad = lax.psum_scatter(
        jnp.einsum("qp,qe->pe", batch_grad, query_emb, preferred_element_type=jnp.float32),
        "dp",
        scatter_dimension=0,
        tiled=True,
    )
    return (query_loss, query_grad, passage_grad, hard_grad)


def solution(mesh):
    return jax.shard_map(
        local,
        mesh=mesh,
        in_specs=(
            P("dp", None),
            P("dp", None),
            P("dp", None),
            P(None, "mp"),
            P("dp"),
            P("dp", None),
        ),
        out_specs=(P("dp"), P("dp", "mp"), P("dp", "mp"), P("dp", None, "mp")),
        check_vma=False,
    )
```

profile of v0, /device:TPU:16, one launch (start us, length us, event | category | flops | bytes accessed | tf_op | source)
XLA Modules:
  0.0 391.2 jit_solution(1972081967569158544)
XLA Ops:
  7.2 2.9 convolution_convert_fusion.1
  10.5 0.9 reduce-window.6
  12.3 2.9 scatter_custom_fusion
  15.3 0.7 all_to_all.9
  16.0 13.5 %all-to-all-start = ((s32[64,1,11]{2,1,0:T(1,128)}), s32[64,1,11]{2,1,0:T(1,128)S(1)}, u32[]{:S(2)}, u32[]{:S(2)}) async-start(s32[64,1,11]{2,1,0:T(1,128)} %bitcast.2), calls=%async_computation | async-start | bytes 65536 | tf_op jit(solution)/shard_map/all_to_all | solution.py:38
  29.5 2.5 convolution_convert_fusion
  32.0 5.2 %all-to-all-done = s32[64,1,11]{2,1,0:T(1,128)S(1)} async-done(((s32[64,1,11]{2,1,0:T(1,128)}), s32[64,1,11]{2,1,0:T(1,128)S(1)}, u32[]{:S(2)}, u32[]{:S(2)}) %all-to-all-start) | async-done | bytes 2848 | tf_op jit(solution)/shard_map/all_to_all | solution.py:38
  38.6 2.8 gather_fusion
  41.5 0.9 reshape.163
  42.4 7.2 %all-to-all-start.1 = ((bf16[64,11,256]{2,1,0:T(8,128)(2,1)}), bf16[64,11,256]{2,1,0:T(8,128)(2,1)}, u32[]{:S(2)}, u32[]{:S(2)}) async-start(bf16[64,11,256]{2,1,0:T(8,128)(2,1)} %reshape.163), calls=%async_computation.1 | async-start | bytes 1048576 | tf_op jit(solution)/shard_map/all_to_all | solution.py:42
  49.7 2.8 fusion.16
  52.5 55.2 %all-gather.2.cloned.1.call-done = bf16[3072,256]{1,0:T(8,128)(2,1)} async-done(((bf16[48,256]{1,0:T(8,128)(2,1)}), bf16[3072,256]{1,0:T(8,128)(2,1)}) %all-gather.2.cloned.1.call-update) | async-done | bytes 1572880 | tf_op jit(solution)/shard_map/all_gather | solution.py:26
  107.7 2.8 fusion.17
  110.6 1.2 reshape.164
  111.8 2.0 gather_fusion.1
  114.2 25.3 %psum.15 = f32[48,7]{0,1:T(8,128)S(1)} all-reduce(f32[48,7]{0,1:T(8,128)S(1)} %bitcast.33), channel_id=1, replica_groups=mesh['dp'=64,'mp'=12] {'mp'}, use_global_device_ids=true, to_apply=%region_6.7 | all-reduce | flops 336 | bytes 2688 | tf_op jit(solution)/shard_map/psum | solution.py:50
  139.5 82.8 %all-reduce.3.cloned.1.call-done = f32[48,3072]{1,0:T(8,128)} async-done(((f32[48,3072]{1,0:T(8,128)}), f32[48,3072]{1,0:T(8,128)}) %all-reduce.3.cloned.1.call-update) | async-done | bytes 589840 | tf_op jit(solution)/shard_map/psum | solution.py:50
  222.3 1.2 multiply_reduce_fusion
  223.6 1.4 fusion
  225.5 3.4 fusion.14
  230.4 0.9 fusion.18
  231.3 1.6 broadcast_multiply_fusion
  233.0 2.5 convolution_add_fusion
  235.4 149.2 %reduce-scatter.2.cloned.1.call-done = f32[48,256]{1,0:T(8,128)} async-done(((f32[3072,256]{1,0:T(8,128)}), f32[48,256]{1,0:T(8,128)}) %reduce-scatter.2.cloned.1.call-update) | async-done | bytes 49168 | tf_op jit(solution)/shard_map/reduce_scatter | solution.py:70
  (48 shorter events, 5.1 us)
Async XLA Ops:
  7.2 22.3 %copy-start = (bf16[336,4096]{1,0:T(8,128)(2,1)S(1)}, bf16[336,4096]{1,0:T(8,128)(2,1)}, u32[]{:S(2)}) copy-start(bf16[336,4096]{1,0:T(8,128)(2,1)} %param.8) | copy-start | bytes 8257540
  7.2 3.0 copy-start.2
  7.2 100.5 %all-gather.2.cloned.1.call-start = ((), (), s32[]{:S(2)}) async-start(), calls=%async_computation.3 | async-start | bytes 1597440 | tf_op jit(solution)/shard_map/all_gather | solution.py:26
  16.0 21.2 %all-to-all-start = ((s32[64,1,11]{2,1,0:T(1,128)}), s32[64,1,11]{2,1,0:T(1,128)S(1)}, u32[]{:S(2)}, u32[]{:S(2)}) async-start(s32[64,1,11]{2,1,0:T(1,128)} %bitcast.2), calls=%async_computation | async-start | bytes 65536 | tf_op jit(solution)/shard_map/all_to_all | solution.py:38
  42.4 68.2 %all-to-all-start.1 = ((bf16[64,11,256]{2,1,0:T(8,128)(2,1)}), bf16[64,11,256]{2,1,0:T(8,128)(2,1)}, u32[]{:S(2)}, u32[]{:S(2)}) async-start(bf16[64,11,256]{2,1,0:T(8,128)(2,1)} %reshape.163), calls=%async_computation.1 | async-start | bytes 1048576 | tf_op jit(solution)/shard_map/all_to_all | solution.py:42
  49.6 172.7 %all-reduce.3.cloned.1.call-start = ((), (), s32[]{:S(2)}) async-start(), calls=%async_computation.4 | async-start | bytes 1179648 | tf_op jit(solution)/shard_map/psum | solution.py:50
  110.5 113.0 %copy-start.4 = (s32[48]{0:T(128)S(1)}, s32[48]{0:T(128)}, u32[]{:S(2)}) copy-start(s32[48]{0:T(128)} %param.10) | copy-start | bytes 580
  110.5 274.1 %reduce-scatter.2.cloned.1.call-start = ((), (), s32[]{:S(2)}) async-start(), calls=%async_computation.5 | async-start | bytes 3194880 | tf_op jit(solution)/shard_map/reduce_scatter | solution.py:70
  225.5 3.4 copy-start.3
  228.9 4.0 %copy-start.1 = (f32[48,3072]{1,0:T(8,128)S(1)}, f32[48,3072]{1,0:T(8,128)}, u32[]{:S(2)}) copy-start(f32[48,3072]{1,0:T(8,128)} %all-reduce.3.cloned.1.call-done) | copy-start | bytes 1769476
Sparse Core Ops, SparseCore 0:
  12.5 95.1 all-gather.1
  110.7 111.6 all-reduce.2
  229.1 155.4 reduce-scatter.1
where the time goes:
time: 392 us; the launch traced here: 391 us
  waiting for transfers between devices  293 us (75%)
  blocking collectives  25.3 us (6%)
  starting transfers between devices  20.8 us (5%)
  matrix products  18 us (5%)
  between operations  14 us (4%)
  local copies, waits for them, and re-layouts  13.1 us (3%)
  other arithmetic  7.47 us (2%)
    reduce_scatter x1, waiting for transfers between devices, local(): lax.psum_scatter(jnp.einsum('qp,qe->pe', batch_grad, query_emb, preferred...  149 us
    psum x1, waiting for transfers between devices, local(): batch_scores, hard_scores = lax.psum((batch_part, hard_part), 'mp')  82.8 us
    all_gather x1, waiting for transfers between devices, local(): all_passages = lax.all_gather(passage_emb, 'dp', axis=0, tiled=True)  55.2 us
    psum x1, blocking collectives, local(): batch_scores, hard_scores = lax.psum((batch_part, hard_part), 'mp')  25.3 us
    all_to_all x1, starting transfers between devices, local(): lax.all_to_all(request.reshape(holder_list, capacity), 'dp', split_axis=0...  13.5 us
  transfers between devices with their start and end apart: 5, of which 4 were waited for; matrix products, arithmetic and copies ran while one was open for 7% of the time, Pallas kernels for 0%

commit v1 on v0

v1 whole, which is shorter than its diff:
```python
import math

import jax
import jax.numpy as jnp
import numpy as np
from jax import lax
from jax.experimental import pallas as pl
from jax.experimental.pallas import tpu as pltpu
from jax.sharding import Mesh
from jax.sharding import PartitionSpec as P

E = 3072
SCALE = 1.0 / math.sqrt(E)
F32 = jnp.float32
BF16 = jnp.bfloat16
I32 = jnp.int32
Q = 48
K = 7
POOL = 336
CHIPS = 32
SLOT = 32
Z = 12
W = Q * CHIPS
WP = W + 128
TL, TC = W + 7, W + 8
L0 = W + 7
NEG = -3.0e38


def iota(shape, dim):
    return lax.broadcasted_iota(I32, shape, dim)


def params(mib=24):
    return pltpu.CompilerParams(vmem_limit_bytes=mib * 2**20)


def call(kernel, out, *args, flops=0, nbytes=0, **kw):
    return pl.pallas_call(
        kernel,
        out_shape=out,
        compiler_params=params(),
        cost_estimate=pl.CostEstimate(flops=flops, bytes_accessed=nbytes, transcendentals=0),
        **kw,
    )(*args)


def dot(a, b, dims=(((1,), (0,)), ((), ()))):
    return lax.dot_general(a, b, dims, preferred_element_type=F32)


def request_kernel(ids_ref, req_ref, slot_ref):
    ids = ids_ref[...]
    owner = lax.shift_right_arithmetic(ids * 49933, 25)
    row = ids - owner * (2 * POOL)
    high, low = lax.shift_right_arithmetic(row, 4).astype(F32), (row & 15).astype(F32)
    marks = jnp.where(owner[None] == iota((CHIPS, 8, 128), 0), 1.0, 0.0)
    flat = marks.reshape(CHIPS * 8, 128).astype(BF16)
    upper = jnp.where(iota((128, 128), 0) < iota((128, 128), 1), 1.0, 0.0).astype(BF16)
    a, b = iota((256, 256), 0), iota((256, 256), 1)
    lower = jnp.where((b < a) & (lax.shift_right_logical(a, 3) == lax.shift_right_logical(b, 3)), 1.0, 0.0).astype(BF16)
    above = dot(lower, flat).astype(BF16)
    before = dot(flat, upper) + dot(above, jnp.ones((128, 128), BF16))
    rank = jnp.sum(marks * before.reshape(CHIPS, 8, 128), axis=0)
    rank_cols = rank.T
    lanes = iota((128, 128), 1).astype(F32)
    total = jnp.zeros((2 * CHIPS, 128), F32)
    for k in range(K):
        mine = owner[k : k + 1, :] == iota((CHIPS, 128), 0)
        left = jnp.concatenate(
            [jnp.where(mine, high[k : k + 1, :], 0.0), jnp.where(mine, low[k : k + 1, :], 0.0)], axis=0
        )
        right = jnp.where(rank_cols[:, k : k + 1] == lanes, 1.0, 0.0)
        total += dot(left.astype(BF16), right.astype(BF16))
    request = (total[:CHIPS] * 16.0 + total[CHIPS:]).astype(I32)
    req_ref[...] = jnp.broadcast_to(request[:, None, :], (CHIPS, 8, 128))
    slot_ref[...] = (owner.astype(F32) * SLOT + rank).T


def project_kernel(qh_ref, ph_ref, nh_ref, w_ref, pos_ref, emb_ref, pass_ref, acc):
    step = pl.program_id(0)

    @pl.when(step == 0)
    def _():
        acc[...] = jnp.zeros_like(acc)

    w = w_ref[...]
    acc[0:Q] += dot(qh_ref[...], w)
    acc[Q : 2 * Q] += dot(ph_ref[...], w)
    acc[2 * Q :] += dot(nh_ref[...], w)

    @pl.when(step == pl.num_programs(0) - 1)
    def _():
        emb_ref[0 : 2 * Q + POOL] = acc[...].astype(BF16)
        pass_ref[...] = jnp.broadcast_to(acc[Q : 2 * Q].astype(BF16)[None], (CHIPS, Q, 256))
        pos = jnp.broadcast_to(pos_ref[...], (16, 256))
        high = lax.shift_right_arithmetic(pos, 6).astype(F32)
        low = (pos & 63).astype(F32)
        emb_ref[2 * Q + POOL :] = jnp.where(iota((16, 256), 0) == 0, high, low).astype(BF16)


def answer_kernel(core_ref, asked_ref, emb_ref, other_ref, send_ref, both_ref, pool):
    core = core_ref[0]
    pool[0:POOL] = emb_ref[2 * Q : 2 * Q + POOL]
    pool[POOL : 2 * POOL] = other_ref[2 * Q : 2 * Q + POOL]
    pool[2 * POOL :] = jnp.zeros((768 - 2 * POOL, 256), BF16)
    first = core == 0

    @pl.when(first)
    def _():
        both_ref[0:Q] = emb_ref[0:Q]
        both_ref[Q:] = other_ref[0:Q]

    @pl.when(jnp.logical_not(first))
    def _():
        both_ref[0:Q] = other_ref[0:Q]
        both_ref[Q:] = emb_ref[0:Q]

    asked = asked_ref[:, 0, :]
    flipped = jnp.where(asked >= POOL, asked - POOL, asked + POOL)
    wanted = jnp.where(core == 1, flipped, asked).astype(F32).T
    lanes = iota((SLOT, 768), 1).astype(F32)
    rows = pool[...]
    for g in range(CHIPS // 4):
        hot = jnp.concatenate(
            [jnp.where(wanted[0:SLOT, j : j + 1] == lanes, 1.0, 0.0) for j in range(4 * g, 4 * g + 4)], axis=0
        )
        found = dot(hot.astype(BF16), rows).astype(BF16)
        for i in range(4):
            send_ref[4 * g + i] = found[SLOT * i : SLOT * (i + 1)]


def score_kernel(both_ref, pass_ref, part_ref):
    queries = both_ref[...]
    for g in range(4):
        block = pass_ref[8 * g : 8 * g + 8].reshape(8 * Q, 256)
        part_ref[:, 8 * Q * g : 8 * Q * (g + 1)] = dot(queries, block, (((1,), (1,)), ((), ())))


def hard_kernel(core_ref, part_ref, rows_ref, emb_ref, other_ref, slot_ref, send_ref, fetched_ref):
    first = core_ref[0] == 0
    mine = emb_ref[0:Q]
    send_ref[:, 0:W] = part_ref[...]
    rows = rows_ref[...].reshape(CHIPS * SLOT, 256)
    places = iota((Q, CHIPS * SLOT), 1).astype(F32)
    slots = slot_ref[...]
    hot = jnp.concatenate([jnp.where(slots[0:Q, k : k + 1] == places, 1.0, 0.0) for k in range(K)], axis=0)
    found = dot(hot.astype(BF16), rows)
    lane = iota((Q, 128), 1)
    mine32 = mine.astype(F32)
    hard = jnp.zeros((Q, 128), F32)
    for k in range(K):
        row = found[Q * k : Q * (k + 1)]
        fetched_ref[k] = row.astype(BF16)
        hard = jnp.where(lane == k, jnp.sum(mine32 * row, axis=1, keepdims=True), hard)

    def target(ref):
        pos = ref[2 * Q + POOL :].astype(F32).T
        pos = (pos[0:Q, 0:1] * 64.0 + pos[0:Q, 1:2]).astype(I32)
        index = pos.astype(F32) + 0.5
        chip = (index * (1.0 / 96.0)).astype(I32)
        dp = (index * (1.0 / 48.0)).astype(I32)
        column = (chip * Q + pos - dp * Q).astype(F32)
        return jnp.where(lane == 7, column, jnp.where(lane == 8, (dp - 2 * chip).astype(F32), 0.0))

    mine_extra, other_extra = hard + target(emb_ref), target(other_ref)
    send_ref[0:Q, W:] = jnp.where(first, mine_extra, other_extra)
    send_ref[Q:, W:] = jnp.where(first, other_extra, mine_extra)


def stats_kernel(core_ref, part_ref, logit_ref, stat_ref):
    core = core_ref[0]
    z = core_ref[1]
    own = (z >= Z // 2) == (core == 1)
    total = part_ref[0]
    for i in range(1, Z):
        total += part_ref[i]
    lane = iota((8, WP), 1)
    valid = (lane < W) | (own & (lane < W + K))
    logits = jnp.where(valid, total * SCALE, NEG)
    peak = jnp.max(logits, axis=1, keepdims=True)
    mass = jnp.sum(jnp.where(valid, jnp.exp(logits - peak), 0.0), axis=1, keepdims=True)
    column = part_ref[0, :, TL : TL + 1]
    here = part_ref[0, :, TC : TC + 1] == core.astype(F32)
    column = jnp.where(here, column, -1.0)
    aim = lane.astype(F32) == column
    hit = jnp.sum(jnp.where(aim, logits, 0.0), axis=1, keepdims=True)
    logit_ref[...] = logits
    lane = iota((8, 128), 1)
    stat_ref[...] = jnp.where(
        lane == 0, peak, jnp.where(lane == 1, mass, jnp.where(lane == 2, hit, jnp.where(lane == 3, column, 0.0)))
    )


def grad_kernel(logit_ref, mine_ref, other_ref, send_ref):
    mine, other = mine_ref[...], other_ref[...]
    peak = jnp.maximum(mine[:, 0:1], other[:, 0:1])
    mass = mine[:, 1:2] * jnp.exp(mine[:, 0:1] - peak) + other[:, 1:2] * jnp.exp(other[:, 0:1] - peak)
    loss = peak + jnp.log(mass) - (mine[:, 2:3] + other[:, 2:3])
    logits = logit_ref[...]
    lane = iota((8, WP), 1)
    probs = jnp.where(logits > NEG, jnp.exp(logits - peak) / mass, 0.0)
    grads = probs - jnp.where(lane.astype(F32) == mine[:, 3:4], 1.0, 0.0)
    high = loss.astype(BF16).astype(F32)
    mid = (loss - high).astype(BF16).astype(F32)
    low = loss - high - mid
    grads = jnp.where(lane == L0, high, jnp.where(lane == L0 + 1, mid, jnp.where(lane == L0 + 2, low, grads)))
    send_ref[...] = jnp.broadcast_to(grads.astype(BF16)[None], (Z, 8, WP))


def turn_kernel(grad_ref, both_ref, send_ref, flat_ref):
    grads = grad_ref[...].astype(F32).reshape(Z * 8, WP).astype(BF16)
    flat_ref[...] = grads
    queries = both_ref[...]
    for g in range(4):
        part = dot(grads[:, 8 * Q * g : 8 * Q * (g + 1)], queries, (((0,), (0,)), ((), ())))
        send_ref[8 * g : 8 * g + 8] = part.astype(BF16).reshape(8, Q, 256)


def query_kernel(core_ref, grad_ref, recv_ref, fetched_ref, emb_ref, mine_ref, other_ref, hard_ref, loss_ref):
    first = core_ref[0] == 0
    total = jnp.zeros((2 * Q, 256), F32)
    for g in range(4):
        block = recv_ref[8 * g : 8 * g + 8].reshape(8 * Q, 256)
        total += dot(grad_ref[:, 8 * Q * g : 8 * Q * (g + 1)], block)
    upper, lower = total[0:Q], total[Q:]
    other_ref[...] = jnp.where(first, lower, upper)
    tail = grad_ref[:, W:].astype(F32)
    mine = jnp.where(first, tail[0:Q], tail[Q:])
    queries = emb_ref[0:Q].astype(F32)
    result = jnp.where(first, upper, lower)
    for k in range(K):
        weight = mine[:, k : k + 1]
        result += weight * fetched_ref[k].astype(F32)
        hard_ref[k] = weight * queries
    mine_ref[...] = result
    loss = mine[:, K : K + 1] + mine[:, K + 1 : K + 2] + mine[:, K + 2 : K + 3]
    loss_ref[...] = jnp.broadcast_to(loss, (Q, 128)).T[0:8]


def passage_kernel(parts_ref, mine_ref, other_ref, out_ref, query_ref):
    total = parts_ref[0].astype(F32)
    for j in range(1, CHIPS):
        total += parts_ref[j].astype(F32)
    out_ref[...] = total
    query_ref[...] = mine_ref[...] + other_ref[...]


def swap(x):
    return lax.ppermute(x, "c", [(0, 1), (1, 0)])


def exchange(x, axes):
    return lax.all_to_all(x, axes, split_axis=0, concat_axis=0, tiled=True)


def shape(dims, dtype):
    return jax.ShapeDtypeStruct(dims, dtype)


SMEM = pl.BlockSpec(memory_space=pltpu.SMEM)
VMEM = pl.BlockSpec(memory_space=pltpu.VMEM)


def local(query_hidden, passage_hidden, negative_hidden, projection, positive, hard_ids):
    place = jnp.stack([lax.axis_index("c"), lax.axis_index("z")]).astype(I32)
    ids = jnp.pad(hard_ids.T, ((0, 1), (0, 128 - Q)), constant_values=-1)
    request, slots = call(request_kernel, (shape((CHIPS, 8, 128), I32), shape((128, 8), F32)), ids)
    asked = exchange(request, ("y", "x"))

    steps = 8
    depth = query_hidden.shape[1] // steps
    pos = jnp.pad(positive[None, :], ((0, 0), (0, 256 - Q)))
    emb, passages = call(
        project_kernel,
        (shape((2 * Q + POOL + 16, 256), BF16), shape((CHIPS, Q, 256), BF16)),
        query_hidden,
        passage_hidden,
        negative_hidden,
        projection,
        pos,
        grid=(steps,),
        in_specs=[
            pl.BlockSpec((Q, depth), lambda i: (0, i)),
            pl.BlockSpec((Q, depth), lambda i: (0, i)),
            pl.BlockSpec((POOL, depth), lambda i: (0, i)),
            pl.BlockSpec((depth, 256), lambda i: (i, 0)),
            pl.BlockSpec((1, 256), lambda i: (0, 0)),
        ],
        out_specs=[
            pl.BlockSpec((2 * Q + POOL + 16, 256), lambda i: (0, 0)),
            pl.BlockSpec((CHIPS, Q, 256), lambda i: (0, 0, 0)),
        ],
        scratch_shapes=[pltpu.VMEM((2 * Q + POOL, 256), F32)],
        flops=2 * 432 * 4096 * 256,
        nbytes=6 * 2**20,
    )
    other = swap(emb)
    passages, asked = lax.optimization_barrier((passages, asked))
    recv = exchange(passages, ("y", "x"))
    answers, both = call(
        answer_kernel,
        (shape((CHIPS, SLOT, 256), BF16), shape((2 * Q, 256), BF16)),
        place,
        asked,
        emb,
        other,
        in_specs=[SMEM, VMEM, VMEM, VMEM],
        scratch_shapes=[pltpu.VMEM((768, 256), BF16)],
        flops=2 * 1024 * 768 * 256,
        nbytes=2 * 2**20,
    )
    answers, recv = lax.optimization_barrier((answers, recv))
    rows = exchange(answers, ("y", "x"))
    part = call(
        score_kernel, shape((2 * Q, W), F32), both, recv, flops=2 * 96 * 1536 * 256, nbytes=2 * 2**20
    )
    send, fetched = call(
        hard_kernel,
        (shape((2 * Q, WP), F32), shape((K, Q, 256), BF16)),
        place,
        part,
        rows,
        emb,
        other,
        slots,
        in_specs=[SMEM, VMEM, VMEM, VMEM, VMEM, VMEM],
        flops=2 * 336 * 1024 * 256,
        nbytes=3 * 2**20,
    )
    parts = exchange(send.reshape(Z, 8, WP), "z")
    logits, stat = call(
        stats_kernel,
        (shape((8, WP), F32), shape((8, 128), F32)),
        place,
        parts,
        in_specs=[SMEM, VMEM],
        nbytes=2**20,
    )
    stat_other = swap(stat)
    grads = exchange(call(grad_kernel, shape((Z, 8, WP), BF16), logits, stat, stat_other, nbytes=2**19), "z")
    sums, flat = call(
        turn_kernel,
        (shape((CHIPS, Q, 256), BF16), shape((Z * 8, WP), BF16)),
        grads,
        both,
        flops=2 * 96 * 1536 * 256,
        nbytes=2 * 2**20,
    )
    sums = exchange(sums, ("y", "x"))
    query_mine, query_other, hard_grad, loss = call(
        query_kernel,
        (shape((Q, 256), F32), shape((Q, 256), F32), shape((K, Q, 256), F32), shape((8, Q), F32)),
        place,
        flat,
        recv,
        fetched,
        emb,
        in_specs=[SMEM, VMEM, VMEM, VMEM, VMEM],
        flops=2 * 96 * 1536 * 256,
        nbytes=3 * 2**20,
    )
    query_back = swap(query_other)
    passage_grad, query_grad = call(
        passage_kernel,
        (shape((Q, 256), F32), shape((Q, 256), F32)),
        sums,
        query_mine,
        query_back,
        nbytes=2**20,
    )
    return (loss[0], query_grad, passage_grad, jnp.transpose(hard_grad, (1, 0, 2)))


def solution(mesh):
    devices = np.asarray(mesh.devices)
    view = Mesh(devices.reshape(8, 4, 2, Z), ("y", "x", "c", "z"))
    dp = ("y", "x", "c")
    return jax.shard_map(
        local,
        mesh=view,
        in_specs=(P(dp, None), P(dp, None), P(dp, None), P(None, "z"), P(dp), P(dp, None)),
        out_specs=(P(dp), P(dp, "z"), P(dp, "z"), P(dp, None, "z")),
        check_vma=False,
    )
```

time: 392 us -> 175 us (0.45)
  the two profiles are of different devices: /device:TPU:16 before, /device:TPU:64 now
where the time goes in v1:
time: 175 us; the launch traced here: 174 us
  blocking collectives  60.4 us (35%)
  waiting for transfers between devices  54.7 us (31%)
  starting transfers between devices  37.2 us (21%)
  Pallas kernels  13.6 us (8%)
  local copies, waits for them, and re-layouts  7.23 us (4%)
    all_to_all x2, blocking collectives, exchange(): return lax.all_to_all(x, axes, split_axis=0, concat_axis=0, tiled=True)  60.4 us
    all_to_all x4, waiting for transfers between devices, exchange(): return lax.all_to_all(x, axes, split_axis=0, concat_axis=0, tiled=True)  51.5 us
    all_to_all x4, starting transfers between devices, exchange(): return lax.all_to_all(x, axes, split_axis=0, concat_axis=0, tiled=True)  31.4 us
    pallas_call x10, Pallas kernels, call(): pl.pallas_call(kernel, out_shape=out, compiler_params=params(), cost_esti...  13.6 us
    ppermute x3, starting transfers between devices, swap(): return lax.ppermute(x, 'c', [(0, 1), (1, 0)])  5.76 us
    unnamed x8, local copies, waits for them, and re-layouts  5.36 us
  transfers between devices with their start and end apart: 7, of which 7 were waited for; matrix products, arithmetic and copies ran while one was open for 1% of the time, Pallas kernels for 5%

profile of v1, /device:TPU:64, one launch (start us, length us, event | category | flops | bytes accessed | tf_op | source)
XLA Modules:
  0.0 173.8 jit_solution(16209106641925067693)
XLA Ops:
  1.3 1.4 shard_map.94
  2.8 10.0 %all-to-all-start = ((s32[32,8,128]{2,1,0:T(8,128)}), s32[32,8,128]{2,1,0:T(8,128)S(1)}, u32[]{:S(2)}, u32[]{:S(2)}) async-start(s32[32,8,128]{2,1,0:T(8,128)} %get-tuple-element.27), calls=%async_computation | async-start | bytes 262144 | tf_op jit(solution)/shard_map/all_to_all | solution.py:254
  13.4 1.8 %copy-done = bf16[336,4096]{1,0:T(8,128)(2,1)S(1)} copy-done((bf16[336,4096]{1,0:T(8,128)(2,1)S(1)}, bf16[336,4096]{1,0:T(8,128)(2,1)}, u32[]{:S(2)}) %copy-start) | copy-done | bytes 2752536
  15.2 1.6 copy-done.1
  16.8 1.0 copy-done.2
  17.8 1.0 copy-done.3
  18.7 4.1 %shard_map.93 = (bf16[448,256]{1,0:T(8,128)(2,1)S(1)}, bf16[32,48,256]{2,1,0:T(8,128)(2,1)}) custom-call(bf16[48,4096]{1,0:T(8,128)(2,1)S(1)} %copy-done.2, bf16[48,4096]{1,0:T(8,128)(2,1)S(1)} %copy-done.3, bf16[336,4096]{1,0:T(8,128)(2,1)S(1)} %copy-done, bf16[4096,256]{1,0:T(8,128)(2,1)S(1)} %copy-done.1, s32[1,256]{1,0:T(1,128)S(1)} %pad.8.pos_ref), custom_call_target="tpu_custom_call" | custom-call | flops 905969664 | bytes 6291456 | tf_op jit(solution)/shard_map/pallas_call | solution.py:39
  23.2 9.5 %all-to-all-start.1 = ((bf16[32,48,256]{2,1,0:T(8,128)(2,1)}), bf16[32,48,256]{2,1,0:T(8,128)(2,1)S(1)}, u32[]{:S(2)}, u32[]{:S(2)}) async-start(bf16[32,48,256]{2,1,0:T(8,128)(2,1)} %get-tuple-element.32), calls=%async_computation.1 | async-start | bytes 1572864 | tf_op jit(solution)/shard_map/all_to_all | solution.py:254
  32.7 1.9 %collective-permute-start = (bf16[448,256]{1,0:T(8,128)(2,1)S(1)}, bf16[448,256]{1,0:T(8,128)(2,1)S(1)}, u32[]{:S(2)}, u32[]{:S(2)}) collective-permute-start(bf16[448,256]{1,0:T(8,128)(2,1)S(1)} %get-tuple-element.29.emb_ref), channel_id=1, source_target_pairs={{0,12},{12,0},{1,13},{13,1},{2,14},{14,2},{3,15},{15,3},{4,16},{16... | collective-permute-start | bytes 688136 | tf_op jit(solution)/shard_map/ppermute | solution.py:250
  34.7 1.4 collective-permute-done.other_ref
  36.1 2.1 %shard_map.95 = (bf16[32,32,256]{2,1,0:T(8,128)(2,1)}, bf16[96,256]{1,0:T(8,128)(2,1)S(1)}) custom-call(s32[2]{0:T(128)S(1)} %pad_add_fusion.core_ref, s32[32,8,128]{2,1,0:T(8,128)S(1)} %all-to-all-done.asked_ref, bf16[448,256]{1,0:T(8,128)(2,1)S(1)} %get-tuple-element.29.emb_ref, bf16[448,256]{1,0:T(8,128)(2,1)S(1)} %collective-permute-done.other_ref), custom_call_target="tpu_custom_call" | custom-call | flops 402653184 | bytes 2097152 | tf_op jit(solution)/shard_map/pallas_call | solution.py:39
  38.2 16.5 %all-to-all-done.1.pass_ref.recv_ref = bf16[32,48,256]{2,1,0:T(8,128)(2,1)S(1)} async-done(((bf16[32,48,256]{2,1,0:T(8,128)(2,1)}), bf16[32,48,256]{2,1,0:T(8,128)(2,1)S(1)}, u32[]{:S(2)}, u32[]{:S(2)}) %all-to-all-start.1) | async-done | bytes 786464 | tf_op jit(solution)/shard_map/all_to_all | solution.py:254
  54.7 5.5 %all-to-all-start.2 = ((bf16[32,32,256]{2,1,0:T(8,128)(2,1)}), bf16[32,32,256]{2,1,0:T(8,128)(2,1)S(1)}, u32[]{:S(2)}, u32[]{:S(2)}) async-start(bf16[32,32,256]{2,1,0:T(8,128)(2,1)} %get-tuple-element.34), calls=%async_computation.2 | async-start | bytes 1048576 | tf_op jit(solution)/shard_map/all_to_all | solution.py:254
  60.5 16.4 %all-to-all-done.2.rows_ref = bf16[32,32,256]{2,1,0:T(8,128)(2,1)S(1)} async-done(((bf16[32,32,256]{2,1,0:T(8,128)(2,1)}), bf16[32,32,256]{2,1,0:T(8,128)(2,1)S(1)}, u32[]{:S(2)}, u32[]{:S(2)}) %all-to-all-start.2) | async-done | bytes 524320 | tf_op jit(solution)/shard_map/all_to_all | solution.py:254
  76.9 1.0 shard_map.97
  77.9 39.1 %all_to_all.30.part_ref = f32[12,8,1664]{2,1,0:T(8,128)S(1)} all-to-all(f32[12,8,1664]{2,1,0:T(8,128)S(1)} %bitcast.8), channel_id=1, replica_groups=mesh['y'=8,'x'=4,'c'=2,'z'=12] {'z'}, dimensions={0} | all-to-all | bytes 1277952 | tf_op jit(solution)/shard_map/all_to_all | solution.py:254
  117.7 1.9 %collective-permute-start.1 = (f32[8,128]{1,0:T(8,128)S(1)}, f32[8,128]{1,0:T(8,128)S(1)}, u32[]{:S(2)}, u32[]{:S(2)}) collective-permute-start(f32[8,128]{1,0:T(8,128)S(1)} %get-tuple-element.38.mine_ref), channel_id=1, source_target_pairs={{0,12},{12,0},{1,13},{13,1},{2,14},{14,2},{3,15},{15,3},{4,16},{16... | collective-permute-start | bytes 12296 | tf_op jit(solution)/shard_map/ppermute | solution.py:250
  119.6 1.1 collective-permute-done.1.other_ref
  121.0 21.3 %all_to_all.31.grad_ref = bf16[12,8,1664]{2,1,0:T(8,128)(2,1)S(1)} all-to-all(bf16[12,8,1664]{2,1,0:T(8,128)(2,1)S(1)} %shard_map.99), channel_id=1, replica_groups=mesh['y'=8,'x'=4,'c'=2,'z'=12] {'z'}, dimensions={0} | all-to-all | bytes 638976 | tf_op jit(solution)/shard_map/all_to_all | solution.py:254
  142.3 1.3 shard_map.100
  143.6 6.5 %all-to-all-start.5 = ((bf16[32,48,256]{2,1,0:T(8,128)(2,1)}), bf16[32,48,256]{2,1,0:T(8,128)(2,1)S(1)}, u32[]{:S(2)}, u32[]{:S(2)}) async-start(bf16[32,48,256]{2,1,0:T(8,128)(2,1)} %get-tuple-element.42), calls=%async_computation.5 | async-start | bytes 1572864 | tf_op jit(solution)/shard_map/all_to_all | solution.py:254
  150.1 1.5 shard_map.101
  151.6 1.9 %collective-permute-start.2 = (f32[48,256]{1,0:T(8,128)S(1)}, f32[48,256]{1,0:T(8,128)S(1)}, u32[]{:S(2)}, u32[]{:S(2)}) collective-permute-start(f32[48,256]{1,0:T(8,128)S(1)} %get-tuple-element.44), channel_id=1, source_target_pairs={{0,12},{12,0},{1,13},{13,1},{2,14},{14,2},{3,15},{15,3},{4,16},{16... | collective-permute-start | bytes 147464 | tf_op jit(solution)/shard_map/ppermute | solution.py:250
  154.7 18.4 %all-to-all-done.5.parts_ref = bf16[32,48,256]{2,1,0:T(8,128)(2,1)S(1)} async-done(((bf16[32,48,256]{2,1,0:T(8,128)(2,1)}), bf16[32,48,256]{2,1,0:T(8,128)(2,1)S(1)}, u32[]{:S(2)}, u32[]{:S(2)}) %all-to-all-start.5) | async-done | bytes 786464 | tf_op jit(solution)/shard_map/all_to_all | solution.py:254
  (14 shorter events, 5.0 us)
Async XLA Ops:
  2.8 20.4 %all-to-all-start = ((s32[32,8,128]{2,1,0:T(8,128)}), s32[32,8,128]{2,1,0:T(8,128)S(1)}, u32[]{:S(2)}, u32[]{:S(2)}) async-start(s32[32,8,128]{2,1,0:T(8,128)} %get-tuple-element.27), calls=%async_computation | async-start | bytes 262144 | tf_op jit(solution)/shard_map/all_to_all | solution.py:254
  13.4 1.8 %copy-start = (bf16[336,4096]{1,0:T(8,128)(2,1)S(1)}, bf16[336,4096]{1,0:T(8,128)(2,1)}, u32[]{:S(2)}) copy-start(bf16[336,4096]{1,0:T(8,128)(2,1)} %nh_ref.1) | copy-start | bytes 8257540
  15.2 1.6 copy-start.1
  16.8 1.0 copy-start.2
  17.8 1.0 copy-start.3
  23.2 31.5 %all-to-all-start.1 = ((bf16[32,48,256]{2,1,0:T(8,128)(2,1)}), bf16[32,48,256]{2,1,0:T(8,128)(2,1)S(1)}, u32[]{:S(2)}, u32[]{:S(2)}) async-start(bf16[32,48,256]{2,1,0:T(8,128)(2,1)} %get-tuple-element.32), calls=%async_computation.1 | async-start | bytes 1572864 | tf_op jit(solution)/shard_map/all_to_all | solution.py:254
  32.7 3.4 %collective-permute-start = (bf16[448,256]{1,0:T(8,128)(2,1)S(1)}, bf16[448,256]{1,0:T(8,128)(2,1)S(1)}, u32[]{:S(2)}, u32[]{:S(2)}) collective-permute-start(bf16[448,256]{1,0:T(8,128)(2,1)S(1)} %get-tuple-element.29.emb_ref), channel_id=1, source_target_pairs={{0,12},{12,0},{1,13},{13,1},{2,14},{14,2},{3,15},{15,3},{4,16},{16... | collective-permute-start | bytes 688136 | tf_op jit(solution)/shard_map/ppermute | solution.py:250
  54.7 22.2 %all-to-all-start.2 = ((bf16[32,32,256]{2,1,0:T(8,128)(2,1)}), bf16[32,32,256]{2,1,0:T(8,128)(2,1)S(1)}, u32[]{:S(2)}, u32[]{:S(2)}) async-start(bf16[32,32,256]{2,1,0:T(8,128)(2,1)} %get-tuple-element.34), calls=%async_computation.2 | async-start | bytes 1048576 | tf_op jit(solution)/shard_map/all_to_all | solution.py:254
  117.7 3.1 %collective-permute-start.1 = (f32[8,128]{1,0:T(8,128)S(1)}, f32[8,128]{1,0:T(8,128)S(1)}, u32[]{:S(2)}, u32[]{:S(2)}) collective-permute-start(f32[8,128]{1,0:T(8,128)S(1)} %get-tuple-element.38.mine_ref), channel_id=1, source_target_pairs={{0,12},{12,0},{1,13},{13,1},{2,14},{14,2},{3,15},{15,3},{4,16},{16... | collective-permute-start | bytes 12296 | tf_op jit(solution)/shard_map/ppermute | solution.py:250
  143.6 29.5 %all-to-all-start.5 = ((bf16[32,48,256]{2,1,0:T(8,128)(2,1)}), bf16[32,48,256]{2,1,0:T(8,128)(2,1)S(1)}, u32[]{:S(2)}, u32[]{:S(2)}) async-start(bf16[32,48,256]{2,1,0:T(8,128)(2,1)} %get-tuple-element.42), calls=%async_computation.5 | async-start | bytes 1572864 | tf_op jit(solution)/shard_map/all_to_all | solution.py:254
  151.6 3.1 %collective-permute-start.2 = (f32[48,256]{1,0:T(8,128)S(1)}, f32[48,256]{1,0:T(8,128)S(1)}, u32[]{:S(2)}, u32[]{:S(2)}) collective-permute-start(f32[48,256]{1,0:T(8,128)S(1)} %get-tuple-element.44), channel_id=1, source_target_pairs={{0,12},{12,0},{1,13},{13,1},{2,14},{14,2},{3,15},{15,3},{4,16},{16... | collective-permute-start | bytes 147464 | tf_op jit(solution)/shard_map/ppermute | solution.py:250

commit v2 on v1

v2 whole, which is shorter than its diff:
```python
import math

import jax
import jax.numpy as jnp
import numpy as np
from jax import lax
from jax.experimental import pallas as pl
from jax.experimental.pallas import tpu as pltpu
from jax.sharding import Mesh
from jax.sharding import PartitionSpec as P

E = 3072
SCALE = 1.0 / math.sqrt(E)
F32 = jnp.float32
BF16 = jnp.bfloat16
I32 = jnp.int32
Q = 48
K = 7
POOL = 336
X, Y, Z = 4, 8, 12
CHIPS = X * Y
SLOT = 24
W = Q * CHIPS
H = W // 2
WP = W + 128
PASS = Y * Q
L0 = W + 7
NEG = -3.0e38
STEP = 8.0
TOP = 32700.0
TCOL, TCORE, ESCORE, EHARD = 7, 8, 9, 10


def iota(shape, dim):
    return lax.broadcasted_iota(I32, shape, dim)


def params(mib=24):
    return pltpu.CompilerParams(vmem_limit_bytes=mib * 2**20)


def call(kernel, out, *args, flops=0, nbytes=0, **kw):
    return pl.pallas_call(
        kernel,
        out_shape=out,
        compiler_params=params(),
        cost_estimate=pl.CostEstimate(flops=flops, bytes_accessed=nbytes, transcendentals=0),
        **kw,
    )(*args)


def dot(a, b, dims=(((1,), (0,)), ((), ()))):
    return lax.dot_general(a, b, dims, preferred_element_type=F32)


def requests(ids):
    owner = lax.shift_right_arithmetic(ids * 49933, 25)
    row = ids - owner * (2 * POOL)
    high, low = lax.shift_right_arithmetic(row, 4).astype(F32), (row & 15).astype(F32)
    marks = jnp.where(owner[None] == iota((CHIPS, 8, 128), 0), 1.0, 0.0)
    flat = marks.reshape(CHIPS * 8, 128).astype(BF16)
    upper = jnp.where(iota((128, 128), 0) < iota((128, 128), 1), 1.0, 0.0).astype(BF16)
    a, b = iota((256, 256), 0), iota((256, 256), 1)
    lower = jnp.where((b < a) & (lax.shift_right_logical(a, 3) == lax.shift_right_logical(b, 3)), 1.0, 0.0).astype(BF16)
    above = dot(lower, flat).astype(BF16)
    before = dot(flat, upper) + dot(above, jnp.ones((128, 128), BF16))
    rank = jnp.sum(marks * before.reshape(CHIPS, 8, 128), axis=0)
    x, y = owner & 3, lax.shift_right_arithmetic(owner, 2)
    places = (x.astype(F32) * 32.0 + rank).T
    lanes = iota((128, 128), 1).astype(F32)
    total = jnp.zeros((2 * Y, 128), F32)
    for k in range(K):
        mine = y[k : k + 1, :] == iota((Y, 128), 0)
        left = jnp.concatenate(
            [jnp.where(mine, high[k : k + 1, :], 0.0), jnp.where(mine, low[k : k + 1, :], 0.0)], axis=0
        )
        right = jnp.where(places[:, k : k + 1] == lanes, 1.0, 0.0)
        total += dot(left.astype(BF16), right.astype(BF16))
    slots = ((x * Y + y).astype(F32) * SLOT + rank).T
    return total, slots


def passage_project_kernel(ids_ref, ph_ref, w_ref, send_ref, slot_ref, acc, wanted):
    step = pl.program_id(0)

    @pl.when(step == 0)
    def _():
        acc[...] = jnp.zeros_like(acc)
        total, slots = requests(ids_ref[...])
        slot_ref[...] = slots
        wanted[:, 0:128] = total
        wanted[:, 128:] = jnp.zeros((2 * Y, 128), F32)

    acc[...] += dot(ph_ref[...], w_ref[...])

    @pl.when(step == pl.num_programs(0) - 1)
    def _():
        passages = acc[...].astype(BF16)
        line = iota((16, 256), 0)
        for y in range(Y):
            send_ref[y, 0:Q] = passages
            parts = jnp.where(line == 0, wanted[y : y + 1], jnp.where(line == 1, wanted[Y + y : Y + y + 1], 0.0))
            send_ref[y, Q:] = parts.astype(BF16)


def project_kernel(qh_ref, nh_ref, w_ref, pos_ref, emb_ref, acc):
    step = pl.program_id(0)

    @pl.when(step == 0)
    def _():
        acc[...] = jnp.zeros_like(acc)

    w = w_ref[...]
    acc[0:Q] += dot(qh_ref[...], w)
    acc[Q:] += dot(nh_ref[...], w)

    @pl.when(step == pl.num_programs(0) - 1)
    def _():
        emb_ref[0 : Q + POOL] = acc[...].astype(BF16)
        pos = jnp.broadcast_to(pos_ref[...], (16, 256))
        high = lax.shift_right_arithmetic(pos, 6).astype(F32)
        low = (pos & 63).astype(F32)
        emb_ref[Q + POOL :] = jnp.where(iota((16, 256), 0) == 0, high, low).astype(BF16)


def relay_kernel(recv_ref, send_ref):
    block = recv_ref[:, 0:Q].reshape(PASS, 256)
    tail = recv_ref[:, Q:].astype(F32)
    high, low = tail[:, 0, 0:128], tail[:, 1, 0:128]
    both = jnp.concatenate([high, low], axis=0)
    for x in range(X):
        send_ref[x, 0:PASS] = block
        part = jnp.concatenate([both[:, 32 * x : 32 * x + 32], jnp.zeros((2 * Y, 224), F32)], axis=1)
        send_ref[x, PASS:] = part.astype(BF16)


def answer_kernel(core_ref, recv_ref, emb_ref, other_ref, send_ref, both_ref, pool):
    core = core_ref[0]
    pool[0:POOL] = emb_ref[Q : Q + POOL]
    pool[POOL : 2 * POOL] = other_ref[Q : Q + POOL]
    pool[2 * POOL :] = jnp.zeros((768 - 2 * POOL, 256), BF16)
    first = core == 0

    @pl.when(first)
    def _():
        both_ref[0:Q] = emb_ref[0:Q]
        both_ref[Q:] = other_ref[0:Q]

    @pl.when(jnp.logical_not(first))
    def _():
        both_ref[0:Q] = other_ref[0:Q]
        both_ref[Q:] = emb_ref[0:Q]

    lanes = iota((SLOT, 768), 1).astype(F32)
    rows = pool[...]
    for x in range(X):
        parts = recv_ref[x, PASS:].astype(F32)
        asked = parts[0:Y, 0:128] * 16.0 + parts[Y:, 0:128]
        flipped = jnp.where(asked >= POOL, asked - POOL, asked + POOL)
        wanted = jnp.where(core == 1, flipped, asked).T
        hot = jnp.concatenate([jnp.where(wanted[0:SLOT, y : y + 1] == lanes, 1.0, 0.0) for y in range(Y)], axis=0)
        found = dot(hot.astype(BF16), rows)
        left = found[:, 0:128].reshape(Y, SLOT, 128)
        right = found[:, 128:].reshape(Y, SLOT, 128)
        send_ref[Y * x : Y * (x + 1)] = jnp.concatenate([left, right], axis=1).astype(BF16)


def score_kernel(both_ref, pass_ref, part_ref):
    queries = both_ref[...]
    for x in range(X):
        part_ref[:, PASS * x : PASS * (x + 1)] = dot(queries, pass_ref[x, 0:PASS], (((1,), (1,)), ((), ())))


def quantize(values):
    most = jnp.maximum(jnp.max(jnp.abs(values), axis=1, keepdims=True), 1e-30)
    power = jnp.ceil(jnp.log2(most) * STEP + 0.02)
    return jnp.floor(values * (TOP * jnp.exp2(power * (-1.0 / STEP))) + 0.5), power


def hard_kernel(core_ref, part_ref, rows_ref, emb_ref, other_ref, slot_ref, send_ref, fetched_ref):
    first = core_ref[0] == 0
    mine = emb_ref[0:Q]
    got = rows_ref[...].astype(F32)
    left = got[:, 0:SLOT].reshape(CHIPS * SLOT, 128)
    right = got[:, SLOT:].reshape(CHIPS * SLOT, 128)
    rows = jnp.concatenate([left, right], axis=1).astype(BF16)
    places = iota((Q, CHIPS * SLOT), 1).astype(F32)
    slots = slot_ref[...]
    hot = jnp.concatenate([jnp.where(slots[0:Q, k : k + 1] == places, 1.0, 0.0) for k in range(K)], axis=0)
    found = dot(hot.astype(BF16), rows)
    lane = iota((Q, 128), 1)
    mine32 = mine.astype(F32)
    hard = jnp.zeros((Q, 128), F32)
    for k in range(K):
        row = found[Q * k : Q * (k + 1)]
        fetched_ref[k] = row.astype(BF16)
        hard = jnp.where(lane == k, jnp.sum(mine32 * row, axis=1, keepdims=True), hard)
    hard, power = quantize(hard)
    hard = jnp.where(lane == EHARD, power, hard)

    def target(ref):
        pos = ref[Q + POOL :].astype(F32).T
        pos = (pos[0:Q, 0:1] * 64.0 + pos[0:Q, 1:2]).astype(I32)
        index = pos.astype(F32) + 0.5
        chip = (index * (1.0 / 96.0)).astype(I32)
        dp = (index * (1.0 / 48.0)).astype(I32)
        place = (chip & 3) * Y + lax.shift_right_arithmetic(chip, 2)
        column = (place * Q + pos - dp * Q).astype(F32)
        return jnp.where(lane == TCOL, column, jnp.where(lane == TCORE, (dp - 2 * chip).astype(F32), 0.0))

    mine_extra, other_extra = hard + target(emb_ref), target(other_ref)
    extra = jnp.concatenate(
        [jnp.where(first, mine_extra, other_extra), jnp.where(first, other_extra, mine_extra)], axis=0
    )
    scores, power = quantize(part_ref[...])
    extra = jnp.where(iota((2 * Q, 128), 1) == ESCORE, power, extra)
    left = jnp.concatenate([scores[:, 0:H], extra], axis=1).reshape(Z, 8, H + 128)
    right = jnp.concatenate([scores[:, H:], jnp.zeros((2 * Q, 128), F32)], axis=1).reshape(Z, 8, H + 128)
    send_ref[...] = jnp.concatenate([left, right], axis=1).astype(I32).astype(jnp.int16)


def stats_kernel(core_ref, part_ref, logit_ref, stat_ref):
    core = core_ref[0]
    z = core_ref[1]
    own = (z >= Z // 2) == (core == 1)
    left = jnp.zeros((8, H), F32)
    right = jnp.zeros((8, H), F32)
    hard = jnp.zeros((8, 128), F32)
    for i in range(Z):
        part = part_ref[i].astype(I32).astype(F32)
        extra = part[0:8, H:]
        scale = jnp.exp2(extra[:, ESCORE : ESCORE + 1] * (1.0 / STEP)) * (SCALE / TOP)
        left += part[0:8, 0:H] * scale
        right += part[8:16, 0:H] * scale
        hard += extra * (jnp.exp2(extra[:, EHARD : EHARD + 1] * (1.0 / STEP)) * (SCALE / TOP))
    lane = iota((8, 128), 1)
    hard = jnp.where(own & (lane < K), hard, NEG)
    logits = jnp.concatenate([left, right, hard], axis=1)
    peak = jnp.max(logits, axis=1, keepdims=True)
    mass = jnp.sum(jnp.where(logits > NEG, jnp.exp(logits - peak), 0.0), axis=1, keepdims=True)
    column = jnp.where(extra[:, TCORE : TCORE + 1] == core.astype(F32), extra[:, TCOL : TCOL + 1], -1.0)
    aim = iota((8, WP), 1).astype(F32) == column
    hit = jnp.sum(jnp.where(aim, logits, 0.0), axis=1, keepdims=True)
    logit_ref[...] = logits
    stat_ref[...] = jnp.where(
        lane == 0, peak, jnp.where(lane == 1, mass, jnp.where(lane == 2, hit, jnp.where(lane == 3, column, 0.0)))
    )


def grad_kernel(logit_ref, mine_ref, other_ref, send_ref):
    mine, other = mine_ref[...], other_ref[...]
    peak = jnp.maximum(mine[:, 0:1], other[:, 0:1])
    mass = mine[:, 1:2] * jnp.exp(mine[:, 0:1] - peak) + other[:, 1:2] * jnp.exp(other[:, 0:1] - peak)
    loss = peak + jnp.log(mass) - (mine[:, 2:3] + other[:, 2:3])
    logits = logit_ref[...]
    lane = iota((8, WP), 1)
    probs = jnp.where(logits > NEG, jnp.exp(logits - peak) / mass, 0.0)
    grads = probs - jnp.where(lane.astype(F32) == mine[:, 3:4], 1.0, 0.0)
    high = loss.astype(BF16).astype(F32)
    mid = (loss - high).astype(BF16).astype(F32)
    low = loss - high - mid
    grads = jnp.where(lane == L0, high, jnp.where(lane == L0 + 1, mid, jnp.where(lane == L0 + 2, low, grads)))
    send_ref[...] = jnp.broadcast_to(grads.astype(BF16)[None], (Z, 8, WP))


def turn_kernel(grad_ref, both_ref, send_ref, flat_ref):
    grads = grad_ref[...].astype(F32).reshape(Z * 8, WP).astype(BF16)
    flat_ref[...] = grads
    queries = both_ref[...]
    for x in range(X):
        part = dot(grads[:, PASS * x : PASS * (x + 1)], queries, (((0,), (0,)), ((), ())))
        send_ref[Y * x : Y * (x + 1)] = part.astype(BF16).reshape(Y, Q, 256)


def query_kernel(core_ref, grad_ref, recv_ref, fetched_ref, emb_ref, mine_ref, other_ref, hard_ref, loss_ref):
    first = core_ref[0] == 0
    total = jnp.zeros((2 * Q, 256), F32)
    for x in range(X):
        total += dot(grad_ref[:, PASS * x : PASS * (x + 1)], recv_ref[x, 0:PASS])
    upper, lower = total[0:Q], total[Q:]
    other_ref[...] = jnp.where(first, lower, upper)
    tail = grad_ref[:, W:].astype(F32)
    mine = jnp.where(first, tail[0:Q], tail[Q:])
    queries = emb_ref[0:Q].astype(F32)
    result = jnp.where(first, upper, lower)
    for k in range(K):
        weight = mine[:, k : k + 1]
        result += weight * fetched_ref[k].astype(F32)
        hard_ref[k] = weight * queries
    mine_ref[...] = result
    loss = mine[:, K : K + 1] + mine[:, K + 1 : K + 2] + mine[:, K + 2 : K + 3]
    loss_ref[...] = jnp.broadcast_to(loss, (Q, 128)).T[0:8]


def passage_kernel(parts_ref, mine_ref, other_ref, out_ref, query_ref):
    total = parts_ref[0].astype(F32)
    for j in range(1, CHIPS):
        total += parts_ref[j].astype(F32)
    out_ref[...] = total
    query_ref[...] = mine_ref[...] + other_ref[...]


def swap(x):
    return lax.ppermute(x, "c", [(0, 1), (1, 0)])


def exchange(x, axes):
    return lax.all_to_all(x, axes, split_axis=0, concat_axis=0, tiled=True)


def shape(dims, dtype):
    return jax.ShapeDtypeStruct(dims, dtype)


SMEM = pl.BlockSpec(memory_space=pltpu.SMEM)
VMEM = pl.BlockSpec(memory_space=pltpu.VMEM)


def local(query_hidden, passage_hidden, negative_hidden, projection, positive, hard_ids):
    place = jnp.stack([lax.axis_index("c"), lax.axis_index("z")]).astype(I32)
    ids = jnp.pad(hard_ids.T, ((0, 1), (0, 128 - Q)), constant_values=-1)
    pos = jnp.pad(positive[None, :], ((0, 0), (0, 256 - Q)))
    steps = 4
    depth = query_hidden.shape[1] // steps
    send, slots = call(
        passage_project_kernel,
        (shape((Y, Q + 16, 256), BF16), shape((128, 8), F32)),
        ids,
        passage_hidden,
        projection,
        grid=(steps,),
        in_specs=[
            pl.BlockSpec((8, 128), lambda i: (0, 0)),
            pl.BlockSpec((Q, depth), lambda i: (0, i)),
            pl.BlockSpec((depth, 256), lambda i: (i, 0)),
        ],
        out_specs=[
            pl.BlockSpec((Y, Q + 16, 256), lambda i: (0, 0, 0)),
            pl.BlockSpec((128, 8), lambda i: (0, 0)),
        ],
        scratch_shapes=[pltpu.VMEM((Q, 256), F32), pltpu.VMEM((2 * Y, 256), F32)],
        flops=2 * 48 * 4096 * 256,
        nbytes=3 * 2**20,
    )
    row = exchange(send, "y")
    emb = call(
        project_kernel,
        shape((Q + POOL + 16, 256), BF16),
        query_hidden,
        negative_hidden,
        projection,
        pos,
        grid=(steps,),
        in_specs=[
            pl.BlockSpec((Q, depth), lambda i: (0, i)),
            pl.BlockSpec((POOL, depth), lambda i: (0, i)),
            pl.BlockSpec((depth, 256), lambda i: (i, 0)),
            pl.BlockSpec((1, 256), lambda i: (0, 0)),
        ],
        out_specs=pl.BlockSpec((Q + POOL + 16, 256), lambda i: (0, 0)),
        scratch_shapes=[pltpu.VMEM((Q + POOL, 256), F32)],
        flops=2 * 384 * 4096 * 256,
        nbytes=6 * 2**20,
    )
    other = swap(emb)
    recv = exchange(call(relay_kernel, shape((X, PASS + 16, 256), BF16), row, nbytes=2**20), "x")
    answers, both = call(
        answer_kernel,
        (shape((CHIPS, 2 * SLOT, 128), BF16), shape((2 * Q, 256), BF16)),
        place,
        recv,
        emb,
        other,
        in_specs=[SMEM, VMEM, VMEM, VMEM],
        scratch_shapes=[pltpu.VMEM((768, 256), BF16)],
        flops=2 * 768 * 768 * 256,
        nbytes=2 * 2**20,
    )
    rows = exchange(answers, ("x", "y"))
    part = call(
        score_kernel, shape((2 * Q, W), F32), both, recv, flops=2 * 96 * 1536 * 256, nbytes=2 * 2**20
    )
    send, fetched = call(
        hard_kernel,
        (shape((Z, 16, H + 128), jnp.int16), shape((K, Q, 256), BF16)),
        place,
        part,
        rows,
        emb,
        other,
        slots,
        in_specs=[SMEM, VMEM, VMEM, VMEM, VMEM, VMEM],
        flops=2 * 336 * 1024 * 256,
        nbytes=3 * 2**20,
    )
    parts = exchange(send, "z")
    logits, stat = call(
        stats_kernel,
        (shape((8, WP), F32), shape((8, 128), F32)),
        place,
        parts,
        in_specs=[SMEM, VMEM],
        nbytes=2**20,
    )
    stat_other = swap(stat)
    grads = exchange(call(grad_kernel, shape((Z, 8, WP), BF16), logits, stat, stat_other, nbytes=2**19), "z")
    sums, flat = call(
        turn_kernel,
        (shape((CHIPS, Q, 256), BF16), shape((Z * 8, WP), BF16)),
        grads,
        both,
        flops=2 * 96 * 1536 * 256,
        nbytes=2 * 2**20,
    )
    sums = exchange(sums, ("x", "y"))
    query_mine, query_other, hard_grad, loss = call(
        query_kernel,
        (shape((Q, 256), F32), shape((Q, 256), F32), shape((K, Q, 256), F32), shape((8, Q), F32)),
        place,
        flat,
        recv,
        fetched,
        emb,
        in_specs=[SMEM, VMEM, VMEM, VMEM, VMEM],
        flops=2 * 96 * 1536 * 256,
        nbytes=3 * 2**20,
    )
    query_back = swap(query_other)
    passage_grad, query_grad = call(
        passage_kernel,
        (shape((Q, 256), F32), shape((Q, 256), F32)),
        sums,
        query_mine,
        query_back,
        nbytes=2**20,
    )
    return (loss[0], query_grad, passage_grad, jnp.transpose(hard_grad, (1, 0, 2)))


def solution(mesh):
    devices = np.asarray(mesh.devices)
    view = Mesh(devices.reshape(Y, X, 2, Z), ("y", "x", "c", "z"))
    dp = ("y", "x", "c")
    return jax.shard_map(
        local,
        mesh=view,
        in_specs=(P(dp, None), P(dp, None), P(dp, None), P(None, "z"), P(dp), P(dp, None)),
        out_specs=(P(dp), P(dp, "z"), P(dp, "z"), P(dp, None, "z")),
        check_vma=False,
    )
```

time: 175 us -> 148 us (0.85)
  the two profiles are of different devices: /device:TPU:64 before, /device:TPU:72 now
where the time goes in v2:
time: 148 us; the launch traced here: 147 us
  blocking collectives  68.8 us (46%)
  waiting for transfers between devices  37.4 us (25%)
  starting transfers between devices  21.2 us (14%)
  Pallas kernels  11.9 us (8%)
  local copies, waits for them, and re-layouts  7.11 us (5%)
    all_to_all x3, blocking collectives, exchange(): return lax.all_to_all(x, axes, split_axis=0, concat_axis=0, tiled=True)  68.8 us
    all_to_all x3, waiting for transfers between devices, exchange(): return lax.all_to_all(x, axes, split_axis=0, concat_axis=0, tiled=True)  34.2 us
    all_to_all x3, starting transfers between devices, exchange(): return lax.all_to_all(x, axes, split_axis=0, concat_axis=0, tiled=True)  15.3 us
    pallas_call x11, Pallas kernels, call(): pl.pallas_call(kernel, out_shape=out, compiler_params=params(), cost_esti...  11.9 us
    unnamed x18, local copies, waits for them, and re-layouts  5.9 us
    ppermute x3, starting transfers between devices, swap(): return lax.ppermute(x, 'c', [(0, 1), (1, 0)])  5.87 us
    ppermute x3, waiting for transfers between devices, swap(): return lax.ppermute(x, 'c', [(0, 1), (1, 0)])  3.15 us
  transfers between devices with their start and end apart: 6, of which 6 were waited for; matrix products, arithmetic and copies ran while one was open for 0% of the time, Pallas kernels for 3%

profile of v2, /device:TPU:72, one launch (start us, length us, event | category | flops | bytes accessed | tf_op | source)
XLA Modules:
  0.0 147.2 jit_solution(6247602764628166457)
XLA Ops:
  1.3 1.6 %copy-done = bf16[4096,256]{1,0:T(8,128)(2,1)S(1)} copy-done((bf16[4096,256]{1,0:T(8,128)(2,1)S(1)}, bf16[4096,256]{1,0:T(8,128)(2,1)}, u32[]{:S(2)}) %copy-start) | copy-done | bytes 2097176
  2.9 1.0 copy-done.4
  3.9 1.7 %shard_map.93 = (bf16[8,64,256]{2,1,0:T(8,128)(2,1)S(1)}, f32[128,8]{1,0:T(8,128)S(1)}) custom-call(s32[8,128]{1,0:T(8,128)S(1)} %pad.8.ids_ref, bf16[48,4096]{1,0:T(8,128)(2,1)S(1)} %copy-done.4, bf16[4096,256]{1,0:T(8,128)(2,1)S(1)} %copy-done), custom_call_target="tpu_custom_call" | custom-call | flops 100663296 | bytes 3145728 | tf_op jit(solution)/shard_map/pallas_call | solution.py:43
  6.3 17.8 %all_to_all.30.recv_ref = bf16[8,64,256]{2,1,0:T(8,128)(2,1)S(1)} all-to-all(bf16[8,64,256]{2,1,0:T(8,128)(2,1)S(1)} %get-tuple-element.20), channel_id=1, replica_groups=mesh['y'=8,'x'=4,'c'=2,'z'=12] {'y'}, dimensions={0} | all-to-all | bytes 524288 | tf_op jit(solution)/shard_map/all_to_all | solution.py:308
  24.1 0.9 copy-done.2
  25.0 4.3 %all-to-all-start.1 = ((bf16[4,400,256]{2,1,0:T(8,128)(2,1)}), bf16[4,400,256]{2,1,0:T(8,128)(2,1)S(1)}, u32[]{:S(2)}, u32[]{:S(2)}) async-start(bf16[4,400,256]{2,1,0:T(8,128)(2,1)} %copy-done.2), calls=%async_computation.1 | async-start | bytes 1638400 | tf_op jit(solution)/shard_map/all_to_all | solution.py:308
  29.3 1.8 %copy-done.3 = bf16[336,4096]{1,0:T(8,128)(2,1)S(1)} copy-done((bf16[336,4096]{1,0:T(8,128)(2,1)S(1)}, bf16[336,4096]{1,0:T(8,128)(2,1)}, u32[]{:S(2)}) %copy-start.3) | copy-done | bytes 2752536
  31.1 2.0 %shard_map.95.emb_ref = bf16[400,256]{1,0:T(8,128)(2,1)S(1)} custom-call(bf16[48,4096]{1,0:T(8,128)(2,1)S(1)} %copy-done.5, bf16[336,4096]{1,0:T(8,128)(2,1)S(1)} %copy-done.3, bf16[4096,256]{1,0:T(8,128)(2,1)S(1)} %copy-done.1, s32[1,256]{1,0:T(1,128)S(1)} %pad.9.pos_ref), custom_call_target="tpu_custom_call" | custom-call | flops 805306368 | bytes 6291456 | tf_op jit(solution)/shard_map/pallas_call | solution.py:43
  33.1 2.1 %collective-permute-start = (bf16[400,256]{1,0:T(8,128)(2,1)S(1)}, bf16[400,256]{1,0:T(8,128)(2,1)S(1)}, u32[]{:S(2)}, u32[]{:S(2)}) collective-permute-start(bf16[400,256]{1,0:T(8,128)(2,1)S(1)} %shard_map.95.emb_ref), channel_id=1, source_target_pairs={{0,12},{12,0},{1,13},{13,1},{2,14},{14,2},{3,15},{15,3},{4,16},{16... | collective-permute-start | bytes 614408 | tf_op jit(solution)/shard_map/ppermute | solution.py:304
  35.3 1.3 collective-permute-done.other_ref
  36.6 2.8 %all-to-all-done.1.recv_ref.pass_ref = bf16[4,400,256]{2,1,0:T(8,128)(2,1)S(1)} async-done(((bf16[4,400,256]{2,1,0:T(8,128)(2,1)}), bf16[4,400,256]{2,1,0:T(8,128)(2,1)S(1)}, u32[]{:S(2)}, u32[]{:S(2)}) %all-to-all-start.1) | async-done | bytes 819232 | tf_op jit(solution)/shard_map/all_to_all | solution.py:308
  39.4 2.0 %shard_map.96 = (bf16[32,48,128]{2,1,0:T(8,128)(2,1)}, bf16[96,256]{1,0:T(8,128)(2,1)S(1)}) custom-call(s32[2]{0:T(128)S(1)} %pad_add_fusion.core_ref, bf16[4,400,256]{2,1,0:T(8,128)(2,1)S(1)} %all-to-all-done.1.recv_ref.pass_ref, bf16[400,256]{1,0:T(8,128)(2,1)S(1)} %shard_map.95.emb_ref, bf16[400,256]{1,0:T(8,128)(2,1)S(1)} %collective-permute-done.other_ref), custom_call_target="tpu_custom_call" | custom-call | flops 301989888 | bytes 2097152 | tf_op jit(solution)/shard_map/pallas_call | solution.py:43
  41.3 6.0 %all-to-all-start.2 = ((bf16[32,48,128]{2,1,0:T(8,128)(2,1)}), bf16[32,48,128]{2,1,0:T(8,128)(2,1)S(1)}, u32[]{:S(2)}, u32[]{:S(2)}) async-start(bf16[32,48,128]{2,1,0:T(8,128)(2,1)} %get-tuple-element.22), calls=%async_computation.2 | async-start | bytes 786432 | tf_op jit(solution)/shard_map/all_to_all | solution.py:308
  47.7 12.9 %all-to-all-done.2.rows_ref = bf16[32,48,128]{2,1,0:T(8,128)(2,1)S(1)} async-done(((bf16[32,48,128]{2,1,0:T(8,128)(2,1)}), bf16[32,48,128]{2,1,0:T(8,128)(2,1)S(1)}, u32[]{:S(2)}, u32[]{:S(2)}) %all-to-all-start.2) | async-done | bytes 393248 | tf_op jit(solution)/shard_map/all_to_all | solution.py:308
  60.6 1.1 shard_map.98
  61.8 29.3 %all_to_all.31.part_ref = s16[12,16,896]{2,1,0:T(8,128)(2,1)S(1)} all-to-all(s16[12,16,896]{2,1,0:T(8,128)(2,1)S(1)} %get-tuple-element.24), channel_id=1, replica_groups=mesh['y'=8,'x'=4,'c'=2,'z'=12] {'z'}, dimensions={0} | all-to-all | bytes 688128 | tf_op jit(solution)/shard_map/all_to_all | solution.py:308
  92.0 1.9 %collective-permute-start.1 = (f32[8,128]{1,0:T(8,128)S(1)}, f32[8,128]{1,0:T(8,128)S(1)}, u32[]{:S(2)}, u32[]{:S(2)}) collective-permute-start(f32[8,128]{1,0:T(8,128)S(1)} %get-tuple-element.26.mine_ref), channel_id=1, source_target_pairs={{0,12},{12,0},{1,13},{13,1},{2,14},{14,2},{3,15},{15,3},{4,16},{16... | collective-permute-start | bytes 12296 | tf_op jit(solution)/shard_map/ppermute | solution.py:304
  93.9 1.1 collective-permute-done.1.other_ref
  95.2 21.8 %all_to_all.32.grad_ref = bf16[12,8,1664]{2,1,0:T(8,128)(2,1)S(1)} all-to-all(bf16[12,8,1664]{2,1,0:T(8,128)(2,1)S(1)} %shard_map.100), channel_id=1, replica_groups=mesh['y'=8,'x'=4,'c'=2,'z'=12] {'z'}, dimensions={0} | all-to-all | bytes 638976 | tf_op jit(solution)/shard_map/all_to_all | solution.py:308
  117.0 1.3 shard_map.101
  118.3 5.0 %all-to-all-start.5 = ((bf16[32,48,256]{2,1,0:T(8,128)(2,1)}), bf16[32,48,256]{2,1,0:T(8,128)(2,1)S(1)}, u32[]{:S(2)}, u32[]{:S(2)}) async-start(bf16[32,48,256]{2,1,0:T(8,128)(2,1)} %get-tuple-element.30), calls=%async_computation.5 | async-start | bytes 1572864 | tf_op jit(solution)/shard_map/all_to_all | solution.py:308
  123.3 1.5 %shard_map.102 = (f32[48,256]{1,0:T(8,128)S(1)}, f32[48,256]{1,0:T(8,128)S(1)}, f32[7,48,256]{2,1,0:T(8,128)}, f32[8,48]{1,0:T(8,128)S(1)}) custom-call(s32[2]{0:T(128)S(1)} %pad_add_fusion.core_ref, bf16[96,1664]{1,0:T(8,128)(2,1)S(1)} %get-tuple-element.27.grad_ref, bf16[4,400,256]{2,1,0:T(8,128)(2,1)S(1)} %all-to-all-done.1.recv_ref.pass_ref, ...), custom_call_target="tpu_custom_call" | custom-call | flops 75497472 | bytes 3145728 | tf_op jit(solution)/shard_map/pallas_call | solution.py:43
  124.8 1.9 %collective-permute-start.2 = (f32[48,256]{1,0:T(8,128)S(1)}, f32[48,256]{1,0:T(8,128)S(1)}, u32[]{:S(2)}, u32[]{:S(2)}) collective-permute-start(f32[48,256]{1,0:T(8,128)S(1)} %get-tuple-element.32), channel_id=1, source_target_pairs={{0,12},{12,0},{1,13},{13,1},{2,14},{14,2},{3,15},{15,3},{4,16},{16... | collective-permute-start | bytes 147464 | tf_op jit(solution)/shard_map/ppermute | solution.py:304
  127.9 18.6 %all-to-all-done.5.parts_ref = bf16[32,48,256]{2,1,0:T(8,128)(2,1)S(1)} async-done(((bf16[32,48,256]{2,1,0:T(8,128)(2,1)}), bf16[32,48,256]{2,1,0:T(8,128)(2,1)S(1)}, u32[]{:S(2)}, u32[]{:S(2)}) %all-to-all-start.5) | async-done | bytes 786464 | tf_op jit(solution)/shard_map/all_to_all | solution.py:308
  (24 shorter events, 4.9 us)
Async XLA Ops:
  1.3 1.6 %copy-start = (bf16[4096,256]{1,0:T(8,128)(2,1)S(1)}, bf16[4096,256]{1,0:T(8,128)(2,1)}, u32[]{:S(2)}) copy-start(bf16[4096,256]{1,0:T(8,128)(2,1)} %w_ref.3) | copy-start | bytes 6291460
  2.9 1.0 copy-start.4
  3.9 25.4 %copy-start.8 = (s32[48]{0:T(128)S(1)}, s32[48]{0:T(128)}, u32[]{:S(2)}) copy-start(s32[48]{0:T(128)} %param.10) | copy-start | bytes 580
  3.9 25.4 %copy-start.1 = (bf16[4096,256]{1,0:T(8,128)(2,1)S(1)}, bf16[4096,256]{1,0:T(8,128)(2,1)}, u32[]{:S(2)}) copy-start(bf16[4096,256]{1,0:T(8,128)(2,1)} %w_ref.3) | copy-start | bytes 6291460
  3.9 25.4 %copy-start.5 = (bf16[48,4096]{1,0:T(8,128)(2,1)S(1)}, bf16[48,4096]{1,0:T(8,128)(2,1)}, u32[]{:S(2)}) copy-start(bf16[48,4096]{1,0:T(8,128)(2,1)} %qh_ref.1) | copy-start | bytes 1179652
  5.6 0.6 copy-start.6
  24.1 0.9 copy-start.2
  25.0 14.3 %all-to-all-start.1 = ((bf16[4,400,256]{2,1,0:T(8,128)(2,1)}), bf16[4,400,256]{2,1,0:T(8,128)(2,1)S(1)}, u32[]{:S(2)}, u32[]{:S(2)}) async-start(bf16[4,400,256]{2,1,0:T(8,128)(2,1)} %copy-done.2), calls=%async_computation.1 | async-start | bytes 1638400 | tf_op jit(solution)/shard_map/all_to_all | solution.py:308
  29.3 1.8 %copy-start.3 = (bf16[336,4096]{1,0:T(8,128)(2,1)S(1)}, bf16[336,4096]{1,0:T(8,128)(2,1)}, u32[]{:S(2)}) copy-start(bf16[336,4096]{1,0:T(8,128)(2,1)} %nh_ref.1) | copy-start | bytes 8257540
  33.1 27.5 %copy-start.7 = (f32[128,8]{1,0:T(8,128)S(1)}, f32[128,8]{1,0:T(8,128)}, u32[]{:S(2)}) copy-start(f32[128,8]{1,0:T(8,128)} %copy-done.6) | copy-start | bytes 12292
  33.1 3.5 %collective-permute-start = (bf16[400,256]{1,0:T(8,128)(2,1)S(1)}, bf16[400,256]{1,0:T(8,128)(2,1)S(1)}, u32[]{:S(2)}, u32[]{:S(2)}) collective-permute-start(bf16[400,256]{1,0:T(8,128)(2,1)S(1)} %shard_map.95.emb_ref), channel_id=1, source_target_pairs={{0,12},{12,0},{1,13},{13,1},{2,14},{14,2},{3,15},{15,3},{4,16},{16... | collective-permute-start | bytes 614408 | tf_op jit(solution)/shard_map/ppermute | solution.py:304
  41.3 19.3 %all-to-all-start.2 = ((bf16[32,48,128]{2,1,0:T(8,128)(2,1)}), bf16[32,48,128]{2,1,0:T(8,128)(2,1)S(1)}, u32[]{:S(2)}, u32[]{:S(2)}) async-start(bf16[32,48,128]{2,1,0:T(8,128)(2,1)} %get-tuple-element.22), calls=%async_computation.2 | async-start | bytes 786432 | tf_op jit(solution)/shard_map/all_to_all | solution.py:308
  92.0 3.1 %collective-permute-start.1 = (f32[8,128]{1,0:T(8,128)S(1)}, f32[8,128]{1,0:T(8,128)S(1)}, u32[]{:S(2)}, u32[]{:S(2)}) collective-permute-start(f32[8,128]{1,0:T(8,128)S(1)} %get-tuple-element.26.mine_ref), channel_id=1, source_target_pairs={{0,12},{12,0},{1,13},{13,1},{2,14},{14,2},{3,15},{15,3},{4,16},{16... | collective-permute-start | bytes 12296 | tf_op jit(solution)/shard_map/ppermute | solution.py:304
  118.3 28.2 %all-to-all-start.5 = ((bf16[32,48,256]{2,1,0:T(8,128)(2,1)}), bf16[32,48,256]{2,1,0:T(8,128)(2,1)S(1)}, u32[]{:S(2)}, u32[]{:S(2)}) async-start(bf16[32,48,256]{2,1,0:T(8,128)(2,1)} %get-tuple-element.30), calls=%async_computation.5 | async-start | bytes 1572864 | tf_op jit(solution)/shard_map/all_to_all | solution.py:308
  124.8 3.1 %collective-permute-start.2 = (f32[48,256]{1,0:T(8,128)S(1)}, f32[48,256]{1,0:T(8,128)S(1)}, u32[]{:S(2)}, u32[]{:S(2)}) collective-permute-start(f32[48,256]{1,0:T(8,128)S(1)} %get-tuple-element.32), channel_id=1, source_target_pairs={{0,12},{12,0},{1,13},{13,1},{2,14},{14,2},{3,15},{15,3},{4,16},{16... | collective-permute-start | bytes 147464 | tf_op jit(solution)/shard_map/ppermute | solution.py:304

commit v3 on v2

v3 whole, which is shorter than its diff:
```python
import math

import jax
import jax.numpy as jnp
import numpy as np
from jax import lax
from jax.experimental import pallas as pl
from jax.experimental.pallas import tpu as pltpu
from jax.sharding import Mesh
from jax.sharding import PartitionSpec as P

E = 3072
STEPS, DEPTH = 4, 1024
SCALE = 1.0 / math.sqrt(E)
F32 = jnp.float32
BF16 = jnp.bfloat16
I32 = jnp.int32
Q = 48
K = 7
POOL = 336
X, YH, YL, Z = 4, 4, 2, 12
PEERS = YH * X
CHIPS = YL * PEERS
SLOT = 24
GROUP = 4 * Q
W = Q * PEERS
WP = W + 128
L0 = W + 7
NEG = -3.0e38
STEP = 8.0
TOP = 32700.0
TCOL, TCORE, ESCORE, EHARD = 7, 8, 9, 10


def iota(shape, dim):
    return lax.broadcasted_iota(I32, shape, dim)


def call(kernel, out, *args, flops=0, nbytes=0, mib=24, **kw):
    return pl.pallas_call(
        kernel,
        out_shape=out,
        compiler_params=pltpu.CompilerParams(vmem_limit_bytes=mib * 2**20),
        cost_estimate=pl.CostEstimate(flops=flops, bytes_accessed=nbytes, transcendentals=0),
        **kw,
    )(*args)


def dot(a, b, dims=(((1,), (0,)), ((), ()))):
    return lax.dot_general(a, b, dims, preferred_element_type=F32)


def request_kernel(place_ref, ids_ref, mine_ref, other_ref, slot_ref):
    block = jnp.concatenate([ids_ref[...], jnp.full((K, 128 - Q), -1, I32)], axis=1)
    ids = jnp.concatenate([block, jnp.full((1, 128), -1, I32)], axis=0)
    owner = lax.shift_right_arithmetic(ids * 49933, 25)
    row = ids - owner * (2 * POOL)
    high, low = lax.shift_right_arithmetic(row, 4).astype(F32), (row & 15).astype(F32)
    marks = jnp.where(owner[None] == iota((CHIPS, 8, 128), 0), 1.0, 0.0)
    flat = marks.reshape(CHIPS * 8, 128).astype(BF16)
    upper = jnp.where(iota((128, 128), 0) < iota((128, 128), 1), 1.0, 0.0).astype(BF16)
    a, b = iota((256, 256), 0), iota((256, 256), 1)
    lower = jnp.where((b < a) & (lax.shift_right_logical(a, 3) == lax.shift_right_logical(b, 3)), 1.0, 0.0).astype(BF16)
    above = dot(lower, flat).astype(BF16)
    before = dot(flat, upper) + dot(above, jnp.ones((128, 128), BF16))
    rank = jnp.sum(marks * before.reshape(CHIPS, 8, 128), axis=0)
    peer = lax.shift_right_arithmetic(owner, 3) * X + (owner & 3)
    parity = lax.shift_right_arithmetic(owner, 2) & 1
    away = parity != place_ref[2]
    cell = jnp.where(owner >= 0, peer + jnp.where(away, 2 * PEERS, 0), -1000)
    ranks = rank.T
    lanes = iota((128, 128), 1).astype(F32)
    line = iota((4 * PEERS, 128), 0)
    total = jnp.zeros((4 * PEERS, 128), F32)
    for k in range(K):
        here = cell[k : k + 1, :]
        left = jnp.where(here == line, high[k : k + 1, :], jnp.where(here + PEERS == line, low[k : k + 1, :], 0.0))
        right = jnp.where(ranks[:, k : k + 1] == lanes, 1.0, 0.0)
        total += dot(left.astype(BF16), right.astype(BF16))
    total = total.astype(BF16)
    mine_ref[...] = total[0 : 2 * PEERS]
    other_ref[...] = total[2 * PEERS :]
    slot_ref[...] = ((parity * PEERS + peer).astype(F32) * SLOT + rank).T


def passage_project_kernel(ph_ref, w_ref, out_ref):
    out_ref[...] = dot(ph_ref[...], w_ref[...]).astype(BF16)


def message_kernel(pass_ref, mine_ref, other_ref, send_ref):
    passages = pass_ref[...]
    mine, other = mine_ref[...].astype(F32), other_ref[...].astype(F32)
    line = iota((16, 128), 0)
    blank = jnp.zeros((16, 128), F32)
    for j in range(PEERS):
        part = jnp.where(
            line == 0,
            mine[j : j + 1],
            jnp.where(
                line == 1,
                mine[PEERS + j : PEERS + j + 1],
                jnp.where(line == 2, other[j : j + 1], jnp.where(line == 3, other[PEERS + j : PEERS + j + 1], 0.0)),
            ),
        )
        send_ref[j, 0:Q] = passages
        send_ref[j, Q:] = jnp.concatenate([part, blank], axis=1).astype(BF16)


def project_kernel(qh_ref, nh_ref, w_ref, pos_ref, emb_ref, acc):
    step = pl.program_id(0)

    @pl.when(step == 0)
    def _():
        acc[...] = jnp.zeros_like(acc)

    w = w_ref[...]
    acc[0:Q] += dot(qh_ref[...], w)
    acc[Q:] += dot(nh_ref[...], w)

    @pl.when(step == pl.num_programs(0) - 1)
    def _():
        emb_ref[0 : Q + POOL] = acc[...].astype(BF16)
        pos = jnp.broadcast_to(pos_ref[...], (16, 256))
        high = lax.shift_right_arithmetic(pos, 6).astype(F32)
        low = (pos & 63).astype(F32)
        emb_ref[Q + POOL :] = jnp.where(iota((16, 256), 0) == 0, high, low).astype(BF16)


def chip_kernel(place_ref, emb_ref, other_ref, chip_ref):
    first = place_ref[0] == 0

    def put(core, ref):
        chip_ref[Q * core : Q * (core + 1)] = ref[0:Q]
        chip_ref[2 * Q + 16 * core : 2 * Q + 16 * (core + 1)] = ref[Q + POOL :]

    @pl.when(first)
    def _():
        put(0, emb_ref)
        put(1, other_ref)

    @pl.when(jnp.logical_not(first))
    def _():
        put(0, other_ref)
        put(1, emb_ref)


def answer_kernel(place_ref, recv_ref, emb_ref, other_ref, send_ref, pass_ref, pool):
    core = place_ref[0]
    pool[0:POOL] = emb_ref[Q : Q + POOL]
    pool[POOL : 2 * POOL] = other_ref[Q : Q + POOL]
    pool[2 * POOL :] = jnp.zeros((768 - 2 * POOL, 256), BF16)
    pass_ref[...] = recv_ref[:, 0:Q].reshape(W, 256)
    tail = recv_ref[:, Q:].astype(F32)
    lanes = iota((SLOT, 768), 1).astype(F32)
    rows = pool[...]
    for part in range(2):
        asked = tail[:, 2 * part, 0:128] * 16.0 + tail[:, 2 * part + 1, 0:128]
        flipped = jnp.where(asked >= POOL, asked - POOL, asked + POOL)
        wanted = jnp.where(core == 1, flipped, asked).T
        base = ((place_ref[2] + part) & 1) * PEERS
        for g in range(2):
            hot = jnp.concatenate(
                [jnp.where(wanted[0:SLOT, j : j + 1] == lanes, 1.0, 0.0) for j in range(8 * g, 8 * g + 8)], axis=0
            )
            found = dot(hot.astype(BF16), rows)
            left = found[:, 0:128].reshape(8, SLOT, 128)
            right = found[:, 128:].reshape(8, SLOT, 128)
            send_ref[pl.ds(base + 8 * g, 8)] = jnp.concatenate([left, right], axis=1).astype(BF16)


def score_kernel(place_ref, chip_ref, next_ref, pass_ref, part_ref, group_ref):
    even = place_ref[2] == 0

    @pl.when(even)
    def _():
        group_ref[0 : 2 * Q] = chip_ref[0 : 2 * Q]
        group_ref[2 * Q :] = next_ref[0 : 2 * Q]

    @pl.when(jnp.logical_not(even))
    def _():
        group_ref[0 : 2 * Q] = next_ref[0 : 2 * Q]
        group_ref[2 * Q :] = chip_ref[0 : 2 * Q]

    part_ref[...] = dot(group_ref[...], pass_ref[...], (((1,), (1,)), ((), ())))


def quantize(values):
    most = jnp.maximum(jnp.max(jnp.abs(values), axis=1, keepdims=True), 1e-30)
    power = jnp.ceil(jnp.log2(most) * STEP + 0.02)
    return jnp.floor(values * (TOP * jnp.exp2(power * (-1.0 / STEP))) + 0.5), power


def hard_kernel(place_ref, part_ref, rows_ref, emb_ref, chip_ref, next_ref, slot_ref, send_ref, fetched_ref):
    parity = place_ref[2]
    got = rows_ref[...].astype(F32)
    left = got[:, 0:SLOT].reshape(CHIPS * SLOT, 128)
    right = got[:, SLOT:].reshape(CHIPS * SLOT, 128)
    rows = jnp.concatenate([left, right], axis=1).astype(BF16)
    places = iota((Q, CHIPS * SLOT), 1).astype(F32)
    slots = slot_ref[...]
    hot = jnp.concatenate([jnp.where(slots[0:Q, k : k + 1] == places, 1.0, 0.0) for k in range(K)], axis=0)
    found = dot(hot.astype(BF16), rows)
    lane = iota((Q, 128), 1)
    mine = emb_ref[0:Q].astype(F32)
    hard = jnp.zeros((Q, 128), F32)
    for k in range(K):
        row = found[Q * k : Q * (k + 1)]
        fetched_ref[k] = row.astype(BF16)
        hard = jnp.where(lane == k, jnp.sum(mine * row, axis=1, keepdims=True), hard)
    hard, power = quantize(hard)
    hard = jnp.where(lane == EHARD, power, hard)

    def target(ref, core):
        pos = ref[2 * Q + 16 * core : 2 * Q + 16 * (core + 1)].astype(F32).T
        pos = (pos[0:Q, 0:1] * 64.0 + pos[0:Q, 1:2]).astype(I32)
        index = pos.astype(F32) + 0.5
        chip = (index * (1.0 / 96.0)).astype(I32)
        dp = (index * (1.0 / 48.0)).astype(I32)
        peer = lax.shift_right_arithmetic(chip, 3) * X + (chip & 3)
        column = (peer * Q + pos - dp * Q).astype(F32)
        block = (dp - 2 * chip + 2 * (lax.shift_right_arithmetic(chip, 2) & 1)).astype(F32)
        return jnp.where(lane == TCOL, column, jnp.where(lane == TCORE, block, 0.0))

    own = 2 * parity + place_ref[0]
    scores, power = quantize(part_ref[...])
    for block in range(4):
        core = block % 2
        aim = jnp.where(parity == block // 2, target(chip_ref, core), target(next_ref, core))
        extra = aim + jnp.where(own == block, hard, 0.0)
        extra = jnp.where(lane == ESCORE, power[Q * block : Q * (block + 1)], extra)
        whole = jnp.concatenate([scores[Q * block : Q * (block + 1)], extra], axis=1)
        send_ref[3 * block : 3 * (block + 1)] = whole.reshape(3, 16, WP).astype(I32).astype(jnp.int16)


def stats_kernel(place_ref, part_ref, logit_ref, stat_ref):
    block = 2 * place_ref[2] + place_ref[0]
    z = place_ref[1]
    own = (z >= 3 * block) & (z < 3 * block + 3)
    scores = jnp.zeros((16, W), F32)
    hard = jnp.zeros((16, 128), F32)
    for i in range(Z):
        part = part_ref[i].astype(I32).astype(F32)
        extra = part[:, W:]
        scores += part[:, 0:W] * (jnp.exp2(extra[:, ESCORE : ESCORE + 1] * (1.0 / STEP)) * (SCALE / TOP))
        hard += extra * (jnp.exp2(extra[:, EHARD : EHARD + 1] * (1.0 / STEP)) * (SCALE / TOP))
    lane = iota((16, 128), 1)
    hard = jnp.where(own & (lane < K), hard, NEG)
    logits = jnp.concatenate([scores, hard], axis=1)
    peak = jnp.max(logits, axis=1, keepdims=True)
    mass = jnp.sum(jnp.where(logits > NEG, jnp.exp(logits - peak), 0.0), axis=1, keepdims=True)
    column = jnp.where(extra[:, TCORE : TCORE + 1] == block.astype(F32), extra[:, TCOL : TCOL + 1], -1.0)
    aim = iota((16, WP), 1).astype(F32) == column
    hit = jnp.sum(jnp.where(aim, logits, 0.0), axis=1, keepdims=True)
    logit_ref[...] = logits
    stat = jnp.where(
        lane == 0, peak, jnp.where(lane == 1, mass, jnp.where(lane == 2, hit, jnp.where(lane == 3, column, 0.0)))
    )
    stat_ref[...] = jnp.broadcast_to(stat[None], (4, 16, 128))


def grad_kernel(place_ref, logit_ref, stat_ref, send_ref):
    stats = [stat_ref[i] for i in range(4)]
    column = stat_ref[2 * place_ref[2] + place_ref[0]][:, 3:4]
    peak = stats[0][:, 0:1]
    for stat in stats[1:]:
        peak = jnp.maximum(peak, stat[:, 0:1])
    mass = sum(stat[:, 1:2] * jnp.exp(stat[:, 0:1] - peak) for stat in stats)
    loss = peak + jnp.log(mass) - sum(stat[:, 2:3] for stat in stats)
    logits = logit_ref[...]
    lane = iota((16, WP), 1)
    probs = jnp.where(logits > NEG, jnp.exp(logits - peak) / mass, 0.0)
    grads = probs - jnp.where(lane.astype(F32) == column, 1.0, 0.0)
    high = loss.astype(BF16).astype(F32)
    mid = (loss - high).astype(BF16).astype(F32)
    low = loss - high - mid
    grads = jnp.where(lane == L0, high, jnp.where(lane == L0 + 1, mid, jnp.where(lane == L0 + 2, low, grads)))
    send_ref[...] = jnp.broadcast_to(grads.astype(BF16)[None], (Z, 16, WP))


def turn_kernel(grad_ref, group_ref, send_ref):
    part = dot(grad_ref[:, 0:W], group_ref[...], (((0,), (0,)), ((), ())))
    send_ref[...] = part.astype(BF16).reshape(PEERS, Q, 256)


def query_kernel(place_ref, grad_ref, pass_ref, fetched_ref, emb_ref, keep_ref, give_ref, hard_ref, loss_ref, total):
    core, parity = place_ref[0], place_ref[2]
    total[...] = dot(grad_ref[:, 0:W], pass_ref[...])
    own = pl.multiple_of((2 * parity + core) * Q, 16)
    mine = grad_ref[pl.ds(own, Q), W:].astype(F32)
    queries = emb_ref[0:Q].astype(F32)
    result = total[pl.ds(own, Q)]
    for k in range(K):
        weight = mine[:, k : k + 1]
        result += weight * fetched_ref[k].astype(F32)
        hard_ref[k] = weight * queries
    total[pl.ds(own, Q)] = result
    for p in range(YL):
        keep_ref[p] = total[pl.ds(pl.multiple_of((2 * p + core) * Q, 16), Q)]
        give_ref[p] = total[pl.ds(pl.multiple_of((2 * p + 1 - core) * Q, 16), Q)]
    loss = mine[:, K : K + 1] + mine[:, K + 1 : K + 2] + mine[:, K + 2 : K + 3]
    loss_ref[...] = jnp.broadcast_to(loss, (Q, 128)).T[0:8]


def pair_kernel(place_ref, keep_ref, got_ref, mine_ref, give_ref):
    parity = place_ref[2]
    mine_ref[...] = keep_ref[parity] + got_ref[parity]
    give_ref[...] = keep_ref[1 - parity] + got_ref[1 - parity]


def passage_kernel(parts_ref, mine_ref, other_ref, out_ref, query_ref):
    total = parts_ref[0].astype(F32)
    for j in range(1, PEERS):
        total += parts_ref[j].astype(F32)
    out_ref[...] = total
    query_ref[...] = mine_ref[...] + other_ref[...]


def swap(x, axis="c"):
    return lax.ppermute(x, axis, [(0, 1), (1, 0)])


def exchange(x, axes):
    return lax.all_to_all(x, axes, split_axis=0, concat_axis=0, tiled=True)


def shape(dims, dtype):
    return jax.ShapeDtypeStruct(dims, dtype)


SMEM = pl.BlockSpec(memory_space=pltpu.SMEM)
VMEM = pl.BlockSpec(memory_space=pltpu.VMEM)


def local(query_hidden, passage_hidden, negative_hidden, projection, positive, hard_ids):
    place = jnp.stack([lax.axis_index("c"), lax.axis_index("z"), lax.axis_index("yl")]).astype(I32)
    wanted, handed, slots = call(
        request_kernel,
        (shape((2 * PEERS, 128), BF16), shape((2 * PEERS, 128), BF16), shape((128, 8), F32)),
        place,
        hard_ids.T,
        in_specs=[SMEM, VMEM],
    )
    handed = swap(handed, "yl")
    passages = call(
        passage_project_kernel,
        shape((Q, 256), BF16),
        passage_hidden,
        projection,
        flops=2 * 48 * 4096 * 256,
        nbytes=3 * 2**20,
    )
    send = call(message_kernel, shape((PEERS, Q + 16, 256), BF16), passages, wanted, handed, nbytes=2**19)
    recv = exchange(send, ("yh", "x"))

    pos = jnp.pad(positive[None, :], ((0, 0), (0, 256 - Q)))
    emb = call(
        project_kernel,
        shape((Q + POOL + 16, 256), BF16),
        query_hidden,
        negative_hidden,
        projection,
        pos,
        grid=(STEPS,),
        in_specs=[
            pl.BlockSpec((Q, DEPTH), lambda i: (0, i)),
            pl.BlockSpec((POOL, DEPTH), lambda i: (0, i)),
            pl.BlockSpec((DEPTH, 256), lambda i: (i, 0)),
            pl.BlockSpec((1, 256), lambda i: (0, 0)),
        ],
        out_specs=pl.BlockSpec((Q + POOL + 16, 256), lambda i: (0, 0)),
        scratch_shapes=[pltpu.VMEM((Q + POOL, 256), F32)],
        flops=2 * 384 * 4096 * 256,
        nbytes=6 * 2**20,
    )
    other = swap(emb)
    chip = call(
        chip_kernel,
        shape((2 * Q + 32, 256), BF16),
        place,
        emb,
        other,
        in_specs=[SMEM, VMEM, VMEM],
        nbytes=2**17,
    )
    beside = swap(chip, "yl")
    recv, emb, other, beside = lax.optimization_barrier((recv, emb, other, beside))
    answers, passages = call(
        answer_kernel,
        (shape((CHIPS, 2 * SLOT, 128), BF16), shape((W, 256), BF16)),
        place,
        recv,
        emb,
        other,
        in_specs=[SMEM] + [VMEM] * 3,
        scratch_shapes=[pltpu.VMEM((768, 256), BF16)],
        flops=2 * 768 * 768 * 256,
        nbytes=2 * 2**20,
    )
    rows = exchange(answers, ("yl", "yh", "x"))
    part, group = call(
        score_kernel,
        (shape((GROUP, W), F32), shape((GROUP, 256), BF16)),
        place,
        chip,
        beside,
        passages,
        in_specs=[SMEM] + [VMEM] * 3,
        flops=2 * 192 * 768 * 256,
        nbytes=2 * 2**20,
    )
    send, fetched = call(
        hard_kernel,
        (shape((Z, 16, WP), jnp.int16), shape((K, Q, 256), BF16)),
        place,
        part,
        rows,
        emb,
        chip,
        beside,
        slots,
        in_specs=[SMEM] + [VMEM] * 6,
        flops=2 * 336 * 768 * 256,
        nbytes=3 * 2**20,
    )
    parts = exchange(send, "z")
    logits, stat = call(
        stats_kernel,
        (shape((16, WP), F32), shape((4, 16, 128), F32)),
        place,
        parts,
        in_specs=[SMEM, VMEM],
        nbytes=2**20,
    )
    stat = exchange(stat, ("yl", "c"))
    grads = call(
        grad_kernel,
        shape((Z, 16, WP), BF16),
        place,
        logits,
        stat,
        in_specs=[SMEM, VMEM, VMEM],
        nbytes=2**19,
    )
    grads = exchange(grads, "z")
    grads = grads.reshape(GROUP, WP)
    sums = call(
        turn_kernel,
        shape((PEERS, Q, 256), BF16),
        grads,
        group,
        flops=2 * 192 * 768 * 256,
        nbytes=2 * 2**20,
    )
    sums = exchange(sums, ("yh", "x"))
    keep, give, hard_grad, loss = call(
        query_kernel,
        (shape((YL, Q, 256), F32), shape((YL, Q, 256), F32), shape((K, Q, 256), F32), shape((8, Q), F32)),
        place,
        grads,
        passages,
        fetched,
        emb,
        in_specs=[SMEM] + [VMEM] * 4,
        scratch_shapes=[pltpu.VMEM((GROUP, 256), F32)],
        flops=2 * 192 * 768 * 256,
        nbytes=3 * 2**20,
    )
    query_mine, query_give = call(
        pair_kernel,
        (shape((Q, 256), F32), shape((Q, 256), F32)),
        place,
        keep,
        swap(give),
        in_specs=[SMEM, VMEM, VMEM],
        nbytes=2**18,
    )
    passage_grad, query_grad = call(
        passage_kernel,
        (shape((Q, 256), F32), shape((Q, 256), F32)),
        sums,
        query_mine,
        swap(query_give, "yl"),
        nbytes=2**19,
    )
    return (loss[0], query_grad, passage_grad, jnp.transpose(hard_grad, (1, 0, 2)))


def solution(mesh):
    devices = np.asarray(mesh.devices)
    view = Mesh(devices.reshape(YH, YL, X, 2, Z), ("yh", "yl", "x", "c", "z"))
    dp = ("yh", "yl", "x", "c")
    return jax.shard_map(
        local,
        mesh=view,
        in_specs=(P(dp, None), P(dp, None), P(dp, None), P(None, "z"), P(dp), P(dp, None)),
        out_specs=(P(dp), P(dp, "z"), P(dp, "z"), P(dp, None, "z")),
        check_vma=False,
    )
```

time: 148 us -> 144 us (0.973)
  the two profiles are of different devices: /device:TPU:72 before, /device:TPU:64 now
where the time goes in v3:
time: 144 us; the launch traced here: 143 us
  blocking collectives  58.6 us (41%)
  starting transfers between devices  34.2 us (24%)
  waiting for transfers between devices  28.5 us (20%)
  Pallas kernels  15.2 us (11%)
  local copies, waits for them, and re-layouts  5.57 us (4%)
    all_to_all x3, blocking collectives, exchange(): return lax.all_to_all(x, axes, split_axis=0, concat_axis=0, tiled=True)  58.6 us
    all_to_all x3, starting transfers between devices, exchange(): return lax.all_to_all(x, axes, split_axis=0, concat_axis=0, tiled=True)  21.6 us
    all_to_all x3, waiting for transfers between devices, exchange(): return lax.all_to_all(x, axes, split_axis=0, concat_axis=0, tiled=True)  17.9 us
    pallas_call x14, Pallas kernels, call(): pl.pallas_call(kernel, out_shape=out, compiler_params=pltpu.CompilerParam...  15.2 us
    ppermute x5, starting transfers between devices, swap(): return lax.ppermute(x, axis, [(0, 1), (1, 0)])  12.6 us
    ppermute x5, waiting for transfers between devices, swap(): return lax.ppermute(x, axis, [(0, 1), (1, 0)])  10.5 us
    unnamed x14, local copies, waits for them, and re-layouts  5.05 us
  transfers between devices with their start and end apart: 8, of which 7 were waited for; matrix products, arithmetic and copies ran while one was open for 0% of the time, Pallas kernels for 4%

profile of v3, /device:TPU:64, one launch (start us, length us, event | category | flops | bytes accessed | tf_op | source)
XLA Modules:
  0.0 142.9 jit_solution(13762172843795626142)
XLA Ops:
  1.4 1.3 shard_map.96
  2.7 3.5 %collective-permute-start.1 = (bf16[32,128]{1,0:T(8,128)(2,1)S(1)}, bf16[32,128]{1,0:T(8,128)(2,1)S(1)}, u32[]{:S(2)}, u32[]{:S(2)}) collective-permute-start(bf16[32,128]{1,0:T(8,128)(2,1)S(1)} %get-tuple-element.28), channel_id=1, source_target_pairs={{0,96},{96,0},{1,97},{97,1},{2,98},{98,2},{3,99},{99,3},{4,100},{1... | collective-permute-start | bytes 24584 | tf_op jit(solution)/shard_map/ppermute | solution.py:319
  6.2 1.6 %copy-done = bf16[4096,256]{1,0:T(8,128)(2,1)S(1)} copy-done((bf16[4096,256]{1,0:T(8,128)(2,1)S(1)}, bf16[4096,256]{1,0:T(8,128)(2,1)}, u32[]{:S(2)}) %copy-start) | copy-done | bytes 2097176
  10.2 8.8 %all-to-all-start = ((bf16[16,64,256]{2,1,0:T(8,128)(2,1)}), bf16[16,64,256]{2,1,0:T(8,128)(2,1)S(1)}, u32[]{:S(2)}, u32[]{:S(2)}) async-start(bf16[16,64,256]{2,1,0:T(8,128)(2,1)} %shard_map.97), calls=%async_computation | async-start | bytes 1048576 | tf_op jit(solution)/shard_map/all_to_all | solution.py:323
  19.0 1.8 %copy-done.2 = bf16[336,4096]{1,0:T(8,128)(2,1)S(1)} copy-done((bf16[336,4096]{1,0:T(8,128)(2,1)S(1)}, bf16[336,4096]{1,0:T(8,128)(2,1)}, u32[]{:S(2)}) %copy-start.2) | copy-done | bytes 2752536
  20.8 2.0 %shard_map.93.emb_ref = bf16[400,256]{1,0:T(8,128)(2,1)S(1)} custom-call(bf16[48,4096]{1,0:T(8,128)(2,1)S(1)} %copy-done.4, bf16[336,4096]{1,0:T(8,128)(2,1)S(1)} %copy-done.2, bf16[4096,256]{1,0:T(8,128)(2,1)S(1)} %copy-done.1, s32[1,256]{1,0:T(1,128)S(1)} %pad.4.pos_ref), custom_call_target="tpu_custom_call" | custom-call | flops 805306368 | bytes 6291456 | tf_op jit(solution)/shard_map/pallas_call | solution.py:40
  22.7 1.9 %collective-permute-start = (bf16[400,256]{1,0:T(8,128)(2,1)S(1)}, bf16[400,256]{1,0:T(8,128)(2,1)S(1)}, u32[]{:S(2)}, u32[]{:S(2)}) collective-permute-start(bf16[400,256]{1,0:T(8,128)(2,1)S(1)} %shard_map.93.emb_ref), channel_id=1, source_target_pairs={{0,12},{12,0},{1,13},{13,1},{2,14},{14,2},{3,15},{15,3},{4,16},{16... | collective-permute-start | bytes 614408 | tf_op jit(solution)/shard_map/ppermute | solution.py:319
  24.7 1.4 collective-permute-done.other_ref
  26.7 3.3 %collective-permute-start.2 = (bf16[128,256]{1,0:T(8,128)(2,1)S(1)}, bf16[128,256]{1,0:T(8,128)(2,1)S(1)}, u32[]{:S(2)}, u32[]{:S(2)}) collective-permute-start(bf16[128,256]{1,0:T(8,128)(2,1)S(1)} %shard_map.94.chip_ref), channel_id=1, source_target_pairs={{0,96},{96,0},{1,97},{97,1},{2,98},{98,2},{3,99},{99,3},{4,100},{1... | collective-permute-start | bytes 196616 | tf_op jit(solution)/shard_map/ppermute | solution.py:319
  29.9 3.9 %collective-permute-done.2.next_ref = bf16[128,256]{1,0:T(8,128)(2,1)S(1)} collective-permute-done((bf16[128,256]{1,0:T(8,128)(2,1)S(1)}, bf16[128,256]{1,0:T(8,128)(2,1)S(1)}, u32[]{:S(2)}, u32[]{:S(2)}) %collective-permute-start.2) | collective-permute-done | bytes 65568 | tf_op jit(solution)/shard_map/ppermute | solution.py:319
  34.4 1.9 %shard_map.98 = (bf16[32,48,128]{2,1,0:T(8,128)(2,1)}, bf16[768,256]{1,0:T(8,128)(2,1)S(1)}) custom-call(s32[3]{0:T(128)S(1)} %pad_add_fusion.place_ref, bf16[16,64,256]{2,1,0:T(8,128)(2,1)S(1)} %all-to-all-done.recv_ref, bf16[400,256]{1,0:T(8,128)(2,1)S(1)} %shard_map.93.emb_ref, bf16[400,256]{1,0:T(8,128)(2,1)S(1)} %collective-permute-done.other_ref), custom_call_target="tpu_custom_call" | custom-call | flops 301989888 | bytes 2097152 | tf_op jit(solution)/shard_map/pallas_call | solution.py:40
  36.3 8.4 %all-to-all-start.1 = ((bf16[32,48,128]{2,1,0:T(8,128)(2,1)}), bf16[32,48,128]{2,1,0:T(8,128)(2,1)S(1)}, u32[]{:S(2)}, u32[]{:S(2)}) async-start(bf16[32,48,128]{2,1,0:T(8,128)(2,1)} %get-tuple-element.35), calls=%async_computation.1 | async-start | bytes 786432 | tf_op jit(solution)/shard_map/all_to_all | solution.py:323
  45.5 13.8 %all-to-all-done.1.rows_ref = bf16[32,48,128]{2,1,0:T(8,128)(2,1)S(1)} async-done(((bf16[32,48,128]{2,1,0:T(8,128)(2,1)}), bf16[32,48,128]{2,1,0:T(8,128)(2,1)S(1)}, u32[]{:S(2)}, u32[]{:S(2)}) %all-to-all-start.1) | async-done | bytes 393248 | tf_op jit(solution)/shard_map/all_to_all | solution.py:323
  59.3 1.8 %shard_map.100 = (s16[12,16,896]{2,1,0:T(8,128)(2,1)S(1)}, bf16[7,48,256]{2,1,0:T(8,128)(2,1)S(1)}) custom-call(s32[3]{0:T(128)S(1)} %pad_add_fusion.place_ref, f32[192,768]{1,0:T(8,128)S(1)} %get-tuple-element.34.part_ref, bf16[32,48,128]{2,1,0:T(8,128)(2,1)S(1)} %all-to-all-done.1.rows_ref, bf16[400,256]{1,0:T(8,128)(2,1)S(1)} %shard_map.93.emb_ref, ...), custom_call_target="tpu_custom_call" | custom-call | flops 132120576 | bytes 3145728 | tf_op jit(solution)/shard_map/pallas_call | solution.py:40
  61.2 29.4 %all_to_all.30.part_ref = s16[12,16,896]{2,1,0:T(8,128)(2,1)S(1)} all-to-all(s16[12,16,896]{2,1,0:T(8,128)(2,1)S(1)} %get-tuple-element.37), channel_id=1, replica_groups=mesh['yh'=4,'yl'=2,'x'=4,'c'=2,'z'=12] {'z'}, dimensions={0} | all-to-all | bytes 688128 | tf_op jit(solution)/shard_map/all_to_all | solution.py:323
  91.5 7.6 %all_to_all.31.stat_ref = f32[4,16,128]{2,1,0:T(8,128)S(1)} all-to-all(f32[4,16,128]{2,1,0:T(8,128)S(1)} %get-tuple-element.39), channel_id=1, replica_groups=mesh['yh'=4,'yl'=2,'x'=4,'c'=2,'z'=12] {'yl','c'}, dimensions={0} | all-to-all | bytes 65536 | tf_op jit(solution)/shard_map/all_to_all | solution.py:323
  99.8 21.6 %all_to_all.32 = bf16[12,16,896]{2,1,0:T(8,128)(2,1)S(1)} all-to-all(bf16[12,16,896]{2,1,0:T(8,128)(2,1)S(1)} %shard_map.102), channel_id=1, replica_groups=mesh['yh'=4,'yl'=2,'x'=4,'c'=2,'z'=12] {'z'}, dimensions={0} | all-to-all | bytes 688128 | tf_op jit(solution)/shard_map/all_to_all | solution.py:323
  122.5 4.5 %all-to-all-start.5 = ((bf16[16,48,256]{2,1,0:T(8,128)(2,1)}), bf16[16,48,256]{2,1,0:T(8,128)(2,1)S(1)}, u32[]{:S(2)}, u32[]{:S(2)}) async-start(bf16[16,48,256]{2,1,0:T(8,128)(2,1)} %shard_map.104), calls=%async_computation.5 | async-start | bytes 786432 | tf_op jit(solution)/shard_map/all_to_all | solution.py:323
  126.9 1.5 %shard_map.103 = (f32[2,48,256]{2,1,0:T(8,128)S(1)}, f32[2,48,256]{2,1,0:T(8,128)S(1)}, f32[7,48,256]{2,1,0:T(8,128)}, f32[8,48]{1,0:T(8,128)S(1)}) custom-call(s32[3]{0:T(128)S(1)} %pad_add_fusion.place_ref, bf16[192,896]{1,0:T(8,128)(2,1)S(1)} %bitcast.10, bf16[768,256]{1,0:T(8,128)(2,1)S(1)} %get-tuple-element.33.pass_ref, ...), custom_call_target="tpu_custom_call" | custom-call | flops 75497472 | bytes 3145728 | tf_op jit(solution)/shard_map/pallas_call | solution.py:40
  128.4 1.9 %collective-permute-start.3 = (f32[2,48,256]{2,1,0:T(8,128)S(1)}, f32[2,48,256]{2,1,0:T(8,128)S(1)}, u32[]{:S(2)}, u32[]{:S(2)}) collective-permute-start(f32[2,48,256]{2,1,0:T(8,128)S(1)} %get-tuple-element.44), channel_id=1, source_target_pairs={{0,12},{12,0},{1,13},{13,1},{2,14},{14,2},{3,15},{15,3},{4,16},{16... | collective-permute-start | bytes 294920 | tf_op jit(solution)/shard_map/ppermute | solution.py:319
  130.3 1.3 collective-permute-done.3.got_ref
  132.2 2.0 %collective-permute-start.4 = (f32[48,256]{1,0:T(8,128)S(1)}, f32[48,256]{1,0:T(8,128)S(1)}, u32[]{:S(2)}, u32[]{:S(2)}) collective-permute-start(f32[48,256]{1,0:T(8,128)S(1)} %get-tuple-element.46), channel_id=1, source_target_pairs={{0,96},{96,0},{1,97},{97,1},{2,98},{98,2},{3,99},{99,3},{4,100},{1... | collective-permute-start | bytes 147464 | tf_op jit(solution)/shard_map/ppermute | solution.py:319
  134.7 4.0 %collective-permute-done.4.other_ref = f32[48,256]{1,0:T(8,128)S(1)} collective-permute-done((f32[48,256]{1,0:T(8,128)S(1)}, f32[48,256]{1,0:T(8,128)S(1)}, u32[]{:S(2)}, u32[]{:S(2)}) %collective-permute-start.4) | collective-permute-done | bytes 49184 | tf_op jit(solution)/shard_map/ppermute | solution.py:319
  138.7 3.5 %all-to-all-done.5.parts_ref = bf16[16,48,256]{2,1,0:T(8,128)(2,1)S(1)} async-done(((bf16[16,48,256]{2,1,0:T(8,128)(2,1)}), bf16[16,48,256]{2,1,0:T(8,128)(2,1)S(1)}, u32[]{:S(2)}, u32[]{:S(2)}) %all-to-all-start.5) | async-done | bytes 393248 | tf_op jit(solution)/shard_map/all_to_all | solution.py:323
  (26 shorter events, 9.5 us)
Async XLA Ops:
  0.6 18.3 %copy-start.6 = (s32[48]{0:T(128)S(1)}, s32[48]{0:T(128)}, u32[]{:S(2)}) copy-start(s32[48]{0:T(128)} %param.10) | copy-start | bytes 580
  0.7 0.7 copy-start.5
  2.7 6.6 %collective-permute-start.1 = (bf16[32,128]{1,0:T(8,128)(2,1)S(1)}, bf16[32,128]{1,0:T(8,128)(2,1)S(1)}, u32[]{:S(2)}, u32[]{:S(2)}) collective-permute-start(bf16[32,128]{1,0:T(8,128)(2,1)S(1)} %get-tuple-element.28), channel_id=1, source_target_pairs={{0,96},{96,0},{1,97},{97,1},{2,98},{98,2},{3,99},{99,3},{4,100},{1... | collective-permute-start | bytes 24584 | tf_op jit(solution)/shard_map/ppermute | solution.py:319
  6.2 1.6 %copy-start = (bf16[4096,256]{1,0:T(8,128)(2,1)S(1)}, bf16[4096,256]{1,0:T(8,128)(2,1)}, u32[]{:S(2)}) copy-start(bf16[4096,256]{1,0:T(8,128)(2,1)} %w_ref.3) | copy-start | bytes 6291460
  7.8 1.0 copy-start.3
  8.8 10.2 %copy-start.1 = (bf16[4096,256]{1,0:T(8,128)(2,1)S(1)}, bf16[4096,256]{1,0:T(8,128)(2,1)}, u32[]{:S(2)}) copy-start(bf16[4096,256]{1,0:T(8,128)(2,1)} %w_ref.3) | copy-start | bytes 6291460
  8.8 10.2 %copy-start.4 = (bf16[48,4096]{1,0:T(8,128)(2,1)S(1)}, bf16[48,4096]{1,0:T(8,128)(2,1)}, u32[]{:S(2)}) copy-start(bf16[48,4096]{1,0:T(8,128)(2,1)} %qh_ref.1) | copy-start | bytes 1179652
  10.2 24.2 %all-to-all-start = ((bf16[16,64,256]{2,1,0:T(8,128)(2,1)}), bf16[16,64,256]{2,1,0:T(8,128)(2,1)S(1)}, u32[]{:S(2)}, u32[]{:S(2)}) async-start(bf16[16,64,256]{2,1,0:T(8,128)(2,1)} %shard_map.97), calls=%async_computation | async-start | bytes 1048576 | tf_op jit(solution)/shard_map/all_to_all | solution.py:323
  19.0 1.8 %copy-start.2 = (bf16[336,4096]{1,0:T(8,128)(2,1)S(1)}, bf16[336,4096]{1,0:T(8,128)(2,1)}, u32[]{:S(2)}) copy-start(bf16[336,4096]{1,0:T(8,128)(2,1)} %nh_ref.1) | copy-start | bytes 8257540
  22.7 3.3 %collective-permute-start = (bf16[400,256]{1,0:T(8,128)(2,1)S(1)}, bf16[400,256]{1,0:T(8,128)(2,1)S(1)}, u32[]{:S(2)}, u32[]{:S(2)}) collective-permute-start(bf16[400,256]{1,0:T(8,128)(2,1)S(1)} %shard_map.93.emb_ref), channel_id=1, source_target_pairs={{0,12},{12,0},{1,13},{13,1},{2,14},{14,2},{3,15},{15,3},{4,16},{16... | collective-permute-start | bytes 614408 | tf_op jit(solution)/shard_map/ppermute | solution.py:319
  26.7 7.2 %collective-permute-start.2 = (bf16[128,256]{1,0:T(8,128)(2,1)S(1)}, bf16[128,256]{1,0:T(8,128)(2,1)S(1)}, u32[]{:S(2)}, u32[]{:S(2)}) collective-permute-start(bf16[128,256]{1,0:T(8,128)(2,1)S(1)} %shard_map.94.chip_ref), channel_id=1, source_target_pairs={{0,96},{96,0},{1,97},{97,1},{2,98},{98,2},{3,99},{99,3},{4,100},{1... | collective-permute-start | bytes 196616 | tf_op jit(solution)/shard_map/ppermute | solution.py:319
  36.3 23.1 %all-to-all-start.1 = ((bf16[32,48,128]{2,1,0:T(8,128)(2,1)}), bf16[32,48,128]{2,1,0:T(8,128)(2,1)S(1)}, u32[]{:S(2)}, u32[]{:S(2)}) async-start(bf16[32,48,128]{2,1,0:T(8,128)(2,1)} %get-tuple-element.35), calls=%async_computation.1 | async-start | bytes 786432 | tf_op jit(solution)/shard_map/all_to_all | solution.py:323
  122.5 19.8 %all-to-all-start.5 = ((bf16[16,48,256]{2,1,0:T(8,128)(2,1)}), bf16[16,48,256]{2,1,0:T(8,128)(2,1)S(1)}, u32[]{:S(2)}, u32[]{:S(2)}) async-start(bf16[16,48,256]{2,1,0:T(8,128)(2,1)} %shard_map.104), calls=%async_computation.5 | async-start | bytes 786432 | tf_op jit(solution)/shard_map/all_to_all | solution.py:323
  128.4 3.2 %collective-permute-start.3 = (f32[2,48,256]{2,1,0:T(8,128)S(1)}, f32[2,48,256]{2,1,0:T(8,128)S(1)}, u32[]{:S(2)}, u32[]{:S(2)}) collective-permute-start(f32[2,48,256]{2,1,0:T(8,128)S(1)} %get-tuple-element.44), channel_id=1, source_target_pairs={{0,12},{12,0},{1,13},{13,1},{2,14},{14,2},{3,15},{15,3},{4,16},{16... | collective-permute-start | bytes 294920 | tf_op jit(solution)/shard_map/ppermute | solution.py:319
  132.2 6.5 %collective-permute-start.4 = (f32[48,256]{1,0:T(8,128)S(1)}, f32[48,256]{1,0:T(8,128)S(1)}, u32[]{:S(2)}, u32[]{:S(2)}) collective-permute-start(f32[48,256]{1,0:T(8,128)S(1)} %get-tuple-element.46), channel_id=1, source_target_pairs={{0,96},{96,0},{1,97},{97,1},{2,98},{98,2},{3,99},{99,3},{4,100},{1... | collective-permute-start | bytes 147464 | tf_op jit(solution)/shard_map/ppermute | solution.py:319

commit v4 on v3

--- a/solution.py
+++ b/solution.py
@@ -91,7 +91,6 @@
     passages = pass_ref[...]
     mine, other = mine_ref[...].astype(F32), other_ref[...].astype(F32)
     line = iota((16, 128), 0)
-    blank = jnp.zeros((16, 128), F32)
     for j in range(PEERS):
         part = jnp.where(
             line == 0,
@@ -102,8 +101,9 @@
                 jnp.where(line == 2, other[j : j + 1], jnp.where(line == 3, other[PEERS + j : PEERS + j + 1], 0.0)),
             ),
         )
-        send_ref[j, 0:Q] = passages
-        send_ref[j, Q:] = jnp.concatenate([part, blank], axis=1).astype(BF16)
+        send_ref[j, 0:Q] = passages[:, 0:128]
+        send_ref[j, Q : 2 * Q] = passages[:, 128:]
+        send_ref[j, 2 * Q :] = part.astype(BF16)
 
 
 def project_kernel(qh_ref, nh_ref, w_ref, pos_ref, emb_ref, acc):
@@ -144,17 +144,16 @@
         put(1, emb_ref)
 
 
-def answer_kernel(place_ref, recv_ref, emb_ref, other_ref, send_ref, pass_ref, pool):
+def answer_kernel(place_ref, recv_ref, emb_ref, other_ref, send_ref, pool):
     core = place_ref[0]
     pool[0:POOL] = emb_ref[Q : Q + POOL]
     pool[POOL : 2 * POOL] = other_ref[Q : Q + POOL]
     pool[2 * POOL :] = jnp.zeros((768 - 2 * POOL, 256), BF16)
-    pass_ref[...] = recv_ref[:, 0:Q].reshape(W, 256)
-    tail = recv_ref[:, Q:].astype(F32)
+    tail = recv_ref[:, 2 * Q :].astype(F32)
     lanes = iota((SLOT, 768), 1).astype(F32)
     rows = pool[...]
     for part in range(2):
-        asked = tail[:, 2 * part, 0:128] * 16.0 + tail[:, 2 * part + 1, 0:128]
+        asked = tail[:, 2 * part] * 16.0 + tail[:, 2 * part + 1]
         flipped = jnp.where(asked >= POOL, asked - POOL, asked + POOL)
         wanted = jnp.where(core == 1, flipped, asked).T
         base = ((place_ref[2] + part) & 1) * PEERS
@@ -168,8 +167,16 @@
             send_ref[pl.ds(base + 8 * g, 8)] = jnp.concatenate([left, right], axis=1).astype(BF16)
 
 
-def score_kernel(place_ref, chip_ref, next_ref, pass_ref, part_ref, group_ref):
+def quantize(values):
+    most = jnp.maximum(jnp.max(jnp.abs(values), axis=1, keepdims=True), 1e-30)
+    power = jnp.ceil(jnp.log2(most) * STEP + 0.02)
+    return jnp.floor(values * (TOP * jnp.exp2(power * (-1.0 / STEP))) + 0.5), power
+
+
+def score_kernel(place_ref, chip_ref, next_ref, recv_ref, score_ref, extra_ref, group_ref, pass_ref):
     even = place_ref[2] == 0
+    pass_ref[:, 0:128] = recv_ref[:, 0:Q].reshape(W, 128)
+    pass_ref[:, 128:] = recv_ref[:, Q : 2 * Q].reshape(W, 128)
 
     @pl.when(even)
     def _():
@@ -181,17 +188,28 @@
         group_ref[0 : 2 * Q] = next_ref[0 : 2 * Q]
         group_ref[2 * Q :] = chip_ref[0 : 2 * Q]
 
-    part_ref[...] = dot(group_ref[...], pass_ref[...], (((1,), (1,)), ((), ())))
-
-
-def quantize(values):
-    most = jnp.maximum(jnp.max(jnp.abs(values), axis=1, keepdims=True), 1e-30)
-    power = jnp.ceil(jnp.log2(most) * STEP + 0.02)
-    return jnp.floor(values * (TOP * jnp.exp2(power * (-1.0 / STEP))) + 0.5), power
-
-
-def hard_kernel(place_ref, part_ref, rows_ref, emb_ref, chip_ref, next_ref, slot_ref, send_ref, fetched_ref):
-    parity = place_ref[2]
+    scores, power = quantize(dot(group_ref[...], pass_ref[...], (((1,), (1,)), ((), ()))))
+    score_ref[...] = scores.reshape(Z, 16, W).astype(I32).astype(jnp.int16)
+    lane = iota((Q, 128), 1)
+
+    def target(ref, core):
+        pos = ref[2 * Q + 16 * core : 2 * Q + 16 * (core + 1)].astype(F32).T
+        pos = (pos[0:Q, 0:1] * 64.0 + pos[0:Q, 1:2]).astype(I32)
+        index = pos.astype(F32) + 0.5
+        chip = (index * (1.0 / 96.0)).astype(I32)
+        dp = (index * (1.0 / 48.0)).astype(I32)
+        peer = lax.shift_right_arithmetic(chip, 3) * X + (chip & 3)
+        column = (peer * Q + pos - dp * Q).astype(F32)
+        block = (dp - 2 * chip + 2 * (lax.shift_right_arithmetic(chip, 2) & 1)).astype(F32)
+        return jnp.where(lane == TCOL, column, jnp.where(lane == TCORE, block, 0.0))
+
+    for block in range(4):
+        core = block % 2
+        aim = jnp.where(place_ref[2] == block // 2, target(chip_ref, core), target(next_ref, core))
+        extra_ref[Q * block : Q * (block + 1)] = jnp.where(lane == ESCORE, power[Q * block : Q * (block + 1)], aim)
+
+
+def hard_kernel(place_ref, score_ref, extra_ref, rows_ref, emb_ref, slot_ref, send_ref, fetched_ref):
     got = rows_ref[...].astype(F32)
     left = got[:, 0:SLOT].reshape(CHIPS * SLOT, 128)
     right = got[:, SLOT:].reshape(CHIPS * SLOT, 128)
@@ -209,27 +227,11 @@
         hard = jnp.where(lane == k, jnp.sum(mine * row, axis=1, keepdims=True), hard)
     hard, power = quantize(hard)
     hard = jnp.where(lane == EHARD, power, hard)
-
-    def target(ref, core):
-        pos = ref[2 * Q + 16 * core : 2 * Q + 16 * (core + 1)].astype(F32).T
-        pos = (pos[0:Q, 0:1] * 64.0 + pos[0:Q, 1:2]).astype(I32)
-        index = pos.astype(F32) + 0.5
-        chip = (index * (1.0 / 96.0)).astype(I32)
-        dp = (index * (1.0 / 48.0)).astype(I32)
-        peer = lax.shift_right_arithmetic(chip, 3) * X + (chip & 3)
-        column = (peer * Q + pos - dp * Q).astype(F32)
-        block = (dp - 2 * chip + 2 * (lax.shift_right_arithmetic(chip, 2) & 1)).astype(F32)
-        return jnp.where(lane == TCOL, column, jnp.where(lane == TCORE, block, 0.0))
-
-    own = 2 * parity + place_ref[0]
-    scores, power = quantize(part_ref[...])
+    own = 2 * place_ref[2] + place_ref[0]
+    send_ref[:, :, 0:W] = score_ref[...]
     for block in range(4):
-        core = block % 2
-        aim = jnp.where(parity == block // 2, target(chip_ref, core), target(next_ref, core))
-        extra = aim + jnp.where(own == block, hard, 0.0)
-        extra = jnp.where(lane == ESCORE, power[Q * block : Q * (block + 1)], extra)
-        whole = jnp.concatenate([scores[Q * block : Q * (block + 1)], extra], axis=1)
-        send_ref[3 * block : 3 * (block + 1)] = whole.reshape(3, 16, WP).astype(I32).astype(jnp.int16)
+        extra = extra_ref[Q * block : Q * (block + 1)] + jnp.where(own == block, hard, 0.0)
+        send_ref[3 * block : 3 * (block + 1), :, W:] = extra.reshape(3, 16, 128).astype(I32).astype(jnp.int16)
 
 
 def stats_kernel(place_ref, part_ref, logit_ref, stat_ref):
@@ -349,7 +351,7 @@
         flops=2 * 48 * 4096 * 256,
         nbytes=3 * 2**20,
     )
-    send = call(message_kernel, shape((PEERS, Q + 16, 256), BF16), passages, wanted, handed, nbytes=2**19)
+    send = call(message_kernel, shape((PEERS, 2 * Q + 16, 128), BF16), passages, wanted, handed, nbytes=2**19)
     recv = exchange(send, ("yh", "x"))
 
     pos = jnp.pad(positive[None, :], ((0, 0), (0, 256 - Q)))
@@ -384,9 +386,9 @@
     )
     beside = swap(chip, "yl")
     recv, emb, other, beside = lax.optimization_barrier((recv, emb, other, beside))
-    answers, passages = call(
+    answers = call(
         answer_kernel,
-        (shape((CHIPS, 2 * SLOT, 128), BF16), shape((W, 256), BF16)),
+        shape((CHIPS, 2 * SLOT, 128), BF16),
         place,
         recv,
         emb,
@@ -397,13 +399,18 @@
         nbytes=2 * 2**20,
     )
     rows = exchange(answers, ("yl", "yh", "x"))
-    part, group = call(
+    scores, extra, group, passages = call(
         score_kernel,
-        (shape((GROUP, W), F32), shape((GROUP, 256), BF16)),
+        (
+            shape((Z, 16, W), jnp.int16),
+            shape((GROUP, 128), F32),
+            shape((GROUP, 256), BF16),
+            shape((W, 256), BF16),
+        ),
         place,
         chip,
         beside,
-        passages,
+        recv,
         in_specs=[SMEM] + [VMEM] * 3,
         flops=2 * 192 * 768 * 256,
         nbytes=2 * 2**20,
@@ -412,15 +419,14 @@
         hard_kernel,
         (shape((Z, 16, WP), jnp.int16), shape((K, Q, 256), BF16)),
         place,
-        part,
+        scores,
+        extra,
         rows,
         emb,
-        chip,
-        beside,
         slots,
-        in_specs=[SMEM] + [VMEM] * 6,
+        in_specs=[SMEM] + [VMEM] * 5,
         flops=2 * 336 * 768 * 256,
-        nbytes=3 * 2**20,
+        nbytes=2 * 2**20,
     )
     parts = exchange(send, "z")
     logits, stat = call(

time: 144 us -> 143 us (level)
  waiting for transfers between devices: 28.5 us -> 27 us
  transfers between devices with their start and end apart: 8 -> 8, of which waited for: 7 -> 7; matrix products, arithmetic and copies ran while one was open for 0% -> 0% of each run, Pallas kernels for 4% -> 5%
where the time goes in v4:
time: 143 us; the launch traced here: 142 us
  blocking collectives  58.6 us (41%)
  starting transfers between devices  35.1 us (25%)
  waiting for transfers between devices  27 us (19%)
  Pallas kernels  15 us (10%)
  local copies, waits for them, and re-layouts  5.57 us (4%)
    all_to_all x3, blocking collectives, exchange(): return lax.all_to_all(x, axes, split_axis=0, concat_axis=0, tiled=True)  58.6 us
    all_to_all x3, starting transfers between devices, exchange(): return lax.all_to_all(x, axes, split_axis=0, concat_axis=0, tiled=True)  22.5 us
    all_to_all x3, waiting for transfers between devices, exchange(): return lax.all_to_all(x, axes, split_axis=0, concat_axis=0, tiled=True)  17.5 us
    pallas_call x14, Pallas kernels, call(): pl.pallas_call(kernel, out_shape=out, compiler_params=pltpu.CompilerParam...  15 us
    ppermute x5, starting transfers between devices, swap(): return lax.ppermute(x, axis, [(0, 1), (1, 0)])  12.6 us
    ppermute x5, waiting for transfers between devices, swap(): return lax.ppermute(x, axis, [(0, 1), (1, 0)])  9.53 us
    unnamed x14, local copies, waits for them, and re-layouts  5.05 us
  transfers between devices with their start and end apart: 8, of which 7 were waited for; matrix products, arithmetic and copies ran while one was open for 0% of the time, Pallas kernels for 5%

profile of v4, /device:TPU:64, one launch (start us, length us, event | category | flops | bytes accessed | tf_op | source)
XLA Modules:
  0.0 142.1 jit_solution(17815562340168090827)
XLA Ops:
  1.4 1.3 shard_map.96
  2.7 3.5 %collective-permute-start.1 = (bf16[32,128]{1,0:T(8,128)(2,1)S(1)}, bf16[32,128]{1,0:T(8,128)(2,1)S(1)}, u32[]{:S(2)}, u32[]{:S(2)}) collective-permute-start(bf16[32,128]{1,0:T(8,128)(2,1)S(1)} %get-tuple-element.28), channel_id=1, source_target_pairs={{0,96},{96,0},{1,97},{97,1},{2,98},{98,2},{3,99},{99,3},{4,100},{1... | collective-permute-start | bytes 24584 | tf_op jit(solution)/shard_map/ppermute | solution.py:321
  6.2 1.6 %copy-done = bf16[4096,256]{1,0:T(8,128)(2,1)S(1)} copy-done((bf16[4096,256]{1,0:T(8,128)(2,1)S(1)}, bf16[4096,256]{1,0:T(8,128)(2,1)}, u32[]{:S(2)}) %copy-start) | copy-done | bytes 2097176
  10.1 8.8 %all-to-all-start = ((bf16[16,112,128]{2,1,0:T(8,128)(2,1)}), bf16[16,112,128]{2,1,0:T(8,128)(2,1)S(1)}, u32[]{:S(2)}, u32[]{:S(2)}) async-start(bf16[16,112,128]{2,1,0:T(8,128)(2,1)} %shard_map.97), calls=%async_computation | async-start | bytes 917504 | tf_op jit(solution)/shard_map/all_to_all | solution.py:325
  19.0 1.8 %copy-done.2 = bf16[336,4096]{1,0:T(8,128)(2,1)S(1)} copy-done((bf16[336,4096]{1,0:T(8,128)(2,1)S(1)}, bf16[336,4096]{1,0:T(8,128)(2,1)}, u32[]{:S(2)}) %copy-start.2) | copy-done | bytes 2752536
  20.7 2.0 %shard_map.93.emb_ref = bf16[400,256]{1,0:T(8,128)(2,1)S(1)} custom-call(bf16[48,4096]{1,0:T(8,128)(2,1)S(1)} %copy-done.4, bf16[336,4096]{1,0:T(8,128)(2,1)S(1)} %copy-done.2, bf16[4096,256]{1,0:T(8,128)(2,1)S(1)} %copy-done.1, s32[1,256]{1,0:T(1,128)S(1)} %pad.4.pos_ref), custom_call_target="tpu_custom_call" | custom-call | flops 805306368 | bytes 6291456 | tf_op jit(solution)/shard_map/pallas_call | solution.py:40
  22.7 1.9 %collective-permute-start = (bf16[400,256]{1,0:T(8,128)(2,1)S(1)}, bf16[400,256]{1,0:T(8,128)(2,1)S(1)}, u32[]{:S(2)}, u32[]{:S(2)}) collective-permute-start(bf16[400,256]{1,0:T(8,128)(2,1)S(1)} %shard_map.93.emb_ref), channel_id=1, source_target_pairs={{0,12},{12,0},{1,13},{13,1},{2,14},{14,2},{3,15},{15,3},{4,16},{16... | collective-permute-start | bytes 614408 | tf_op jit(solution)/shard_map/ppermute | solution.py:321
  24.6 1.4 collective-permute-done.other_ref
  26.6 3.3 %collective-permute-start.2 = (bf16[128,256]{1,0:T(8,128)(2,1)S(1)}, bf16[128,256]{1,0:T(8,128)(2,1)S(1)}, u32[]{:S(2)}, u32[]{:S(2)}) collective-permute-start(bf16[128,256]{1,0:T(8,128)(2,1)S(1)} %shard_map.94.chip_ref), channel_id=1, source_target_pairs={{0,96},{96,0},{1,97},{97,1},{2,98},{98,2},{3,99},{99,3},{4,100},{1... | collective-permute-start | bytes 196616 | tf_op jit(solution)/shard_map/ppermute | solution.py:321
  29.9 2.9 %collective-permute-done.2.next_ref = bf16[128,256]{1,0:T(8,128)(2,1)S(1)} collective-permute-done((bf16[128,256]{1,0:T(8,128)(2,1)S(1)}, bf16[128,256]{1,0:T(8,128)(2,1)S(1)}, u32[]{:S(2)}, u32[]{:S(2)}) %collective-permute-start.2) | collective-permute-done | bytes 65568 | tf_op jit(solution)/shard_map/ppermute | solution.py:321
  33.5 1.9 %shard_map.99 = bf16[32,48,128]{2,1,0:T(8,128)(2,1)} custom-call(s32[3]{0:T(128)S(1)} %pad_add_fusion.place_ref, bf16[16,112,128]{2,1,0:T(8,128)(2,1)S(1)} %all-to-all-done.recv_ref, bf16[400,256]{1,0:T(8,128)(2,1)S(1)} %shard_map.93.emb_ref, bf16[400,256]{1,0:T(8,128)(2,1)S(1)} %collective-permute-done.other_ref), custom_call_target="tpu_custom_call" | custom-call | flops 301989888 | bytes 2097152 | tf_op jit(solution)/shard_map/pallas_call | solution.py:40
  35.4 9.2 %all-to-all-start.1 = ((bf16[32,48,128]{2,1,0:T(8,128)(2,1)}), bf16[32,48,128]{2,1,0:T(8,128)(2,1)S(1)}, u32[]{:S(2)}, u32[]{:S(2)}) async-start(bf16[32,48,128]{2,1,0:T(8,128)(2,1)} %shard_map.99), calls=%async_computation.1 | async-start | bytes 786432 | tf_op jit(solution)/shard_map/all_to_all | solution.py:325
  44.6 1.4 %shard_map.98 = (s16[12,16,768]{2,1,0:T(8,128)(2,1)S(1)}, f32[192,128]{1,0:T(8,128)S(1)}, bf16[192,256]{1,0:T(8,128)(2,1)S(1)}, bf16[768,256]{1,0:T(8,128)(2,1)S(1)}) custom-call(s32[3]{0:T(128)S(1)} %pad_add_fusion.place_ref, bf16[128,256]{1,0:T(8,128)(2,1)S(1)} %shard_map.94.chip_ref, bf16[128,256]{1,0:T(8,128)(2,1)S(1)} %collective-permute-done.2.next_ref, ...), custom_call_target="tpu_custom_call" | custom-call | flops 75497472 | bytes 2097152 | tf_op jit(solution)/shard_map/pallas_call | solution.py:40
  46.1 13.2 %all-to-all-done.1.rows_ref = bf16[32,48,128]{2,1,0:T(8,128)(2,1)S(1)} async-done(((bf16[32,48,128]{2,1,0:T(8,128)(2,1)}), bf16[32,48,128]{2,1,0:T(8,128)(2,1)S(1)}, u32[]{:S(2)}, u32[]{:S(2)}) %all-to-all-start.1) | async-done | bytes 393248 | tf_op jit(solution)/shard_map/all_to_all | solution.py:325
  60.4 29.4 %all_to_all.30.part_ref = s16[12,16,896]{2,1,0:T(8,128)(2,1)S(1)} all-to-all(s16[12,16,896]{2,1,0:T(8,128)(2,1)S(1)} %get-tuple-element.36), channel_id=1, replica_groups=mesh['yh'=4,'yl'=2,'x'=4,'c'=2,'z'=12] {'z'}, dimensions={0} | all-to-all | bytes 688128 | tf_op jit(solution)/shard_map/all_to_all | solution.py:325
  90.7 7.6 %all_to_all.31.stat_ref = f32[4,16,128]{2,1,0:T(8,128)S(1)} all-to-all(f32[4,16,128]{2,1,0:T(8,128)S(1)} %get-tuple-element.38), channel_id=1, replica_groups=mesh['yh'=4,'yl'=2,'x'=4,'c'=2,'z'=12] {'yl','c'}, dimensions={0} | all-to-all | bytes 65536 | tf_op jit(solution)/shard_map/all_to_all | solution.py:325
  99.1 21.6 %all_to_all.32 = bf16[12,16,896]{2,1,0:T(8,128)(2,1)S(1)} all-to-all(bf16[12,16,896]{2,1,0:T(8,128)(2,1)S(1)} %shard_map.102), channel_id=1, replica_groups=mesh['yh'=4,'yl'=2,'x'=4,'c'=2,'z'=12] {'z'}, dimensions={0} | all-to-all | bytes 688128 | tf_op jit(solution)/shard_map/all_to_all | solution.py:325
  121.7 4.5 %all-to-all-start.5 = ((bf16[16,48,256]{2,1,0:T(8,128)(2,1)}), bf16[16,48,256]{2,1,0:T(8,128)(2,1)S(1)}, u32[]{:S(2)}, u32[]{:S(2)}) async-start(bf16[16,48,256]{2,1,0:T(8,128)(2,1)} %shard_map.104), calls=%async_computation.5 | async-start | bytes 786432 | tf_op jit(solution)/shard_map/all_to_all | solution.py:325
  126.2 1.5 %shard_map.103 = (f32[2,48,256]{2,1,0:T(8,128)S(1)}, f32[2,48,256]{2,1,0:T(8,128)S(1)}, f32[7,48,256]{2,1,0:T(8,128)}, f32[8,48]{1,0:T(8,128)S(1)}) custom-call(s32[3]{0:T(128)S(1)} %pad_add_fusion.place_ref, bf16[192,896]{1,0:T(8,128)(2,1)S(1)} %bitcast.10, bf16[768,256]{1,0:T(8,128)(2,1)S(1)} %get-tuple-element.39.pass_ref, ...), custom_call_target="tpu_custom_call" | custom-call | flops 75497472 | bytes 3145728 | tf_op jit(solution)/shard_map/pallas_call | solution.py:40
  127.7 1.9 %collective-permute-start.3 = (f32[2,48,256]{2,1,0:T(8,128)S(1)}, f32[2,48,256]{2,1,0:T(8,128)S(1)}, u32[]{:S(2)}, u32[]{:S(2)}) collective-permute-start(f32[2,48,256]{2,1,0:T(8,128)S(1)} %get-tuple-element.44), channel_id=1, source_target_pairs={{0,12},{12,0},{1,13},{13,1},{2,14},{14,2},{3,15},{15,3},{4,16},{16... | collective-permute-start | bytes 294920 | tf_op jit(solution)/shard_map/ppermute | solution.py:321
  129.6 1.3 collective-permute-done.3.got_ref
  131.4 2.0 %collective-permute-start.4 = (f32[48,256]{1,0:T(8,128)S(1)}, f32[48,256]{1,0:T(8,128)S(1)}, u32[]{:S(2)}, u32[]{:S(2)}) collective-permute-start(f32[48,256]{1,0:T(8,128)S(1)} %get-tuple-element.46), channel_id=1, source_target_pairs={{0,96},{96,0},{1,97},{97,1},{2,98},{98,2},{3,99},{99,3},{4,100},{1... | collective-permute-start | bytes 147464 | tf_op jit(solution)/shard_map/ppermute | solution.py:321
  134.0 3.9 %collective-permute-done.4.other_ref = f32[48,256]{1,0:T(8,128)S(1)} collective-permute-done((f32[48,256]{1,0:T(8,128)S(1)}, f32[48,256]{1,0:T(8,128)S(1)}, u32[]{:S(2)}, u32[]{:S(2)}) %collective-permute-start.4) | collective-permute-done | bytes 49184 | tf_op jit(solution)/shard_map/ppermute | solution.py:321
  137.9 3.5 %all-to-all-done.5.parts_ref = bf16[16,48,256]{2,1,0:T(8,128)(2,1)S(1)} async-done(((bf16[16,48,256]{2,1,0:T(8,128)(2,1)}), bf16[16,48,256]{2,1,0:T(8,128)(2,1)S(1)}, u32[]{:S(2)}, u32[]{:S(2)}) %all-to-all-start.5) | async-done | bytes 393248 | tf_op jit(solution)/shard_map/all_to_all | solution.py:325
  (26 shorter events, 9.9 us)
Async XLA Ops:
  0.6 18.3 %copy-start.6 = (s32[48]{0:T(128)S(1)}, s32[48]{0:T(128)}, u32[]{:S(2)}) copy-start(s32[48]{0:T(128)} %param.10) | copy-start | bytes 580
  0.7 0.7 copy-start.5
  2.7 6.6 %collective-permute-start.1 = (bf16[32,128]{1,0:T(8,128)(2,1)S(1)}, bf16[32,128]{1,0:T(8,128)(2,1)S(1)}, u32[]{:S(2)}, u32[]{:S(2)}) collective-permute-start(bf16[32,128]{1,0:T(8,128)(2,1)S(1)} %get-tuple-element.28), channel_id=1, source_target_pairs={{0,96},{96,0},{1,97},{97,1},{2,98},{98,2},{3,99},{99,3},{4,100},{1... | collective-permute-start | bytes 24584 | tf_op jit(solution)/shard_map/ppermute | solution.py:321
  6.2 1.6 %copy-start = (bf16[4096,256]{1,0:T(8,128)(2,1)S(1)}, bf16[4096,256]{1,0:T(8,128)(2,1)}, u32[]{:S(2)}) copy-start(bf16[4096,256]{1,0:T(8,128)(2,1)} %w_ref.3) | copy-start | bytes 6291460
  7.8 1.0 copy-start.3
  8.8 10.1 %copy-start.1 = (bf16[4096,256]{1,0:T(8,128)(2,1)S(1)}, bf16[4096,256]{1,0:T(8,128)(2,1)}, u32[]{:S(2)}) copy-start(bf16[4096,256]{1,0:T(8,128)(2,1)} %w_ref.3) | copy-start | bytes 6291460
  8.8 10.1 %copy-start.4 = (bf16[48,4096]{1,0:T(8,128)(2,1)S(1)}, bf16[48,4096]{1,0:T(8,128)(2,1)}, u32[]{:S(2)}) copy-start(bf16[48,4096]{1,0:T(8,128)(2,1)} %qh_ref.1) | copy-start | bytes 1179652
  10.1 23.3 %all-to-all-start = ((bf16[16,112,128]{2,1,0:T(8,128)(2,1)}), bf16[16,112,128]{2,1,0:T(8,128)(2,1)S(1)}, u32[]{:S(2)}, u32[]{:S(2)}) async-start(bf16[16,112,128]{2,1,0:T(8,128)(2,1)} %shard_map.97), calls=%async_computation | async-start | bytes 917504 | tf_op jit(solution)/shard_map/all_to_all | solution.py:325
  18.9 1.8 %copy-start.2 = (bf16[336,4096]{1,0:T(8,128)(2,1)S(1)}, bf16[336,4096]{1,0:T(8,128)(2,1)}, u32[]{:S(2)}) copy-start(bf16[336,4096]{1,0:T(8,128)(2,1)} %nh_ref.1) | copy-start | bytes 8257540
  22.7 3.3 %collective-permute-start = (bf16[400,256]{1,0:T(8,128)(2,1)S(1)}, bf16[400,256]{1,0:T(8,128)(2,1)S(1)}, u32[]{:S(2)}, u32[]{:S(2)}) collective-permute-start(bf16[400,256]{1,0:T(8,128)(2,1)S(1)} %shard_map.93.emb_ref), channel_id=1, source_target_pairs={{0,12},{12,0},{1,13},{13,1},{2,14},{14,2},{3,15},{15,3},{4,16},{16... | collective-permute-start | bytes 614408 | tf_op jit(solution)/shard_map/ppermute | solution.py:321
  26.6 6.2 %collective-permute-start.2 = (bf16[128,256]{1,0:T(8,128)(2,1)S(1)}, bf16[128,256]{1,0:T(8,128)(2,1)S(1)}, u32[]{:S(2)}, u32[]{:S(2)}) collective-permute-start(bf16[128,256]{1,0:T(8,128)(2,1)S(1)} %shard_map.94.chip_ref), channel_id=1, source_target_pairs={{0,96},{96,0},{1,97},{97,1},{2,98},{98,2},{3,99},{99,3},{4,100},{1... | collective-permute-start | bytes 196616 | tf_op jit(solution)/shard_map/ppermute | solution.py:321
  35.4 23.9 %all-to-all-start.1 = ((bf16[32,48,128]{2,1,0:T(8,128)(2,1)}), bf16[32,48,128]{2,1,0:T(8,128)(2,1)S(1)}, u32[]{:S(2)}, u32[]{:S(2)}) async-start(bf16[32,48,128]{2,1,0:T(8,128)(2,1)} %shard_map.99), calls=%async_computation.1 | async-start | bytes 786432 | tf_op jit(solution)/shard_map/all_to_all | solution.py:325
  121.7 19.8 %all-to-all-start.5 = ((bf16[16,48,256]{2,1,0:T(8,128)(2,1)}), bf16[16,48,256]{2,1,0:T(8,128)(2,1)S(1)}, u32[]{:S(2)}, u32[]{:S(2)}) async-start(bf16[16,48,256]{2,1,0:T(8,128)(2,1)} %shard_map.104), calls=%async_computation.5 | async-start | bytes 786432 | tf_op jit(solution)/shard_map/all_to_all | solution.py:325
  127.7 3.2 %collective-permute-start.3 = (f32[2,48,256]{2,1,0:T(8,128)S(1)}, f32[2,48,256]{2,1,0:T(8,128)S(1)}, u32[]{:S(2)}, u32[]{:S(2)}) collective-permute-start(f32[2,48,256]{2,1,0:T(8,128)S(1)} %get-tuple-element.44), channel_id=1, source_target_pairs={{0,12},{12,0},{1,13},{13,1},{2,14},{14,2},{3,15},{15,3},{4,16},{16... | collective-permute-start | bytes 294920 | tf_op jit(solution)/shard_map/ppermute | solution.py:321
  131.4 6.5 %collective-permute-start.4 = (f32[48,256]{1,0:T(8,128)S(1)}, f32[48,256]{1,0:T(8,128)S(1)}, u32[]{:S(2)}, u32[]{:S(2)}) collective-permute-start(f32[48,256]{1,0:T(8,128)S(1)} %get-tuple-element.46), channel_id=1, source_target_pairs={{0,96},{96,0},{1,97},{97,1},{2,98},{98,2},{3,99},{99,3},{4,100},{1... | collective-permute-start | bytes 147464 | tf_op jit(solution)/shard_map/ppermute | solution.py:321

commit v5 on v4

--- a/solution.py
+++ b/solution.py
@@ -126,10 +126,12 @@
         emb_ref[Q + POOL :] = jnp.where(iota((16, 256), 0) == 0, high, low).astype(BF16)
 
 
-def chip_kernel(place_ref, emb_ref, other_ref, chip_ref):
+def chip_kernel(place_ref, emb_ref, other_ref, chip_ref, pool_ref):
     first = place_ref[0] == 0
+    pool_ref[2 * POOL :] = jnp.zeros((768 - 2 * POOL, 256), BF16)
 
     def put(core, ref):
+        pool_ref[POOL * core : POOL * (core + 1)] = ref[Q : Q + POOL]
         chip_ref[Q * core : Q * (core + 1)] = ref[0:Q]
         chip_ref[2 * Q + 16 * core : 2 * Q + 16 * (core + 1)] = ref[Q + POOL :]
 
@@ -144,18 +146,13 @@
         put(1, emb_ref)
 
 
-def answer_kernel(place_ref, recv_ref, emb_ref, other_ref, send_ref, pool):
-    core = place_ref[0]
-    pool[0:POOL] = emb_ref[Q : Q + POOL]
-    pool[POOL : 2 * POOL] = other_ref[Q : Q + POOL]
-    pool[2 * POOL :] = jnp.zeros((768 - 2 * POOL, 256), BF16)
+def answer_kernel(place_ref, recv_ref, pool_ref, send_ref):
     tail = recv_ref[:, 2 * Q :].astype(F32)
     lanes = iota((SLOT, 768), 1).astype(F32)
-    rows = pool[...]
+    rows = pool_ref[...]
     for part in range(2):
         asked = tail[:, 2 * part] * 16.0 + tail[:, 2 * part + 1]
-        flipped = jnp.where(asked >= POOL, asked - POOL, asked + POOL)
-        wanted = jnp.where(core == 1, flipped, asked).T
+        wanted = asked.T
         base = ((place_ref[2] + part) & 1) * PEERS
         for g in range(2):
             hot = jnp.concatenate(
@@ -173,7 +170,11 @@
     return jnp.floor(values * (TOP * jnp.exp2(power * (-1.0 / STEP))) + 0.5), power
 
 
-def score_kernel(place_ref, chip_ref, next_ref, recv_ref, score_ref, extra_ref, group_ref, pass_ref):
+def score_kernel(place_ref, chip_ref, next_ref, recv_ref, slot_ref, score_ref, extra_ref, group_ref, pass_ref, hot_ref):
+    places = iota((Q, CHIPS * SLOT), 1).astype(F32)
+    slots = slot_ref[...]
+    for k in range(K):
+        hot_ref[Q * k : Q * (k + 1)] = jnp.where(slots[0:Q, k : k + 1] == places, 1.0, 0.0).astype(BF16)
     even = place_ref[2] == 0
     pass_ref[:, 0:128] = recv_ref[:, 0:Q].reshape(W, 128)
     pass_ref[:, 128:] = recv_ref[:, Q : 2 * Q].reshape(W, 128)
@@ -209,15 +210,12 @@
         extra_ref[Q * block : Q * (block + 1)] = jnp.where(lane == ESCORE, power[Q * block : Q * (block + 1)], aim)
 
 
-def hard_kernel(place_ref, score_ref, extra_ref, rows_ref, emb_ref, slot_ref, send_ref, fetched_ref):
+def hard_kernel(place_ref, score_ref, extra_ref, rows_ref, emb_ref, hot_ref, send_ref, fetched_ref):
     got = rows_ref[...].astype(F32)
     left = got[:, 0:SLOT].reshape(CHIPS * SLOT, 128)
     right = got[:, SLOT:].reshape(CHIPS * SLOT, 128)
     rows = jnp.concatenate([left, right], axis=1).astype(BF16)
-    places = iota((Q, CHIPS * SLOT), 1).astype(F32)
-    slots = slot_ref[...]
-    hot = jnp.concatenate([jnp.where(slots[0:Q, k : k + 1] == places, 1.0, 0.0) for k in range(K)], axis=0)
-    found = dot(hot.astype(BF16), rows)
+    found = dot(hot_ref[...], rows)
     lane = iota((Q, 128), 1)
     mine = emb_ref[0:Q].astype(F32)
     hard = jnp.zeros((Q, 128), F32)
@@ -298,15 +296,15 @@
     total[pl.ds(own, Q)] = result
     for p in range(YL):
         keep_ref[p] = total[pl.ds(pl.multiple_of((2 * p + core) * Q, 16), Q)]
-        give_ref[p] = total[pl.ds(pl.multiple_of((2 * p + 1 - core) * Q, 16), Q)]
+        give_ref[p] = total[pl.ds(pl.multiple_of((2 * p + 1 - core) * Q, 16), Q)].astype(BF16)
     loss = mine[:, K : K + 1] + mine[:, K + 1 : K + 2] + mine[:, K + 2 : K + 3]
     loss_ref[...] = jnp.broadcast_to(loss, (Q, 128)).T[0:8]
 
 
 def pair_kernel(place_ref, keep_ref, got_ref, mine_ref, give_ref):
     parity = place_ref[2]
-    mine_ref[...] = keep_ref[parity] + got_ref[parity]
-    give_ref[...] = keep_ref[1 - parity] + got_ref[1 - parity]
+    mine_ref[...] = keep_ref[parity] + got_ref[parity].astype(F32)
+    give_ref[...] = (keep_ref[1 - parity] + got_ref[1 - parity].astype(F32)).astype(BF16)
 
 
 def passage_kernel(parts_ref, mine_ref, other_ref, out_ref, query_ref):
@@ -314,7 +312,7 @@
     for j in range(1, PEERS):
         total += parts_ref[j].astype(F32)
     out_ref[...] = total
-    query_ref[...] = mine_ref[...] + other_ref[...]
+    query_ref[...] = mine_ref[...] + other_ref[...].astype(F32)
 
 
 def swap(x, axis="c"):
@@ -375,9 +373,9 @@
         nbytes=6 * 2**20,
     )
     other = swap(emb)
-    chip = call(
+    chip, pool = call(
         chip_kernel,
-        shape((2 * Q + 32, 256), BF16),
+        (shape((2 * Q + 32, 256), BF16), shape((768, 256), BF16)),
         place,
         emb,
         other,
@@ -385,33 +383,33 @@
         nbytes=2**17,
     )
     beside = swap(chip, "yl")
-    recv, emb, other, beside = lax.optimization_barrier((recv, emb, other, beside))
+    recv, pool, beside = lax.optimization_barrier((recv, pool, beside))
     answers = call(
         answer_kernel,
         shape((CHIPS, 2 * SLOT, 128), BF16),
         place,
         recv,
-        emb,
-        other,
-        in_specs=[SMEM] + [VMEM] * 3,
-        scratch_shapes=[pltpu.VMEM((768, 256), BF16)],
+        pool,
+        in_specs=[SMEM] + [VMEM] * 2,
         flops=2 * 768 * 768 * 256,
         nbytes=2 * 2**20,
     )
     rows = exchange(answers, ("yl", "yh", "x"))
-    scores, extra, group, passages = call(
+    scores, extra, group, passages, hot = call(
         score_kernel,
         (
             shape((Z, 16, W), jnp.int16),
             shape((GROUP, 128), F32),
             shape((GROUP, 256), BF16),
             shape((W, 256), BF16),
+            shape((K * Q, CHIPS * SLOT), BF16),
         ),
         place,
         chip,
         beside,
         recv,
-        in_specs=[SMEM] + [VMEM] * 3,
+        slots,
+        in_specs=[SMEM] + [VMEM] * 4,
         flops=2 * 192 * 768 * 256,
         nbytes=2 * 2**20,
     )
@@ -423,7 +421,7 @@
         extra,
         rows,
         emb,
-        slots,
+        hot,
         in_specs=[SMEM] + [VMEM] * 5,
         flops=2 * 336 * 768 * 256,
         nbytes=2 * 2**20,
@@ -460,7 +458,7 @@
     sums = exchange(sums, ("yh", "x"))
     keep, give, hard_grad, loss = call(
         query_kernel,
-        (shape((YL, Q, 256), F32), shape((YL, Q, 256), F32), shape((K, Q, 256), F32), shape((8, Q), F32)),
+        (shape((YL, Q, 256), F32), shape((YL, Q, 256), BF16), shape((K, Q, 256), F32), shape((8, Q), F32)),
         place,
         grads,
         passages,
@@ -473,7 +471,7 @@
     )
     query_mine, query_give = call(
         pair_kernel,
-        (shape((Q, 256), F32), shape((Q, 256), F32)),
+        (shape((Q, 256), F32), shape((Q, 256), BF16)),
         place,
         keep,
         swap(give),

time: 143 us -> 143 us (level)
  no operation moved by 1% of the time
where the time goes in v5:
time: 143 us; the launch traced here: 142 us
  blocking collectives  58.6 us (41%)
  starting transfers between devices  35.1 us (25%)
  waiting for transfers between devices  26.9 us (19%)
  Pallas kernels  15.1 us (11%)
  local copies, waits for them, and re-layouts  5.57 us (4%)
    all_to_all x3, blocking collectives, exchange(): return lax.all_to_all(x, axes, split_axis=0, concat_axis=0, tiled=True)  58.6 us
    all_to_all x3, starting transfers between devices, exchange(): return lax.all_to_all(x, axes, split_axis=0, concat_axis=0, tiled=True)  22.5 us
    all_to_all x3, waiting for transfers between devices, exchange(): return lax.all_to_all(x, axes, split_axis=0, concat_axis=0, tiled=True)  17.9 us
    pallas_call x14, Pallas kernels, call(): pl.pallas_call(kernel, out_shape=out, compiler_params=pltpu.CompilerParam...  15.1 us
    ppermute x5, starting transfers between devices, swap(): return lax.ppermute(x, axis, [(0, 1), (1, 0)])  12.6 us
    ppermute x5, waiting for transfers between devices, swap(): return lax.ppermute(x, axis, [(0, 1), (1, 0)])  8.99 us
    unnamed x14, local copies, waits for them, and re-layouts  5.05 us
  transfers between devices with their start and end apart: 8, of which 7 were waited for; matrix products, arithmetic and copies ran while one was open for 0% of the time, Pallas kernels for 5%

profile of v5, /device:TPU:64, one launch (start us, length us, event | category | flops | bytes accessed | tf_op | source)
XLA Modules:
  0.0 142.1 jit_solution(4022065893193462829)
XLA Ops:
  1.4 1.3 shard_map.96
  2.7 3.5 %collective-permute-start.1 = (bf16[32,128]{1,0:T(8,128)(2,1)S(1)}, bf16[32,128]{1,0:T(8,128)(2,1)S(1)}, u32[]{:S(2)}, u32[]{:S(2)}) collective-permute-start(bf16[32,128]{1,0:T(8,128)(2,1)S(1)} %get-tuple-element.31), channel_id=1, source_target_pairs={{0,96},{96,0},{1,97},{97,1},{2,98},{98,2},{3,99},{99,3},{4,100},{1... | collective-permute-start | bytes 24584 | tf_op jit(solution)/shard_map/ppermute | solution.py:319
  6.2 1.6 %copy-done = bf16[4096,256]{1,0:T(8,128)(2,1)S(1)} copy-done((bf16[4096,256]{1,0:T(8,128)(2,1)S(1)}, bf16[4096,256]{1,0:T(8,128)(2,1)}, u32[]{:S(2)}) %copy-start) | copy-done | bytes 2097176
  10.1 8.8 %all-to-all-start = ((bf16[16,112,128]{2,1,0:T(8,128)(2,1)}), bf16[16,112,128]{2,1,0:T(8,128)(2,1)S(1)}, u32[]{:S(2)}, u32[]{:S(2)}) async-start(bf16[16,112,128]{2,1,0:T(8,128)(2,1)} %shard_map.97), calls=%async_computation | async-start | bytes 917504 | tf_op jit(solution)/shard_map/all_to_all | solution.py:323
  19.0 1.8 %copy-done.2 = bf16[336,4096]{1,0:T(8,128)(2,1)S(1)} copy-done((bf16[336,4096]{1,0:T(8,128)(2,1)S(1)}, bf16[336,4096]{1,0:T(8,128)(2,1)}, u32[]{:S(2)}) %copy-start.2) | copy-done | bytes 2752536
  20.7 2.0 %shard_map.93.emb_ref = bf16[400,256]{1,0:T(8,128)(2,1)S(1)} custom-call(bf16[48,4096]{1,0:T(8,128)(2,1)S(1)} %copy-done.4, bf16[336,4096]{1,0:T(8,128)(2,1)S(1)} %copy-done.2, bf16[4096,256]{1,0:T(8,128)(2,1)S(1)} %copy-done.1, s32[1,256]{1,0:T(1,128)S(1)} %pad.4.pos_ref), custom_call_target="tpu_custom_call" | custom-call | flops 805306368 | bytes 6291456 | tf_op jit(solution)/shard_map/pallas_call | solution.py:40
  22.7 1.9 %collective-permute-start = (bf16[400,256]{1,0:T(8,128)(2,1)S(1)}, bf16[400,256]{1,0:T(8,128)(2,1)S(1)}, u32[]{:S(2)}, u32[]{:S(2)}) collective-permute-start(bf16[400,256]{1,0:T(8,128)(2,1)S(1)} %shard_map.93.emb_ref), channel_id=1, source_target_pairs={{0,12},{12,0},{1,13},{13,1},{2,14},{14,2},{3,15},{15,3},{4,16},{16... | collective-permute-start | bytes 614408 | tf_op jit(solution)/shard_map/ppermute | solution.py:319
  24.7 1.4 collective-permute-done.other_ref
  26.7 3.3 %collective-permute-start.2 = (bf16[128,256]{1,0:T(8,128)(2,1)S(1)}, bf16[128,256]{1,0:T(8,128)(2,1)S(1)}, u32[]{:S(2)}, u32[]{:S(2)}) collective-permute-start(bf16[128,256]{1,0:T(8,128)(2,1)S(1)} %get-tuple-element.29.chip_ref), channel_id=1, source_target_pairs={{0,96},{96,0},{1,97},{97,1},{2,98},{98,2},{3,99},{99,3},{4,100},{1... | collective-permute-start | bytes 196616 | tf_op jit(solution)/shard_map/ppermute | solution.py:319
  29.9 2.9 %collective-permute-done.2.next_ref = bf16[128,256]{1,0:T(8,128)(2,1)S(1)} collective-permute-done((bf16[128,256]{1,0:T(8,128)(2,1)S(1)}, bf16[128,256]{1,0:T(8,128)(2,1)S(1)}, u32[]{:S(2)}, u32[]{:S(2)}) %collective-permute-start.2) | collective-permute-done | bytes 65568 | tf_op jit(solution)/shard_map/ppermute | solution.py:319
  33.5 1.9 %shard_map.99 = bf16[32,48,128]{2,1,0:T(8,128)(2,1)} custom-call(s32[3]{0:T(128)S(1)} %pad_add_fusion.place_ref, bf16[16,112,128]{2,1,0:T(8,128)(2,1)S(1)} %all-to-all-done.recv_ref, bf16[768,256]{1,0:T(8,128)(2,1)S(1)} %get-tuple-element.38.pool_ref), custom_call_target="tpu_custom_call" | custom-call | flops 301989888 | bytes 2097152 | tf_op jit(solution)/shard_map/pallas_call | solution.py:40
  35.4 9.2 %all-to-all-start.1 = ((bf16[32,48,128]{2,1,0:T(8,128)(2,1)}), bf16[32,48,128]{2,1,0:T(8,128)(2,1)S(1)}, u32[]{:S(2)}, u32[]{:S(2)}) async-start(bf16[32,48,128]{2,1,0:T(8,128)(2,1)} %shard_map.99), calls=%async_computation.1 | async-start | bytes 786432 | tf_op jit(solution)/shard_map/all_to_all | solution.py:323
  44.6 1.6 %shard_map.98 = (s16[12,16,768]{2,1,0:T(8,128)(2,1)S(1)}, f32[192,128]{1,0:T(8,128)S(1)}, bf16[192,256]{1,0:T(8,128)(2,1)S(1)}, bf16[768,256]{1,0:T(8,128)(2,1)S(1)}, bf16[336,768]{1,0:T(8,128)(2,1)S(1)}) custom-call(s32[3]{0:T(128)S(1)} %pad_add_fusion.place_ref, bf16[128,256]{1,0:T(8,128)(2,1)S(1)} %get-tuple-element.29.chip_ref, ...), custom_call_target="tpu_custom_call" | custom-call | flops 75497472 | bytes 2097152 | tf_op jit(solution)/shard_map/pallas_call | solution.py:40
  46.2 13.1 %all-to-all-done.1.rows_ref = bf16[32,48,128]{2,1,0:T(8,128)(2,1)S(1)} async-done(((bf16[32,48,128]{2,1,0:T(8,128)(2,1)}), bf16[32,48,128]{2,1,0:T(8,128)(2,1)S(1)}, u32[]{:S(2)}, u32[]{:S(2)}) %all-to-all-start.1) | async-done | bytes 393248 | tf_op jit(solution)/shard_map/all_to_all | solution.py:323
  60.3 29.4 %all_to_all.30.part_ref = s16[12,16,896]{2,1,0:T(8,128)(2,1)S(1)} all-to-all(s16[12,16,896]{2,1,0:T(8,128)(2,1)S(1)} %get-tuple-element.40), channel_id=1, replica_groups=mesh['yh'=4,'yl'=2,'x'=4,'c'=2,'z'=12] {'z'}, dimensions={0} | all-to-all | bytes 688128 | tf_op jit(solution)/shard_map/all_to_all | solution.py:323
  90.6 7.6 %all_to_all.31.stat_ref = f32[4,16,128]{2,1,0:T(8,128)S(1)} all-to-all(f32[4,16,128]{2,1,0:T(8,128)S(1)} %get-tuple-element.42), channel_id=1, replica_groups=mesh['yh'=4,'yl'=2,'x'=4,'c'=2,'z'=12] {'yl','c'}, dimensions={0} | all-to-all | bytes 65536 | tf_op jit(solution)/shard_map/all_to_all | solution.py:323
  99.0 21.6 %all_to_all.32 = bf16[12,16,896]{2,1,0:T(8,128)(2,1)S(1)} all-to-all(bf16[12,16,896]{2,1,0:T(8,128)(2,1)S(1)} %shard_map.102), channel_id=1, replica_groups=mesh['yh'=4,'yl'=2,'x'=4,'c'=2,'z'=12] {'z'}, dimensions={0} | all-to-all | bytes 688128 | tf_op jit(solution)/shard_map/all_to_all | solution.py:323
  121.6 4.5 %all-to-all-start.5 = ((bf16[16,48,256]{2,1,0:T(8,128)(2,1)}), bf16[16,48,256]{2,1,0:T(8,128)(2,1)S(1)}, u32[]{:S(2)}, u32[]{:S(2)}) async-start(bf16[16,48,256]{2,1,0:T(8,128)(2,1)} %shard_map.104), calls=%async_computation.5 | async-start | bytes 786432 | tf_op jit(solution)/shard_map/all_to_all | solution.py:323
  126.1 1.5 %shard_map.103 = (f32[2,48,256]{2,1,0:T(8,128)S(1)}, bf16[2,48,256]{2,1,0:T(8,128)(2,1)S(1)}, f32[7,48,256]{2,1,0:T(8,128)}, f32[8,48]{1,0:T(8,128)S(1)}) custom-call(s32[3]{0:T(128)S(1)} %pad_add_fusion.place_ref, bf16[192,896]{1,0:T(8,128)(2,1)S(1)} %bitcast.10, bf16[768,256]{1,0:T(8,128)(2,1)S(1)} %get-tuple-element.43.pass_ref, ...), custom_call_target="tpu_custom_call" | custom-call | flops 75497472 | bytes 3145728 | tf_op jit(solution)/shard_map/pallas_call | solution.py:40
  127.6 1.9 %collective-permute-start.3 = (bf16[2,48,256]{2,1,0:T(8,128)(2,1)S(1)}, bf16[2,48,256]{2,1,0:T(8,128)(2,1)S(1)}, u32[]{:S(2)}, u32[]{:S(2)}) collective-permute-start(bf16[2,48,256]{2,1,0:T(8,128)(2,1)S(1)} %get-tuple-element.48), channel_id=1, source_target_pairs={{0,12},{12,0},{1,13},{13,1},{2,14},{14,2},{3,15},{15,3},{4,16},{16... | collective-permute-start | bytes 147464 | tf_op jit(solution)/shard_map/ppermute | solution.py:319
  129.5 1.2 collective-permute-done.3.got_ref
  131.3 2.0 %collective-permute-start.4 = (bf16[48,256]{1,0:T(8,128)(2,1)S(1)}, bf16[48,256]{1,0:T(8,128)(2,1)S(1)}, u32[]{:S(2)}, u32[]{:S(2)}) collective-permute-start(bf16[48,256]{1,0:T(8,128)(2,1)S(1)} %get-tuple-element.50), channel_id=1, source_target_pairs={{0,96},{96,0},{1,97},{97,1},{2,98},{98,2},{3,99},{99,3},{4,100},{1... | collective-permute-start | bytes 73736 | tf_op jit(solution)/shard_map/ppermute | solution.py:319
  133.8 3.5 %collective-permute-done.4.other_ref = bf16[48,256]{1,0:T(8,128)(2,1)S(1)} collective-permute-done((bf16[48,256]{1,0:T(8,128)(2,1)S(1)}, bf16[48,256]{1,0:T(8,128)(2,1)S(1)}, u32[]{:S(2)}, u32[]{:S(2)}) %collective-permute-start.4) | collective-permute-done | bytes 24608 | tf_op jit(solution)/shard_map/ppermute | solution.py:319
  137.3 4.1 %all-to-all-done.5.parts_ref = bf16[16,48,256]{2,1,0:T(8,128)(2,1)S(1)} async-done(((bf16[16,48,256]{2,1,0:T(8,128)(2,1)}), bf16[16,48,256]{2,1,0:T(8,128)(2,1)S(1)}, u32[]{:S(2)}, u32[]{:S(2)}) %all-to-all-start.5) | async-done | bytes 393248 | tf_op jit(solution)/shard_map/all_to_all | solution.py:323
  (26 shorter events, 9.8 us)
Async XLA Ops:
  0.6 18.3 %copy-start.6 = (s32[48]{0:T(128)S(1)}, s32[48]{0:T(128)}, u32[]{:S(2)}) copy-start(s32[48]{0:T(128)} %param.10) | copy-start | bytes 580
  0.7 0.7 copy-start.5
  2.7 6.6 %collective-permute-start.1 = (bf16[32,128]{1,0:T(8,128)(2,1)S(1)}, bf16[32,128]{1,0:T(8,128)(2,1)S(1)}, u32[]{:S(2)}, u32[]{:S(2)}) collective-permute-start(bf16[32,128]{1,0:T(8,128)(2,1)S(1)} %get-tuple-element.31), channel_id=1, source_target_pairs={{0,96},{96,0},{1,97},{97,1},{2,98},{98,2},{3,99},{99,3},{4,100},{1... | collective-permute-start | bytes 24584 | tf_op jit(solution)/shard_map/ppermute | solution.py:319
  6.2 1.6 %copy-start = (bf16[4096,256]{1,0:T(8,128)(2,1)S(1)}, bf16[4096,256]{1,0:T(8,128)(2,1)}, u32[]{:S(2)}) copy-start(bf16[4096,256]{1,0:T(8,128)(2,1)} %w_ref.3) | copy-start | bytes 6291460
  7.8 1.0 copy-start.3
  8.8 10.1 %copy-start.1 = (bf16[4096,256]{1,0:T(8,128)(2,1)S(1)}, bf16[4096,256]{1,0:T(8,128)(2,1)}, u32[]{:S(2)}) copy-start(bf16[4096,256]{1,0:T(8,128)(2,1)} %w_ref.3) | copy-start | bytes 6291460
  8.8 10.1 %copy-start.4 = (bf16[48,4096]{1,0:T(8,128)(2,1)S(1)}, bf16[48,4096]{1,0:T(8,128)(2,1)}, u32[]{:S(2)}) copy-start(bf16[48,4096]{1,0:T(8,128)(2,1)} %qh_ref.1) | copy-start | bytes 1179652
  10.1 23.3 %all-to-all-start = ((bf16[16,112,128]{2,1,0:T(8,128)(2,1)}), bf16[16,112,128]{2,1,0:T(8,128)(2,1)S(1)}, u32[]{:S(2)}, u32[]{:S(2)}) async-start(bf16[16,112,128]{2,1,0:T(8,128)(2,1)} %shard_map.97), calls=%async_computation | async-start | bytes 917504 | tf_op jit(solution)/shard_map/all_to_all | solution.py:323
  19.0 1.8 %copy-start.2 = (bf16[336,4096]{1,0:T(8,128)(2,1)S(1)}, bf16[336,4096]{1,0:T(8,128)(2,1)}, u32[]{:S(2)}) copy-start(bf16[336,4096]{1,0:T(8,128)(2,1)} %nh_ref.1) | copy-start | bytes 8257540
  22.7 3.3 %collective-permute-start = (bf16[400,256]{1,0:T(8,128)(2,1)S(1)}, bf16[400,256]{1,0:T(8,128)(2,1)S(1)}, u32[]{:S(2)}, u32[]{:S(2)}) collective-permute-start(bf16[400,256]{1,0:T(8,128)(2,1)S(1)} %shard_map.93.emb_ref), channel_id=1, source_target_pairs={{0,12},{12,0},{1,13},{13,1},{2,14},{14,2},{3,15},{15,3},{4,16},{16... | collective-permute-start | bytes 614408 | tf_op jit(solution)/shard_map/ppermute | solution.py:319
  26.7 6.2 %collective-permute-start.2 = (bf16[128,256]{1,0:T(8,128)(2,1)S(1)}, bf16[128,256]{1,0:T(8,128)(2,1)S(1)}, u32[]{:S(2)}, u32[]{:S(2)}) collective-permute-start(bf16[128,256]{1,0:T(8,128)(2,1)S(1)} %get-tuple-element.29.chip_ref), channel_id=1, source_target_pairs={{0,96},{96,0},{1,97},{97,1},{2,98},{98,2},{3,99},{99,3},{4,100},{1... | collective-permute-start | bytes 196616 | tf_op jit(solution)/shard_map/ppermute | solution.py:319
  35.4 23.9 %all-to-all-start.1 = ((bf16[32,48,128]{2,1,0:T(8,128)(2,1)}), bf16[32,48,128]{2,1,0:T(8,128)(2,1)S(1)}, u32[]{:S(2)}, u32[]{:S(2)}) async-start(bf16[32,48,128]{2,1,0:T(8,128)(2,1)} %shard_map.99), calls=%async_computation.1 | async-start | bytes 786432 | tf_op jit(solution)/shard_map/all_to_all | solution.py:323
  121.6 19.8 %all-to-all-start.5 = ((bf16[16,48,256]{2,1,0:T(8,128)(2,1)}), bf16[16,48,256]{2,1,0:T(8,128)(2,1)S(1)}, u32[]{:S(2)}, u32[]{:S(2)}) async-start(bf16[16,48,256]{2,1,0:T(8,128)(2,1)} %shard_map.104), calls=%async_computation.5 | async-start | bytes 786432 | tf_op jit(solution)/shard_map/all_to_all | solution.py:323
  127.6 3.1 %collective-permute-start.3 = (bf16[2,48,256]{2,1,0:T(8,128)(2,1)S(1)}, bf16[2,48,256]{2,1,0:T(8,128)(2,1)S(1)}, u32[]{:S(2)}, u32[]{:S(2)}) collective-permute-start(bf16[2,48,256]{2,1,0:T(8,128)(2,1)S(1)} %get-tuple-element.48), channel_id=1, source_target_pairs={{0,12},{12,0},{1,13},{13,1},{2,14},{14,2},{3,15},{15,3},{4,16},{16... | collective-permute-start | bytes 147464 | tf_op jit(solution)/shard_map/ppermute | solution.py:319
  131.3 6.0 %collective-permute-start.4 = (bf16[48,256]{1,0:T(8,128)(2,1)S(1)}, bf16[48,256]{1,0:T(8,128)(2,1)S(1)}, u32[]{:S(2)}, u32[]{:S(2)}) collective-permute-start(bf16[48,256]{1,0:T(8,128)(2,1)S(1)} %get-tuple-element.50), channel_id=1, source_target_pairs={{0,96},{96,0},{1,97},{97,1},{2,98},{98,2},{3,99},{99,3},{4,100},{1... | collective-permute-start | bytes 73736 | tf_op jit(solution)/shard_map/ppermute | solution.py:319

commit v6 on v4

--- a/solution.py
+++ b/solution.py
@@ -384,8 +384,8 @@
         in_specs=[SMEM, VMEM, VMEM],
         nbytes=2**17,
     )
+    recv, emb, other, chip = lax.optimization_barrier((recv, emb, other, chip))
     beside = swap(chip, "yl")
-    recv, emb, other, beside = lax.optimization_barrier((recv, emb, other, beside))
     answers = call(
         answer_kernel,
         shape((CHIPS, 2 * SLOT, 128), BF16),

time: 143 us -> 143 us (level)
    ppermute x5, waiting for transfers between devices: 9.53 us -> 14.4 us  [swap(): return lax.ppermute(x, axis, [(0, 1), (1, 0)])]
    all_to_all x3, waiting for transfers between devices: 17.5 us -> 14 us  [exchange(): return lax.all_to_all(x, axes, split_axis=0, concat_axis=0, tiled=True)]
where the time goes in v6:
time: 143 us
  blocking collectives  57.5 us (40%)
  starting transfers between devices  35.3 us (25%)
  waiting for transfers between devices  28.4 us (20%)
  Pallas kernels  15 us (10%)
  local copies, waits for them, and re-layouts  5.57 us (4%)
    all_to_all x3, blocking collectives, exchange(): return lax.all_to_all(x, axes, split_axis=0, concat_axis=0, tiled=True)  57.5 us
    all_to_all x3, starting transfers between devices, exchange(): return lax.all_to_all(x, axes, split_axis=0, concat_axis=0, tiled=True)  22.3 us
    pallas_call x14, Pallas kernels, call(): pl.pallas_call(kernel, out_shape=out, compiler_params=pltpu.CompilerParam...  15 us
    ppermute x5, waiting for transfers between devices, swap(): return lax.ppermute(x, axis, [(0, 1), (1, 0)])  14.4 us
    all_to_all x3, waiting for transfers between devices, exchange(): return lax.all_to_all(x, axes, split_axis=0, concat_axis=0, tiled=True)  14 us
    ppermute x5, starting transfers between devices, swap(): return lax.ppermute(x, axis, [(0, 1), (1, 0)])  13.1 us
    unnamed x14, local copies, waits for them, and re-layouts  5.05 us
  transfers between devices with their start and end apart: 8, of which 7 were waited for; matrix products, arithmetic and copies ran while one was open for 0% of the time, Pallas kernels for 5%

profile of v6, /device:TPU:64, one launch (start us, length us, event | category | flops | bytes accessed | tf_op | source)
XLA Modules:
  0.0 142.7 jit_solution(14430687098877251600)
XLA Ops:
  1.4 1.3 shard_map.94
  2.7 3.5 %collective-permute-start = (bf16[32,128]{1,0:T(8,128)(2,1)S(1)}, bf16[32,128]{1,0:T(8,128)(2,1)S(1)}, u32[]{:S(2)}, u32[]{:S(2)}) collective-permute-start(bf16[32,128]{1,0:T(8,128)(2,1)S(1)} %get-tuple-element.28), channel_id=1, source_target_pairs={{0,96},{96,0},{1,97},{97,1},{2,98},{98,2},{3,99},{99,3},{4,100},{1... | collective-permute-start | bytes 24584 | tf_op jit(solution)/shard_map/ppermute | solution.py:321
  6.2 1.6 %copy-done = bf16[4096,256]{1,0:T(8,128)(2,1)S(1)} copy-done((bf16[4096,256]{1,0:T(8,128)(2,1)S(1)}, bf16[4096,256]{1,0:T(8,128)(2,1)}, u32[]{:S(2)}) %copy-start) | copy-done | bytes 2097176
  10.1 8.8 %all-to-all-start = ((bf16[16,112,128]{2,1,0:T(8,128)(2,1)}), bf16[16,112,128]{2,1,0:T(8,128)(2,1)S(1)}, u32[]{:S(2)}, u32[]{:S(2)}) async-start(bf16[16,112,128]{2,1,0:T(8,128)(2,1)} %shard_map.95), calls=%async_computation | async-start | bytes 917504 | tf_op jit(solution)/shard_map/all_to_all | solution.py:325
  19.0 1.8 %copy-done.2 = bf16[336,4096]{1,0:T(8,128)(2,1)S(1)} copy-done((bf16[336,4096]{1,0:T(8,128)(2,1)S(1)}, bf16[336,4096]{1,0:T(8,128)(2,1)}, u32[]{:S(2)}) %copy-start.2) | copy-done | bytes 2752536
  20.7 2.0 %shard_map.96.emb_ref = bf16[400,256]{1,0:T(8,128)(2,1)S(1)} custom-call(bf16[48,4096]{1,0:T(8,128)(2,1)S(1)} %copy-done.4, bf16[336,4096]{1,0:T(8,128)(2,1)S(1)} %copy-done.2, bf16[4096,256]{1,0:T(8,128)(2,1)S(1)} %copy-done.1, s32[1,256]{1,0:T(1,128)S(1)} %pad.4.pos_ref), custom_call_target="tpu_custom_call" | custom-call | flops 805306368 | bytes 6291456 | tf_op jit(solution)/shard_map/pallas_call | solution.py:40
  22.7 1.9 %collective-permute-start.1 = (bf16[400,256]{1,0:T(8,128)(2,1)S(1)}, bf16[400,256]{1,0:T(8,128)(2,1)S(1)}, u32[]{:S(2)}, u32[]{:S(2)}) collective-permute-start(bf16[400,256]{1,0:T(8,128)(2,1)S(1)} %shard_map.96.emb_ref), channel_id=1, source_target_pairs={{0,12},{12,0},{1,13},{13,1},{2,14},{14,2},{3,15},{15,3},{4,16},{16... | collective-permute-start | bytes 614408 | tf_op jit(solution)/shard_map/ppermute | solution.py:321
  24.6 1.4 collective-permute-done.1.other_ref
  26.6 6.8 %all-to-all-done.recv_ref = bf16[16,112,128]{2,1,0:T(8,128)(2,1)S(1)} async-done(((bf16[16,112,128]{2,1,0:T(8,128)(2,1)}), bf16[16,112,128]{2,1,0:T(8,128)(2,1)S(1)}, u32[]{:S(2)}, u32[]{:S(2)}) %all-to-all-start) | async-done | bytes 458784 | tf_op jit(solution)/shard_map/all_to_all | solution.py:325
  33.5 1.9 %shard_map.99 = bf16[32,48,128]{2,1,0:T(8,128)(2,1)} custom-call(s32[3]{0:T(128)S(1)} %pad_add_fusion.place_ref, bf16[16,112,128]{2,1,0:T(8,128)(2,1)S(1)} %all-to-all-done.recv_ref, bf16[400,256]{1,0:T(8,128)(2,1)S(1)} %shard_map.96.emb_ref, bf16[400,256]{1,0:T(8,128)(2,1)S(1)} %collective-permute-done.1.other_ref), custom_call_target="tpu_custom_call" | custom-call | flops 301989888 | bytes 2097152 | tf_op jit(solution)/shard_map/pallas_call | solution.py:40
  35.4 6.4 %all-to-all-start.1 = ((bf16[32,48,128]{2,1,0:T(8,128)(2,1)}), bf16[32,48,128]{2,1,0:T(8,128)(2,1)S(1)}, u32[]{:S(2)}, u32[]{:S(2)}) async-start(bf16[32,48,128]{2,1,0:T(8,128)(2,1)} %shard_map.99), calls=%async_computation.1 | async-start | bytes 786432 | tf_op jit(solution)/shard_map/all_to_all | solution.py:325
  41.8 3.7 %collective-permute-start.2 = (bf16[128,256]{1,0:T(8,128)(2,1)S(1)}, bf16[128,256]{1,0:T(8,128)(2,1)S(1)}, u32[]{:S(2)}, u32[]{:S(2)}) collective-permute-start(bf16[128,256]{1,0:T(8,128)(2,1)S(1)} %shard_map.97.chip_ref), channel_id=1, source_target_pairs={{0,96},{96,0},{1,97},{97,1},{2,98},{98,2},{3,99},{99,3},{4,100},{1... | collective-permute-start | bytes 196616 | tf_op jit(solution)/shard_map/ppermute | solution.py:321
  45.5 7.7 %collective-permute-done.2.next_ref = bf16[128,256]{1,0:T(8,128)(2,1)S(1)} collective-permute-done((bf16[128,256]{1,0:T(8,128)(2,1)S(1)}, bf16[128,256]{1,0:T(8,128)(2,1)S(1)}, u32[]{:S(2)}, u32[]{:S(2)}) %collective-permute-start.2) | collective-permute-done | bytes 65568 | tf_op jit(solution)/shard_map/ppermute | solution.py:321
  53.2 1.4 %shard_map.98 = (s16[12,16,768]{2,1,0:T(8,128)(2,1)S(1)}, f32[192,128]{1,0:T(8,128)S(1)}, bf16[192,256]{1,0:T(8,128)(2,1)S(1)}, bf16[768,256]{1,0:T(8,128)(2,1)S(1)}) custom-call(s32[3]{0:T(128)S(1)} %pad_add_fusion.place_ref, bf16[128,256]{1,0:T(8,128)(2,1)S(1)} %shard_map.97.chip_ref, bf16[128,256]{1,0:T(8,128)(2,1)S(1)} %collective-permute-done.2.next_ref, ...), custom_call_target="tpu_custom_call" | custom-call | flops 75497472 | bytes 2097152 | tf_op jit(solution)/shard_map/pallas_call | solution.py:40
  54.7 3.6 %all-to-all-done.1.rows_ref = bf16[32,48,128]{2,1,0:T(8,128)(2,1)S(1)} async-done(((bf16[32,48,128]{2,1,0:T(8,128)(2,1)}), bf16[32,48,128]{2,1,0:T(8,128)(2,1)S(1)}, u32[]{:S(2)}, u32[]{:S(2)}) %all-to-all-start.1) | async-done | bytes 393248 | tf_op jit(solution)/shard_map/all_to_all | solution.py:325
  59.4 28.7 %all_to_all.30.part_ref = s16[12,16,896]{2,1,0:T(8,128)(2,1)S(1)} all-to-all(s16[12,16,896]{2,1,0:T(8,128)(2,1)S(1)} %get-tuple-element.36), channel_id=1, replica_groups=mesh['yh'=4,'yl'=2,'x'=4,'c'=2,'z'=12] {'z'}, dimensions={0} | all-to-all | bytes 688128 | tf_op jit(solution)/shard_map/all_to_all | solution.py:325
  89.0 6.9 %all_to_all.31.stat_ref = f32[4,16,128]{2,1,0:T(8,128)S(1)} all-to-all(f32[4,16,128]{2,1,0:T(8,128)S(1)} %get-tuple-element.38), channel_id=1, replica_groups=mesh['yh'=4,'yl'=2,'x'=4,'c'=2,'z'=12] {'yl','c'}, dimensions={0} | all-to-all | bytes 65536 | tf_op jit(solution)/shard_map/all_to_all | solution.py:325
  96.7 21.9 %all_to_all.32 = bf16[12,16,896]{2,1,0:T(8,128)(2,1)S(1)} all-to-all(bf16[12,16,896]{2,1,0:T(8,128)(2,1)S(1)} %shard_map.102), channel_id=1, replica_groups=mesh['yh'=4,'yl'=2,'x'=4,'c'=2,'z'=12] {'z'}, dimensions={0} | all-to-all | bytes 688128 | tf_op jit(solution)/shard_map/all_to_all | solution.py:325
  119.6 7.1 %all-to-all-start.5 = ((bf16[16,48,256]{2,1,0:T(8,128)(2,1)}), bf16[16,48,256]{2,1,0:T(8,128)(2,1)S(1)}, u32[]{:S(2)}, u32[]{:S(2)}) async-start(bf16[16,48,256]{2,1,0:T(8,128)(2,1)} %shard_map.104), calls=%async_computation.5 | async-start | bytes 786432 | tf_op jit(solution)/shard_map/all_to_all | solution.py:325
  126.7 1.5 %shard_map.103 = (f32[2,48,256]{2,1,0:T(8,128)S(1)}, f32[2,48,256]{2,1,0:T(8,128)S(1)}, f32[7,48,256]{2,1,0:T(8,128)}, f32[8,48]{1,0:T(8,128)S(1)}) custom-call(s32[3]{0:T(128)S(1)} %pad_add_fusion.place_ref, bf16[192,896]{1,0:T(8,128)(2,1)S(1)} %bitcast.10, bf16[768,256]{1,0:T(8,128)(2,1)S(1)} %get-tuple-element.39.pass_ref, ...), custom_call_target="tpu_custom_call" | custom-call | flops 75497472 | bytes 3145728 | tf_op jit(solution)/shard_map/pallas_call | solution.py:40
  128.2 1.9 %collective-permute-start.3 = (f32[2,48,256]{2,1,0:T(8,128)S(1)}, f32[2,48,256]{2,1,0:T(8,128)S(1)}, u32[]{:S(2)}, u32[]{:S(2)}) collective-permute-start(f32[2,48,256]{2,1,0:T(8,128)S(1)} %get-tuple-element.44), channel_id=1, source_target_pairs={{0,12},{12,0},{1,13},{13,1},{2,14},{14,2},{3,15},{15,3},{4,16},{16... | collective-permute-start | bytes 294920 | tf_op jit(solution)/shard_map/ppermute | solution.py:321
  132.0 2.0 %collective-permute-start.4 = (f32[48,256]{1,0:T(8,128)S(1)}, f32[48,256]{1,0:T(8,128)S(1)}, u32[]{:S(2)}, u32[]{:S(2)}) collective-permute-start(f32[48,256]{1,0:T(8,128)S(1)} %get-tuple-element.46), channel_id=1, source_target_pairs={{0,96},{96,0},{1,97},{97,1},{2,98},{98,2},{3,99},{99,3},{4,100},{1... | collective-permute-start | bytes 147464 | tf_op jit(solution)/shard_map/ppermute | solution.py:321
  134.5 3.9 %collective-permute-done.4.other_ref = f32[48,256]{1,0:T(8,128)S(1)} collective-permute-done((f32[48,256]{1,0:T(8,128)S(1)}, f32[48,256]{1,0:T(8,128)S(1)}, u32[]{:S(2)}, u32[]{:S(2)}) %collective-permute-start.4) | collective-permute-done | bytes 49184 | tf_op jit(solution)/shard_map/ppermute | solution.py:321
  138.5 3.5 %all-to-all-done.5.parts_ref = bf16[16,48,256]{2,1,0:T(8,128)(2,1)S(1)} async-done(((bf16[16,48,256]{2,1,0:T(8,128)(2,1)}), bf16[16,48,256]{2,1,0:T(8,128)(2,1)S(1)}, u32[]{:S(2)}, u32[]{:S(2)}) %all-to-all-start.5) | async-done | bytes 393248 | tf_op jit(solution)/shard_map/all_to_all | solution.py:325
  (26 shorter events, 10.5 us)
Async XLA Ops:
  0.6 18.3 %copy-start.6 = (s32[48]{0:T(128)S(1)}, s32[48]{0:T(128)}, u32[]{:S(2)}) copy-start(s32[48]{0:T(128)} %param.10) | copy-start | bytes 580
  0.7 0.7 copy-start.5
  2.7 6.6 %collective-permute-start = (bf16[32,128]{1,0:T(8,128)(2,1)S(1)}, bf16[32,128]{1,0:T(8,128)(2,1)S(1)}, u32[]{:S(2)}, u32[]{:S(2)}) collective-permute-start(bf16[32,128]{1,0:T(8,128)(2,1)S(1)} %get-tuple-element.28), channel_id=1, source_target_pairs={{0,96},{96,0},{1,97},{97,1},{2,98},{98,2},{3,99},{99,3},{4,100},{1... | collective-permute-start | bytes 24584 | tf_op jit(solution)/shard_map/ppermute | solution.py:321
  6.2 1.6 %copy-start = (bf16[4096,256]{1,0:T(8,128)(2,1)S(1)}, bf16[4096,256]{1,0:T(8,128)(2,1)}, u32[]{:S(2)}) copy-start(bf16[4096,256]{1,0:T(8,128)(2,1)} %w_ref.3) | copy-start | bytes 6291460
  7.8 1.0 copy-start.3
  8.8 10.1 %copy-start.1 = (bf16[4096,256]{1,0:T(8,128)(2,1)S(1)}, bf16[4096,256]{1,0:T(8,128)(2,1)}, u32[]{:S(2)}) copy-start(bf16[4096,256]{1,0:T(8,128)(2,1)} %w_ref.3) | copy-start | bytes 6291460
  8.8 10.1 %copy-start.4 = (bf16[48,4096]{1,0:T(8,128)(2,1)S(1)}, bf16[48,4096]{1,0:T(8,128)(2,1)}, u32[]{:S(2)}) copy-start(bf16[48,4096]{1,0:T(8,128)(2,1)} %qh_ref.1) | copy-start | bytes 1179652
  10.1 23.3 %all-to-all-start = ((bf16[16,112,128]{2,1,0:T(8,128)(2,1)}), bf16[16,112,128]{2,1,0:T(8,128)(2,1)S(1)}, u32[]{:S(2)}, u32[]{:S(2)}) async-start(bf16[16,112,128]{2,1,0:T(8,128)(2,1)} %shard_map.95), calls=%async_computation | async-start | bytes 917504 | tf_op jit(solution)/shard_map/all_to_all | solution.py:325
  18.9 1.8 %copy-start.2 = (bf16[336,4096]{1,0:T(8,128)(2,1)S(1)}, bf16[336,4096]{1,0:T(8,128)(2,1)}, u32[]{:S(2)}) copy-start(bf16[336,4096]{1,0:T(8,128)(2,1)} %nh_ref.1) | copy-start | bytes 8257540
  22.7 3.3 %collective-permute-start.1 = (bf16[400,256]{1,0:T(8,128)(2,1)S(1)}, bf16[400,256]{1,0:T(8,128)(2,1)S(1)}, u32[]{:S(2)}, u32[]{:S(2)}) collective-permute-start(bf16[400,256]{1,0:T(8,128)(2,1)S(1)} %shard_map.96.emb_ref), channel_id=1, source_target_pairs={{0,12},{12,0},{1,13},{13,1},{2,14},{14,2},{3,15},{15,3},{4,16},{16... | collective-permute-start | bytes 614408 | tf_op jit(solution)/shard_map/ppermute | solution.py:321
  35.4 22.9 %all-to-all-start.1 = ((bf16[32,48,128]{2,1,0:T(8,128)(2,1)}), bf16[32,48,128]{2,1,0:T(8,128)(2,1)S(1)}, u32[]{:S(2)}, u32[]{:S(2)}) async-start(bf16[32,48,128]{2,1,0:T(8,128)(2,1)} %shard_map.99), calls=%async_computation.1 | async-start | bytes 786432 | tf_op jit(solution)/shard_map/all_to_all | solution.py:325
  41.8 11.4 %collective-permute-start.2 = (bf16[128,256]{1,0:T(8,128)(2,1)S(1)}, bf16[128,256]{1,0:T(8,128)(2,1)S(1)}, u32[]{:S(2)}, u32[]{:S(2)}) collective-permute-start(bf16[128,256]{1,0:T(8,128)(2,1)S(1)} %shard_map.97.chip_ref), channel_id=1, source_target_pairs={{0,96},{96,0},{1,97},{97,1},{2,98},{98,2},{3,99},{99,3},{4,100},{1... | collective-permute-start | bytes 196616 | tf_op jit(solution)/shard_map/ppermute | solution.py:321
  119.6 22.4 %all-to-all-start.5 = ((bf16[16,48,256]{2,1,0:T(8,128)(2,1)}), bf16[16,48,256]{2,1,0:T(8,128)(2,1)S(1)}, u32[]{:S(2)}, u32[]{:S(2)}) async-start(bf16[16,48,256]{2,1,0:T(8,128)(2,1)} %shard_map.104), calls=%async_computation.5 | async-start | bytes 786432 | tf_op jit(solution)/shard_map/all_to_all | solution.py:325
  128.2 3.2 %collective-permute-start.3 = (f32[2,48,256]{2,1,0:T(8,128)S(1)}, f32[2,48,256]{2,1,0:T(8,128)S(1)}, u32[]{:S(2)}, u32[]{:S(2)}) collective-permute-start(f32[2,48,256]{2,1,0:T(8,128)S(1)} %get-tuple-element.44), channel_id=1, source_target_pairs={{0,12},{12,0},{1,13},{13,1},{2,14},{14,2},{3,15},{15,3},{4,16},{16... | collective-permute-start | bytes 294920 | tf_op jit(solution)/shard_map/ppermute | solution.py:321
  132.0 6.5 %collective-permute-start.4 = (f32[48,256]{1,0:T(8,128)S(1)}, f32[48,256]{1,0:T(8,128)S(1)}, u32[]{:S(2)}, u32[]{:S(2)}) collective-permute-start(f32[48,256]{1,0:T(8,128)S(1)} %get-tuple-element.46), channel_id=1, source_target_pairs={{0,96},{96,0},{1,97},{97,1},{2,98},{98,2},{3,99},{99,3},{4,100},{1... | collective-permute-start | bytes 147464 | tf_op jit(solution)/shard_map/ppermute | solution.py:321
